TPU v7x, 32 devices: a whole 2x2x4 slice. The times are simulated.
32 devices in a mesh: groups: 1, expert: 8 (over z, y), dp: 2 (over x), seq: 2 (over core).
Axes of the slice: x: 2, y: 2, z: 4, core: 2. Of those that a mesh axis runs over, the one named last changes fastest.
Arguments:
- hidden_rows: bfloat16 [4096, 1024], P(('groups', 'expert', 'dp', 'seq')), may hold values from -6 to 6
- out_grad: bfloat16 [4096, 1024], P(('groups', 'expert', 'dp', 'seq')), may hold values from -3 to 3
- gates: float32 [4096, 6], P(('groups', 'expert', 'dp', 'seq')), may hold values from 0.1 to 0.6
- routes: int32 [4096, 6], P(('groups', 'expert', 'dp', 'seq')), may hold values from 0 to 15, all different within a row; in each aligned block of 128 rows (0 to 127, 128 to 255, ...) at most 49 rows name the same one
- w_gate: bfloat16 [16, 1024, 704], P(('expert', 'seq'), None, 'dp'), may hold values from -0.1875 to 0.1875
- w_up: bfloat16 [16, 1024, 704], P(('expert', 'seq'), None, 'dp'), may hold values from -0.1875 to 0.1875
- w_down: bfloat16 [16, 704, 1024], P(('expert', 'seq'), 'dp'), may hold values from -0.21875 to 0.21875
Outputs:
- mixed: bfloat16 [4096, 1024], P(('groups', 'expert', 'dp', 'seq'))
- grad_rows: bfloat16 [4096, 1024], P(('groups', 'expert', 'dp', 'seq'))
- grad_gates: float32 [4096, 6], P(('groups', 'expert', 'dp', 'seq'))
Inputs may be any that keep to these rules, and one draw needn't show every extreme that they name: `routes`: the 6 entries of a row differ. Among the rows of one device no expert is named more than 49 times, and in every draw some device names some expert exactly 49 times.
All inputs are finite; a program needn't handle non-finite values.
Results may differ from a plain program's by a relative error of at most 0.0065.
Values may be sent and summed in bfloat16 or wider, within the bound.
No kernel may reach another device: no remote copies, remote signals or barrier semaphores. Data moves between devices by JAX's collectives and lax.ppermute only.
A program may use at most 64 MiB of HBM per device.

v0:
```python
import jax
import jax.numpy as jnp
from jax import lax
from jax.sharding import PartitionSpec as P


def expert_pass(rows, scaled, gate_weight, up_weight, down_weight):
    gate_val = jnp.dot(rows, gate_weight, preferred_element_type=jnp.float32)
    up_val = jnp.dot(rows, up_weight, preferred_element_type=jnp.float32)
    sig = jax.nn.sigmoid(gate_val)
    act = (gate_val * sig * up_val).astype(jnp.bfloat16)
    out = jnp.dot(act, down_weight, preferred_element_type=jnp.float32).astype(jnp.bfloat16)
    d_act = jnp.dot(scaled, down_weight.T, preferred_element_type=jnp.float32)
    d_gate = (d_act * up_val * sig * (1.0 + gate_val * (1.0 - sig))).astype(jnp.bfloat16)
    d_up = (d_act * gate_val * sig).astype(jnp.bfloat16)
    back = jnp.dot(d_gate, gate_weight.T, preferred_element_type=jnp.float32)
    back = back + jnp.dot(d_up, up_weight.T, preferred_element_type=jnp.float32)
    return (out, back.astype(jnp.bfloat16))


def local(hidden_rows, out_grad, gates, routes, w_gate, w_up, w_down):
    tokens_here, width = hidden_rows.shape
    top = routes.shape[1]
    local_experts = w_gate.shape[0]
    n_expert = lax.axis_size("expert")
    n_seq = lax.axis_size("seq")
    experts = n_expert * n_seq * local_experts
    capacity = max(tokens_here * top // experts + 1, 2)
    flat = routes.reshape(-1)
    onehot = (flat[:, None] == jnp.arange(experts, dtype=jnp.int32)[None, :]).astype(jnp.int32)
    before = jnp.cumsum(onehot, axis=0) - onehot
    slot = jnp.sum(before * onehot, axis=1)
    place = flat * capacity + slot
    token = jnp.arange(flat.shape[0], dtype=jnp.int32) // top
    gate_flat = gates.reshape(-1)
    scaled = (gate_flat[:, None] * out_grad[token].astype(jnp.float32)).astype(jnp.bfloat16)
    empty = jnp.zeros((experts * capacity, width), jnp.bfloat16)
    send_rows = empty.at[place].set(hidden_rows[token])
    send_grads = empty.at[place].set(scaled)
    full_gate, full_up, full_down = (
        lax.all_gather(w_gate, "dp", axis=2, tiled=True),
        lax.all_gather(w_up, "dp", axis=2, tiled=True),
        lax.all_gather(w_down, "dp", axis=1, tiled=True),
    )
    rows = lax.all_to_all(
        send_rows.reshape(experts, capacity, width),
        ("expert", "seq"),
        split_axis=0,
        concat_axis=0,
        tiled=True,
    )
    count = rows.shape[1]
    rows_four = rows.reshape(-1, local_experts, count, width)
    grads_four = lax.all_to_all(
        send_grads.reshape(experts, capacity, width),
        ("expert", "seq"),
        split_axis=0,
        concat_axis=0,
        tiled=True,
    ).reshape(-1, local_experts, count, width)
    out, back = expert_pass(
        rows_four[:, 0].reshape(-1, width),
        grads_four[:, 0].reshape(-1, width),
        full_gate[0],
        full_up[0],
        full_down[0],
    )
    outs = out.reshape(-1, 1, count, width)
    backs = back.reshape(-1, 1, count, width)
    out_all = outs.reshape(rows.shape)
    back_all = backs.reshape(rows.shape)
    out_all, back_all = (out_all, back_all)
    came_out = lax.all_to_all(out_all, ("expert", "seq"), split_axis=0, concat_axis=0, tiled=True)
    came_back = lax.all_to_all(back_all, ("expert", "seq"), split_axis=0, concat_axis=0, tiled=True)
    out_routes = (
        came_out.reshape(experts * capacity, width)[place]
        .astype(jnp.float32)
        .reshape(tokens_here, top, width)
    )
    back_routes = (
        came_back.reshape(experts * capacity, width)[place]
        .astype(jnp.float32)
        .reshape(tokens_here, top, width)
    )
    mixed = jnp.sum(gates[:, :, None] * out_routes, axis=1).astype(jnp.bfloat16)
    grad_rows = jnp.sum(back_routes, axis=1).astype(jnp.bfloat16)
    grad_gates = jnp.sum(out_grad.astype(jnp.float32)[:, None, :] * out_routes, axis=2)
    return (mixed, grad_rows, grad_gates)


def solution(mesh):
    in_specs = (
        P(("groups", "expert", "dp", "seq"), None),
        P(("groups", "expert", "dp", "seq"), None),
        P(("groups", "expert", "dp", "seq"), None),
        P(("groups", "expert", "dp", "seq"), None),
        P(("expert", "seq"), None, "dp"),
        P(("expert", "seq"), None, "dp"),
        P(("expert", "seq"), "dp", None),
    )
    out_specs = (
        P(("groups", "expert", "dp", "seq"), None),
        P(("groups", "expert", "dp", "seq"), None),
        P(("groups", "expert", "dp", "seq"), None),
    )
    return jax.shard_map(local, mesh=mesh, in_specs=in_specs, out_specs=out_specs, check_vma=False)
```

profile of v0, /device:TPU:13, one launch (start us, length us, event | category | flops | bytes accessed | tf_op | source)
XLA Modules:
  0.0 240.8 jit_solution(2736943444602190017)
XLA Ops:
  11.4 13.8 %scatter_custom_fusion = bf16[784,1024]{1,0:T(8,128)(2,1)S(1)} fusion(s32[768]{0:T(1024)S(1)} %fusion.20, bf16[128,1024]{1,0:T(8,128)(2,1)S(1)} %copy-done, s32[1024]{0:T(1024)S(1)} %pad_clamp_fusion.1, bf16[]{:T(256)} %constant.8.clone.1), kind=kCustom, calls=%fused_computation.16 | custom fusion | bytes 1605634 | tf_op jit(solution)/shard_map/scatter | solution.py:38
  26.8 6.7 %all-to-all-start = ((bf16[16,49,1024]{2,1,0:T(8,128)(2,1)}), bf16[16,49,1024]{2,1,0:T(8,128)(2,1)S(1)}, u32[]{:S(2)}, u32[]{:S(2)}) async-start(bf16[16,49,1024]{2,1,0:T(8,128)(2,1)} %reshape.127), calls=%async_computation | async-start | bytes 3670016 | tf_op jit(solution)/shard_map/all_to_all | solution.py:45
  35.2 15.1 %scatter_custom_fusion.1 = bf16[784,1024]{1,0:T(8,128)(2,1)} fusion(s32[768]{0:T(1024)S(1)} %fusion.20, f32[768]{0:T(1024)S(1)} %mul.81, bf16[]{:T(256)} %constant.8.clone.1, bf16[128,1024]{1,0:T(8,128)(2,1)S(1)} %copy-done.4, s32[1024]{0:T(1024)S(1)} %pad_clamp_fusion.1), kind=kCustom, calls=%fused_computation.15 | custom fusion | flops 2359296 | bytes 1875970 | tf_op jit(solution)/shard_map/scatter | solution.py:39
  50.4 2.6 %reshape.129 = bf16[16,49,1024]{2,1,0:T(8,128)(2,1)} reshape(bf16[784,1024]{1,0:T(8,128)(2,1)} %scatter_custom_fusion.1) | data formatting | bytes 3211264 | tf_op jit(solution)/shard_map/reshape | solution.py:55
  53.0 22.7 %all-to-all-done = bf16[16,49,1024]{2,1,0:T(8,128)(2,1)S(1)} async-done(((bf16[16,49,1024]{2,1,0:T(8,128)(2,1)}), bf16[16,49,1024]{2,1,0:T(8,128)(2,1)S(1)}, u32[]{:S(2)}, u32[]{:S(2)}) %all-to-all-start) | async-done | bytes 1605664 | tf_op jit(solution)/shard_map/all_to_all | solution.py:45
  75.7 4.5 %all-to-all-start.2 = ((bf16[16,49,1024]{2,1,0:T(8,128)(2,1)}), bf16[16,49,1024]{2,1,0:T(8,128)(2,1)}, u32[]{:S(2)}, u32[]{:S(2)}) async-start(bf16[16,49,1024]{2,1,0:T(8,128)(2,1)} %reshape.129), calls=%async_computation.2 | async-start | bytes 3670016 | tf_op jit(solution)/shard_map/all_to_all | solution.py:54
  82.3 4.8 %fusion.8 = f32[784,704]{1,0:T(8,128)} fusion(bf16[784,1024]{1,0:T(8,128)(2,1)} %reshape_squeeze_reshape.6, bf16[1,1024,704]{1,2,0:T(8,128)(2,1)} %all-gather.6.cloned.1.call-done), kind=kOutput, calls=%fused_computation.23 | convolution fusion | flops 1130364928 | bytes 5255168 | tf_op jit(solution)/shard_map/dot_general | solution.py:9
  87.2 2.3 all-gather.4.cloned.1.call-done
  89.5 4.2 %fusion.12 = f32[784,704]{1,0:T(8,128)} fusion(bf16[784,1024]{1,0:T(8,128)(2,1)S(1)} %copy-done.3, bf16[1,1024,704]{1,2,0:T(8,128)(2,1)} %all-gather.4.cloned.1.call-done), kind=kOutput, calls=%fused_computation.27 | convolution fusion | flops 1130364928 | bytes 5255168 | tf_op jit(solution)/shard_map/dot_general | solution.py:8
  93.7 23.1 %all-gather.8.cloned.1.call-done = bf16[1,704,1024]{2,1,0:T(8,128)(2,1)} async-done(((bf16[1,352,1024]{2,1,0:T(8,128)(2,1)}), bf16[1,704,1024]{2,1,0:T(8,128)(2,1)}) %all-gather.8.cloned.1.call-update) | async-done | bytes 1441808 | tf_op jit(solution)/shard_map/all_gather | solution.py:43
  116.8 4.3 %convolution_convert_fusion = bf16[784,1024]{1,0:T(8,128)(2,1)S(1)} fusion(bf16[1,704,1024]{2,1,0:T(8,128)(2,1)} %all-gather.8.cloned.1.call-done, f32[784,704]{1,0:T(8,128)} %fusion.8, f32[784,704]{1,0:T(8,128)} %fusion.12), kind=kOutput, calls=%fused_computation.14 | convolution fusion | flops 1134479360 | bytes 7462912 | tf_op jit(solution)/shard_map/dot_general | solution.py:12
  122.7 6.4 %all-to-all-start.1 = ((bf16[16,49,1024]{2,1,0:T(8,128)(2,1)}), bf16[16,49,1024]{2,1,0:T(8,128)(2,1)S(1)}, u32[]{:S(2)}, u32[]{:S(2)}) async-start(bf16[16,49,1024]{2,1,0:T(8,128)(2,1)} %reshape_reshape.6), calls=%async_computation.1 | async-start | bytes 3670016 | tf_op jit(solution)/shard_map/all_to_all | solution.py:73
  129.0 2.6 %reshape_squeeze_reshape.7 = bf16[784,1024]{1,0:T(8,128)(2,1)} reshape(bf16[16,49,1024]{2,1,0:T(8,128)(2,1)} %all-to-all-done.2) | data formatting | bytes 3211264 | tf_op jit(solution)/shard_map/reshape;squeeze;reshape | solution.py:63
  131.6 3.4 %fusion.4 = f32[784,704]{1,0:T(8,128)S(1)} fusion(bf16[784,1024]{1,0:T(8,128)(2,1)} %reshape_squeeze_reshape.7, bf16[1,704,1024]{2,1,0:T(8,128)(2,1)} %all-gather.8.cloned.1.call-done), kind=kOutput, calls=%fused_computation.19 | convolution fusion | flops 1130364928 | bytes 5255168 | tf_op jit(solution)/shard_map/dot_general | solution.py:13
  137.5 2.6 %add_convert_fusion = bf16[784,1024]{1,0:T(8,128)(2,1)} fusion(f32[784,1024]{1,0:T(8,128)S(1)} %fusion.10, bf16[1,1024,704]{1,2,0:T(8,128)(2,1)S(1)} %copy-done.6, f32[784,704]{1,0:T(8,128)S(1)} %fusion.4, f32[784,704]{1,0:T(8,128)S(1)} %copy-done.9), kind=kOutput, calls=%fused_computation.8 | convolution fusion | flops 1135282176 | bytes 10674176 | tf_op jit(solution)/shard_map/dot_general | solution.py:17
  140.2 2.6 %reshape_reshape.7 = bf16[16,49,1024]{2,1,0:T(8,128)(2,1)} reshape(bf16[784,1024]{1,0:T(8,128)(2,1)} %add_convert_fusion) | data formatting | bytes 3211264 | tf_op jit(solution)/shard_map/reshape;reshape | solution.py:71
  142.8 28.0 %all-to-all-done.1 = bf16[16,49,1024]{2,1,0:T(8,128)(2,1)S(1)} async-done(((bf16[16,49,1024]{2,1,0:T(8,128)(2,1)}), bf16[16,49,1024]{2,1,0:T(8,128)(2,1)S(1)}, u32[]{:S(2)}, u32[]{:S(2)}) %all-to-all-start.1) | async-done | bytes 1605664 | tf_op jit(solution)/shard_map/all_to_all | solution.py:73
  172.1 4.9 %all-to-all-start.3 = ((bf16[16,49,1024]{2,1,0:T(8,128)(2,1)}), bf16[16,49,1024]{2,1,0:T(8,128)(2,1)}, u32[]{:S(2)}, u32[]{:S(2)}) async-start(bf16[16,49,1024]{2,1,0:T(8,128)(2,1)} %reshape_reshape.7), calls=%async_computation.3 | async-start | bytes 3670016 | tf_op jit(solution)/shard_map/all_to_all | solution.py:74
  179.6 2.8 %gather_fusion = bf16[768,1024]{1,0:T(8,128)(2,1)S(1)} fusion(bf16[784,1024]{1,0:T(8,128)(2,1)S(1)} %reshape.128, s32[1024]{0:T(1024)S(1)} %pad_clamp_fusion), kind=kCustom, calls=%fused_computation.1 | custom fusion | bytes 3148800 | tf_op jit(solution)/shard_map/gather | solution.py:76
  184.5 34.4 %all-to-all-done.3 = bf16[16,49,1024]{2,1,0:T(8,128)(2,1)} async-done(((bf16[16,49,1024]{2,1,0:T(8,128)(2,1)}), bf16[16,49,1024]{2,1,0:T(8,128)(2,1)}, u32[]{:S(2)}, u32[]{:S(2)}) %all-to-all-start.3) | async-done | bytes 1605664 | tf_op jit(solution)/shard_map/all_to_all | solution.py:74
  220.6 3.6 %gather_fusion.1 = bf16[768,1024]{1,0:T(8,128)(2,1)} fusion(bf16[784,1024]{1,0:T(8,128)(2,1)S(1)} %reshape.130, s32[1024]{0:T(1024)S(1)} %pad_clamp_fusion), kind=kCustom, calls=%fused_computation.3 | custom fusion | bytes 3148800 | tf_op jit(solution)/shard_map/gather | solution.py:81
  224.2 2.5 %gather.18 = bf16[128,6,1024]{2,1,0:T(8,128)(2,1)S(1)} reshape(bf16[768,1024]{1,0:T(8,128)(2,1)} %gather_fusion.1) | data formatting | bytes 3145728 | tf_op jit(solution)/shard_map/gather | solution.py:81
  226.7 2.2 reduce_sum.44
  228.9 4.8 %multiply_reduce_fusion = (f32[128,6]{1,0:T(8,128)S(1)}, bf16[128,1024]{1,0:T(8,128)(2,1)}) fusion(f32[128,6,1024]{2,1,0:T(8,128)} %reshape.131, f32[128,1024]{1,0:T(8,128)S(1)} %copy-done.2, f32[128,6]{1,0:T(8,128)S(1)} %copy.17), kind=kLoop, calls=%fused_computation.6 | loop fusion | flops 3013888 | bytes 3938304 | tf_op jit(solution)/shard_map/reduce_sum | solution.py:87
  (54 shorter events, 21.9 us)
Async XLA Ops:
  7.2 4.3 %copy-start = (bf16[128,1024]{1,0:T(8,128)(2,1)S(1)}, bf16[128,1024]{1,0:T(8,128)(2,1)}, u32[]{:S(2)}) copy-start(bf16[128,1024]{1,0:T(8,128)(2,1)} %param.7) | copy-start | bytes 786436
  26.8 8.2 %copy-start.5 = (f32[128,6]{0,1:T(8,128)S(1)}, f32[128,6]{0,1:T(8,128)}, u32[]{:S(2)}) copy-start(f32[128,6]{0,1:T(8,128)} %param.9) | copy-start | bytes 9220
  26.8 48.9 %all-to-all-start = ((bf16[16,49,1024]{2,1,0:T(8,128)(2,1)}), bf16[16,49,1024]{2,1,0:T(8,128)(2,1)S(1)}, u32[]{:S(2)}, u32[]{:S(2)}) async-start(bf16[16,49,1024]{2,1,0:T(8,128)(2,1)} %reshape.127), calls=%async_computation | async-start | bytes 3670016 | tf_op jit(solution)/shard_map/all_to_all | solution.py:45
  33.5 1.8 copy-start.4
  33.5 48.9 %all-gather.6.cloned.1.call-start = ((), (), s32[]{:S(2)}) async-start(), calls=%async_computation.5 | async-start | bytes 2162688 | tf_op jit(solution)/shard_map/all_gather | solution.py:42
  34.2 55.3 %all-gather.4.cloned.1.call-start = ((), (), s32[]{:S(2)}) async-start(), calls=%async_computation.4 | async-start | bytes 2162688 | tf_op jit(solution)/shard_map/all_gather | solution.py:41
  75.7 47.0 %all-to-all-start.2 = ((bf16[16,49,1024]{2,1,0:T(8,128)(2,1)}), bf16[16,49,1024]{2,1,0:T(8,128)(2,1)}, u32[]{:S(2)}, u32[]{:S(2)}) async-start(bf16[16,49,1024]{2,1,0:T(8,128)(2,1)} %reshape.129), calls=%async_computation.2 | async-start | bytes 3670016 | tf_op jit(solution)/shard_map/all_to_all | solution.py:54
  80.2 36.7 %all-gather.8.cloned.1.call-start = ((), (), s32[]{:S(2)}) async-start(), calls=%async_computation.6 | async-start | bytes 2162688 | tf_op jit(solution)/shard_map/all_gather | solution.py:43
  82.3 7.2 %copy-start.3 = (bf16[784,1024]{1,0:T(8,128)(2,1)S(1)}, bf16[784,1024]{1,0:T(8,128)(2,1)}, u32[]{:S(2)}) copy-start(bf16[784,1024]{1,0:T(8,128)(2,1)} %reshape_squeeze_reshape.6) | copy-start | bytes 4816900
  122.7 48.2 %all-to-all-start.1 = ((bf16[16,49,1024]{2,1,0:T(8,128)(2,1)}), bf16[16,49,1024]{2,1,0:T(8,128)(2,1)S(1)}, u32[]{:S(2)}, u32[]{:S(2)}) async-start(bf16[16,49,1024]{2,1,0:T(8,128)(2,1)} %reshape_reshape.6), calls=%async_computation.1 | async-start | bytes 3670016 | tf_op jit(solution)/shard_map/all_to_all | solution.py:73
  131.6 3.5 %copy-start.7 = (bf16[1,1024,704]{1,2,0:T(8,128)(2,1)S(1)}, bf16[1,1024,704]{1,2,0:T(8,128)(2,1)}, u32[]{:S(2)}) copy-start(bf16[1,1024,704]{1,2,0:T(8,128)(2,1)} %all-gather.4.cloned.1.call-done) | copy-start | bytes 4325380
  131.6 3.5 %copy-start.8 = (f32[784,704]{1,0:T(8,128)S(1)}, f32[784,704]{1,0:T(8,128)}, u32[]{:S(2)}) copy-start(f32[784,704]{1,0:T(8,128)} %fusion.8) | copy-start | bytes 6623236
  131.6 3.8 %copy-start.9 = (f32[784,704]{1,0:T(8,128)S(1)}, f32[784,704]{1,0:T(8,128)}, u32[]{:S(2)}) copy-start(f32[784,704]{1,0:T(8,128)} %fusion.12) | copy-start | bytes 6623236
  135.4 2.1 copy-start.6
  170.8 1.3 copy-start.1
  172.1 46.8 %all-to-all-start.3 = ((bf16[16,49,1024]{2,1,0:T(8,128)(2,1)}), bf16[16,49,1024]{2,1,0:T(8,128)(2,1)}, u32[]{:S(2)}, u32[]{:S(2)}) async-start(bf16[16,49,1024]{2,1,0:T(8,128)(2,1)} %reshape_reshape.7), calls=%async_computation.3 | async-start | bytes 3670016 | tf_op jit(solution)/shard_map/all_to_all | solution.py:74
  226.7 2.2 copy-start.2
Sparse Core Ops, SparseCore 0:
  35.9 26.2 all-gather.5
  63.7 25.7 all-gather.3
  91.1 25.7 all-gather.7
where the time goes:
time: 242 us; the launch traced here: 241 us
  waiting for transfers between devices  112 us (46%)
  local copies, waits for them, and re-layouts  44.7 us (18%)
  other arithmetic  25.6 us (11%)
  starting transfers between devices  23 us (10%)
  matrix products  21.6 us (9%)
  between operations  13.9 us (6%)
    all_to_all x1, waiting for transfers between devices, local(): lax.all_to_all(back_all, ('expert', 'seq'), split_axis=0, concat_axis=0,...  34.4 us
    all_to_all x1, waiting for transfers between devices, local(): lax.all_to_all(out_all, ('expert', 'seq'), split_axis=0, concat_axis=0, t...  28 us
    all_gather x1, waiting for transfers between devices, local(): lax.all_gather(w_down, 'dp', axis=1, tiled=True)  23.1 us
    all_to_all x1, waiting for transfers between devices, local(): lax.all_to_all(send_rows.reshape(experts, capacity, width), ('expert', 's...  22.7 us
    scatter x1, other arithmetic, local(): send_grads = empty.at[place].set(scaled)  15.1 us
    scatter x1, local copies, waits for them, and re-layouts, local(): send_rows = empty.at[place].set(hidden_rows[token])  13.8 us
    all_to_all x1, starting transfers between devices, local(): lax.all_to_all(send_rows.reshape(experts, capacity, width), ('expert', 's...  6.69 us
    all_to_all x1, starting transfers between devices, local(): lax.all_to_all(out_all, ('expert', 'seq'), split_axis=0, concat_axis=0, t...  6.36 us
  transfers between devices with their start and end apart: 7, of which 5 were waited for; matrix products, arithmetic and copies ran while one was open for 23% of the time, Pallas kernels for 0%

commit v1 on v0

v1 whole, which is shorter than its diff:
```python
import functools

import jax
import jax.numpy as jnp
from jax import lax
from jax.experimental import pallas as pl
from jax.experimental.pallas import tpu as pltpu
from jax.sharding import PartitionSpec as P

NT = (((1,), (1,)), ((), ()))
NN = (((1,), (0,)), ((), ()))


def dot(a, b, dims):
    return lax.dot_general(a, b, dims, preferred_element_type=jnp.float32)


def expert_kernel(held, parts, x_ref, o_ref, g_ref, *refs):
    pieces, (mixed_ref, back_ref, gate_grad_ref, w_buf, sem) = refs[: 3 * held * parts], refs[3 * held * parts :]
    piece = w_buf.shape[2] // parts

    def copies(e):
        for h in range(parts):
            for kind in range(3):
                src = pieces[(e * parts + h) * 3 + kind]
                yield pltpu.make_async_copy(src, w_buf.at[kind, e, pl.ds(h * piece, piece)], sem.at[e, h, kind])

    for e in range(held):
        for copy in copies(e):
            copy.start()
    x, o = x_ref[...], o_ref[...]
    columns = lax.broadcasted_iota(jnp.int32, gate_grad_ref.shape, 1)
    gate_grads = jnp.zeros(gate_grad_ref.shape, jnp.float32)
    for e in range(held):
        for copy in copies(e):
            copy.wait()
        gate = g_ref[:, e : e + 1]
        gate_val = dot(x, w_buf[0, e], NT)
        up_val = dot(x, w_buf[1, e], NT)
        d_out = dot(o, w_buf[2, e], NT)
        sig = jax.nn.sigmoid(gate_val)
        silu = gate_val * sig
        act = silu * up_val
        gate_grads = jnp.where(columns == e, jnp.sum(act * d_out, axis=1, keepdims=True), gate_grads)
        d_act = gate * d_out
        d_gate = (d_act * up_val * (sig + silu * (1.0 - sig))).astype(jnp.bfloat16)
        d_up = (d_act * silu).astype(jnp.bfloat16)
        mixed = dot((gate * act).astype(jnp.bfloat16), w_buf[2, e], NN)
        back = dot(d_gate, w_buf[0, e], NN) + dot(d_up, w_buf[1, e], NN)
        if e == 0:
            mixed_ref[...] = mixed
            back_ref[...] = back
        else:
            mixed_ref[...] += mixed
            back_ref[...] += back
    gate_grad_ref[...] = gate_grads


def experts_of(x, o, gate, pieces):
    rows, width = x.shape
    held, parts = len(pieces), len(pieces[0])
    hidden = parts * pieces[0][0][0].shape[0]
    flat = [w for of_expert in pieces for part in of_expert for w in part]
    vmem = pl.BlockSpec(memory_space=pltpu.VMEM)
    return pl.pallas_call(
        functools.partial(expert_kernel, held, parts),
        out_shape=(
            jax.ShapeDtypeStruct((rows, width), jnp.float32),
            jax.ShapeDtypeStruct((rows, width), jnp.float32),
            jax.ShapeDtypeStruct((rows, 128), jnp.float32),
        ),
        in_specs=[vmem] * 3 + [pl.BlockSpec(memory_space=pl.ANY)] * len(flat),
        out_specs=(vmem,) * 3,
        scratch_shapes=[
            pltpu.VMEM((3, held, hidden, width), jnp.bfloat16),
            pltpu.SemaphoreType.DMA((held, parts, 3)),
        ],
        compiler_params=pltpu.CompilerParams(vmem_limit_bytes=40 << 20),
        cost_estimate=pl.CostEstimate(
            flops=12 * rows * width * hidden * held,
            bytes_accessed=6 * hidden * width * held + 12 * rows * width,
            transcendentals=rows * hidden * held,
        ),
    )(x, o, gate, *flat)


def ring_order(n):
    return [0, 2, 4, 6, 7, 5, 3, 1] if n == 8 else list(range(n))


def local(hidden_rows, out_grad, gates, routes, w_gate, w_up, w_down):
    tokens, width = hidden_rows.shape
    n, n_dp, n_seq = lax.axis_size("expert"), lax.axis_size("dp"), lax.axis_size("seq")
    here = w_gate.shape[0]
    experts = n * n_seq * here
    order = ring_order(n)
    fw = [(order[i], order[(i + 1) % n]) for i in range(n)]
    bw = [(b, a) for a, b in fw]
    place = jnp.array([order.index(i) for i in range(n)], jnp.int32)
    at_place = jnp.array(order, jnp.int32)
    me = lax.axis_index("expert")
    my_seq = lax.axis_index("seq")
    my_place = place[me]

    def shifted(a, axis, size, by):
        return lax.ppermute(a, axis, [((i + by) % size, i) for i in range(size)])

    names = jnp.arange(experts, dtype=jnp.int32)
    chosen = routes[:, :, None] == names
    dense = jnp.sum(jnp.where(chosen, gates[:, :, None], 0.0), axis=1)
    dense_all = lax.all_gather(dense, "expert", axis=0)
    wanted = jnp.concatenate(
        [(me * n_seq + (my_seq + r) % n_seq) * here + jnp.arange(here, dtype=jnp.int32) for r in range(n_seq)]
    )
    gate_of = jnp.einsum("jte,he->jth", dense_all, (wanted[:, None] == names).astype(jnp.float32), precision="highest")

    def gates_at(distance):
        return lax.dynamic_index_in_dim(gate_of, at_place[(my_place + distance) % n], 0, keepdims=False)

    kinds = [w_down] + [jnp.swapaxes(w, 1, 2) for w in (w_gate, w_up)]
    by_dp = [kinds] + [[shifted(w, "dp", n_dp, r) for w in kinds] for r in range(1, n_dp)]
    by_seq = [by_dp] + [[[shifted(w, "seq", n_seq, r) for w in share] for share in by_dp] for r in range(1, n_seq)]
    pieces = [
        [(share[1][l], share[2][l], share[0][l]) for share in of_core] for of_core in by_seq for l in range(here)
    ]

    own = jnp.stack([hidden_rows, out_grad])
    ahead, behind = (n - 1) // 2, (n - 1) // 2
    half = tokens // 2
    arrived = {0: own}
    for s in range(1, ahead + 1):
        arrived[-s] = lax.ppermute(arrived[1 - s], "expert", fw)
        arrived[s] = lax.ppermute(arrived[s - 1], "expert", bw)
    far = n // 2
    even = n % 2 == 0
    if even:
        top = lax.ppermute(arrived[1 - far][:, :half], "expert", fw)
        low = lax.ppermute(arrived[far - 1][:, half:], "expert", bw)
        arrived[far] = jnp.concatenate([top, low], axis=1)

    gate_grads = {}

    def block(distances):
        both = [arrived[d] for d in distances]
        x = jnp.concatenate([b[0] for b in both]) if len(both) > 1 else both[0][0]
        o = jnp.concatenate([b[1] for b in both]) if len(both) > 1 else both[0][1]
        gate = jnp.concatenate([gates_at(d) for d in distances])
        mixed, back, grads = experts_of(x, o, gate, pieces)
        for i, d in enumerate(distances):
            gate_grads[d % n] = grads[i * tokens : (i + 1) * tokens, : n_seq * here]
        return [(mixed[i * tokens : (i + 1) * tokens], back[i * tokens : (i + 1) * tokens]) for i in range(len(distances))]

    def rounded(a):
        return a.astype(jnp.bfloat16)

    def plus(part, travelled):
        return part + travelled.astype(jnp.float32)

    send_fw = send_bw = None
    if even:
        ((mixed, back),) = block([far])
        send_fw = [lax.ppermute(rounded(a[:half]), "expert", fw) for a in (mixed, back)]
        send_bw = [lax.ppermute(rounded(a[half:]), "expert", bw) for a in (mixed, back)]
    for s in range(ahead, 0, -1):
        if s == 1:
            parts_fw, parts_bw, parts_own = block([1, -1, 0])
        else:
            parts_fw, parts_bw = block([s, -s])
        if send_fw is None:
            out_fw, out_bw = [rounded(a) for a in parts_fw], [rounded(a) for a in parts_bw]
        elif send_fw[0].shape[0] < tokens:
            out_fw = [rounded(jnp.concatenate([plus(a[:half], t), a[half:]])) for a, t in zip(parts_fw, send_fw)]
            out_bw = [rounded(jnp.concatenate([a[:half], plus(a[half:], t)])) for a, t in zip(parts_bw, send_bw)]
        else:
            out_fw = [rounded(plus(a, t)) for a, t in zip(parts_fw, send_fw)]
            out_bw = [rounded(plus(a, t)) for a, t in zip(parts_bw, send_bw)]
        send_fw = [lax.ppermute(a, "expert", fw) for a in out_fw]
        send_bw = [lax.ppermute(a, "expert", bw) for a in out_bw]
    mixed, grad_rows = [
        rounded(plus(plus(a, f), b)) for a, f, b in zip(parts_own, send_fw, send_bw)
    ]

    stacked = jnp.stack([gate_grads[d] for d in range(n)])
    to_device = jnp.take(stacked, (place - my_place) % n, axis=0)
    came = lax.all_to_all(to_device, "expert", split_axis=0, concat_axis=0, tiled=True)
    sender = jnp.arange(experts, dtype=jnp.int32)
    core, slot_here = (sender // here) % n_seq, sender % here
    slot = ((core - my_seq) % n_seq) * here + slot_here
    by_expert = jnp.stack([came[j] for j in range(n)], axis=1).reshape(tokens, experts)
    column = (sender // (n_seq * here)) * (n_seq * here) + slot
    flat = jnp.einsum("te,fe->tf", by_expert, (column[:, None] == sender).astype(jnp.float32), precision="highest")
    grad_gates = jnp.sum(jnp.where(chosen, flat[:, None, :], 0.0), axis=2)
    return (mixed, grad_rows, grad_gates)


def solution(mesh):
    tokens = P(("groups", "expert", "dp", "seq"), None)
    in_specs = (tokens,) * 4 + (P(("expert", "seq"), None, "dp"),) * 2 + (P(("expert", "seq"), "dp", None),)
    return jax.shard_map(local, mesh=mesh, in_specs=in_specs, out_specs=(tokens,) * 3, check_vma=False)
```

time: 242 us -> 196 us (0.81)
  the two profiles are of different devices: /device:TPU:13 before, /device:TPU:0 now
where the time goes in v1:
time: 196 us; the launch traced here: 195 us
  Pallas kernels  36.8 us (19%)
  starting transfers between devices  35.5 us (18%)
  waiting for transfers between devices  32.3 us (16%)
  blocking collectives  31.3 us (16%)
  between operations  23.1 us (12%)
  local copies, waits for them, and re-layouts  21.2 us (11%)
  other arithmetic  13.6 us (7%)
    pallas_call x4, Pallas kernels, experts_of(): pl.pallas_call(functools.partial(expert_kernel, held, parts), out_shape=(...  36.8 us
    all_gather x1, blocking collectives, local(): dense_all = lax.all_gather(dense, 'expert', axis=0)  31.3 us
    ppermute x6, waiting for transfers between devices, local(): send_fw = [lax.ppermute(a, 'expert', fw) for a in out_fw]  14.1 us
    ppermute x6, starting transfers between devices, local(): send_bw = [lax.ppermute(a, 'expert', bw) for a in out_bw]  9.44 us
    unnamed x61, local copies, waits for them, and re-layouts  7.1 us
    ppermute x6, waiting for transfers between devices, local(): send_bw = [lax.ppermute(a, 'expert', bw) for a in out_bw]  5.01 us
    all_to_all x1, starting transfers between devices, local(): lax.all_to_all(to_device, 'expert', split_axis=0, concat_axis=0, tiled=True)  5.01 us
    ppermute x1, waiting for transfers between devices, local(): top = lax.ppermute(arrived[1 - far][:, :half], 'expert', fw)  4.63 us
  transfers between devices with their start and end apart: 34, of which 15 were waited for; matrix products, arithmetic and copies ran while one was open for 15% of the time, Pallas kernels for 11%

profile of v1, /device:TPU:0, one launch (start us, length us, event | category | flops | bytes accessed | tf_op | source)
XLA Modules:
  0.0 194.8 jit_solution(6200323028601127975)
XLA Ops:
  0.7 2.0 %pad_maximum_fusion.2 = bf16[2,128,1024]{2,1,0:T(8,128)(2,1)} fusion(bf16[1,128,1024]{2,1,0:T(8,128)(2,1)} %bitcast.177, bf16[1,128,1024]{2,1,0:T(8,128)(2,1)} %bitcast.178), kind=kLoop, calls=%fused_computation.3 | loop fusion | flops 262144 | bytes 1048576 | tf_op jit(solution)/shard_map/stack | solution.py:127
  2.6 3.0 %collective-permute-start.1 = (bf16[2,128,1024]{2,1,0:T(8,128)(2,1)}, bf16[2,128,1024]{2,1,0:T(8,128)(2,1)}, u32[]{:S(2)}, u32[]{:S(2)}) collective-permute-start(bf16[2,128,1024]{2,1,0:T(8,128)(2,1)} %pad_maximum_fusion.2), channel_id=1, source_target_pairs={{0,8},{8,16},{16,24},{24,28},{28,20},{20,12},{12,4},{4,0},{1,9},{9... | collective-permute-start | bytes 1572872 | tf_op jit(solution)/shard_map/ppermute | solution.py:132
  5.7 1.9 collective-permute-start.2
  15.7 1.6 fusion.25
  28.2 31.3 %all-gather = f32[1024,16]{0,1:T(8,128)S(1)} all-gather(f32[128,16]{0,1:T(8,128)S(1)} %select_reduce_fusion.1), channel_id=2, replica_groups=mesh['groups'=1,'expert'=8,'dp'=2,'seq'=2] {'expert'}, dimensions={0}, use_global_device_ids=true | all-gather | bytes 73728 | tf_op jit(solution)/shard_map/all_gather | solution.py:111
  68.2 2.0 %collective-permute-start.11 = (bf16[2,128,1024]{2,1,0:T(8,128)(2,1)}, bf16[2,128,1024]{2,1,0:T(8,128)(2,1)}, u32[]{:S(2)}, u32[]{:S(2)}) collective-permute-start(bf16[2,128,1024]{2,1,0:T(8,128)(2,1)} %collective-permute-done), channel_id=1, source_target_pairs={{8,0},{16,8},{24,16},{28,24},{20,28},{12,20},{4,12},{0,4},{9,1},{1... | collective-permute-start | bytes 1572872 | tf_op jit(solution)/shard_map/ppermute | solution.py:133
  74.3 3.8 %collective-permute-done.4 = bf16[1,352,1024]{2,1,0:T(8,128)(2,1)} collective-permute-done((bf16[1,352,1024]{2,1,0:T(8,128)(2,1)S(1)}, bf16[1,352,1024]{2,1,0:T(8,128)(2,1)}, u32[]{:S(2)}, u32[]{:S(2)}) %collective-permute-start.4) | collective-permute-done | bytes 720928 | tf_op jit(solution)/shard_map/ppermute | solution.py:106
  81.8 2.0 %collective-permute-start.13 = (bf16[2,128,1024]{2,1,0:T(8,128)(2,1)}, bf16[2,128,1024]{2,1,0:T(8,128)(2,1)S(1)}, u32[]{:S(2)}, u32[]{:S(2)}) collective-permute-start(bf16[2,128,1024]{2,1,0:T(8,128)(2,1)} %collective-permute-done.11), channel_id=1, source_target_pairs={{8,0},{16,8},{24,16},{28,24},{20,28},{12,20},{4,12},{0,4},{9,1},{1... | collective-permute-start | bytes 1572872 | tf_op jit(solution)/shard_map/ppermute | solution.py:133
  83.9 8.8 %shard_map.113 = (f32[256,1024]{1,0:T(8,128)S(1)}, f32[256,1024]{1,0:T(8,128)S(1)}, f32[256,128]{1,0:T(8,128)S(1)}) custom-call(bf16[256,1024]{1,0:T(8,128)(2,1)S(1)} %get-tuple-element.81.x_ref, bf16[256,1024]{1,0:T(8,128)(2,1)S(1)} %get-tuple-element.82.o_ref, f32[256,2]{1,0:T(8,128)S(1)} %copy-done.15, bf16[352,1024]{1,0:T(8,128)(2,1)S(1)} %bitcast.134, ...), custom_call_target="tpu_custom_call" | custom-call | flops 4429185024 | bytes 11796480 | tf_op jit(solution)/shard_map/pallas_call | solution.py:65
  93.7 11.6 %shard_map.112 = (f32[384,1024]{1,0:T(8,128)S(1)}, f32[384,1024]{1,0:T(8,128)S(1)}, f32[384,128]{1,0:T(8,128)S(1)}) custom-call(bf16[384,1024]{1,0:T(8,128)(2,1)S(1)} %get-tuple-element.83.x_ref, bf16[384,1024]{1,0:T(8,128)(2,1)S(1)} %get-tuple-element.84.o_ref, f32[384,2]{1,0:T(8,128)S(1)} %copy.88.g_ref, bf16[352,1024]{1,0:T(8,128)(2,1)S(1)} %bitcast.135, ...), custom_call_target="tpu_custom_call" | custom-call | flops 6643777536 | bytes 13369344 | tf_op jit(solution)/shard_map/pallas_call | solution.py:65
  109.0 9.1 %shard_map.114 = (f32[256,1024]{1,0:T(8,128)S(1)}, f32[256,1024]{1,0:T(8,128)S(1)}, f32[256,128]{1,0:T(8,128)S(1)}) custom-call(bf16[256,1024]{1,0:T(8,128)(2,1)S(1)} %get-tuple-element.79.x_ref, bf16[256,1024]{1,0:T(8,128)(2,1)S(1)} %get-tuple-element.80.o_ref, f32[256,2]{1,0:T(8,128)S(1)} %copy.90.g_ref, bf16[352,1024]{1,0:T(8,128)(2,1)S(1)} %bitcast.136, ...), custom_call_target="tpu_custom_call" | custom-call | flops 4429185024 | bytes 11796480 | tf_op jit(solution)/shard_map/pallas_call | solution.py:65
  122.4 4.6 %collective-permute-done.15 = bf16[2,64,1024]{2,1,0:T(8,128)(2,1)S(1)} collective-permute-done((bf16[2,64,1024]{2,1,0:T(8,128)(2,1)S(1)}, bf16[2,64,1024]{2,1,0:T(8,128)(2,1)S(1)}, u32[]{:S(2)}, u32[]{:S(2)}) %collective-permute-start.15) | collective-permute-done | bytes 262176 | tf_op jit(solution)/shard_map/ppermute | solution.py:137
  127.9 7.3 %shard_map.115 = (f32[128,1024]{1,0:T(8,128)S(1)}, f32[128,1024]{1,0:T(8,128)S(1)}, f32[128,128]{1,0:T(8,128)S(1)}) custom-call(bf16[128,1024]{1,0:T(8,128)(2,1)S(1)} %get-tuple-element.58.x_ref, bf16[128,1024]{1,0:T(8,128)(2,1)S(1)} %get-tuple-element.57.o_ref, f32[128,2]{1,0:T(8,128)S(1)} %bitcast.176, bf16[352,1024]{1,0:T(8,128)(2,1)S(1)} %bitcast.137, ...), custom_call_target="tpu_custom_call" | custom-call | flops 2214592512 | bytes 10223616 | tf_op jit(solution)/shard_map/pallas_call | solution.py:65
  136.0 1.7 collective-permute-start.17
  144.5 5.0 %all-to-all-start = ((f32[8,128,2]{1,2,0:T(2,128)}), f32[8,128,2]{1,2,0:T(2,128)S(1)}, u32[]{:S(2)}, u32[]{:S(2)}) async-start(f32[8,128,2]{1,2,0:T(2,128)} %broadcast_select_fusion), calls=%async_computation | async-start | bytes 16384 | tf_op jit(solution)/shard_map/all_to_all | solution.py:185
  150.3 2.0 %collective-permute-start.25 = (bf16[64,1024]{1,0:T(8,128)(2,1)}, bf16[64,1024]{1,0:T(8,128)(2,1)}, u32[]{:S(2)}, u32[]{:S(2)}) collective-permute-start(bf16[64,1024]{1,0:T(8,128)(2,1)} %get-tuple-element.59), channel_id=1, source_target_pairs={{0,8},{8,16},{16,24},{24,28},{28,20},{20,12},{12,4},{4,0},{1,9},{9... | collective-permute-start | bytes 393224 | tf_op jit(solution)/shard_map/ppermute | solution.py:162
  152.3 3.8 %all-to-all-done = f32[8,128,2]{1,2,0:T(2,128)S(1)} async-done(((f32[8,128,2]{1,2,0:T(2,128)}), f32[8,128,2]{1,2,0:T(2,128)S(1)}, u32[]{:S(2)}, u32[]{:S(2)}) %all-to-all-start) | async-done | bytes 8224 | tf_op jit(solution)/shard_map/all_to_all | solution.py:185
  159.7 1.6 collective-permute-start.22
  162.9 1.6 collective-permute-start.30
  164.5 3.9 %collective-permute-done.18 = bf16[128,1024]{1,0:T(8,128)(2,1)S(1)} collective-permute-done((bf16[128,1024]{1,0:T(8,128)(2,1)S(1)}, bf16[128,1024]{1,0:T(8,128)(2,1)S(1)}, u32[]{:S(2)}, u32[]{:S(2)}) %collective-permute-start.18) | collective-permute-done | bytes 262176 | tf_op jit(solution)/shard_map/ppermute | solution.py:177
  171.2 2.9 %collective-permute-done.26 = bf16[128,1024]{1,0:T(8,128)(2,1)S(1)} collective-permute-done((bf16[128,1024]{1,0:T(8,128)(2,1)S(1)}, bf16[128,1024]{1,0:T(8,128)(2,1)S(1)}, u32[]{:S(2)}, u32[]{:S(2)}) %collective-permute-start.26) | collective-permute-done | bytes 262176 | tf_op jit(solution)/shard_map/ppermute | solution.py:177
  176.8 2.9 %collective-permute-done.19 = bf16[128,1024]{1,0:T(8,128)(2,1)S(1)} collective-permute-done((bf16[128,1024]{1,0:T(8,128)(2,1)S(1)}, bf16[128,1024]{1,0:T(8,128)(2,1)S(1)}, u32[]{:S(2)}, u32[]{:S(2)}) %collective-permute-start.19) | collective-permute-done | bytes 262176 | tf_op jit(solution)/shard_map/ppermute | solution.py:177
  182.4 2.9 %collective-permute-done.27 = bf16[128,1024]{1,0:T(8,128)(2,1)S(1)} collective-permute-done((bf16[128,1024]{1,0:T(8,128)(2,1)S(1)}, bf16[128,1024]{1,0:T(8,128)(2,1)S(1)}, u32[]{:S(2)}, u32[]{:S(2)}) %collective-permute-start.27) | collective-permute-done | bytes 262176 | tf_op jit(solution)/shard_map/ppermute | solution.py:177
  190.4 2.0 %collective-permute-done.32 = bf16[128,1024]{1,0:T(8,128)(2,1)S(1)} collective-permute-done((bf16[128,1024]{1,0:T(8,128)(2,1)S(1)}, bf16[128,1024]{1,0:T(8,128)(2,1)S(1)}, u32[]{:S(2)}, u32[]{:S(2)}) %collective-permute-start.32) | collective-permute-done | bytes 262176 | tf_op jit(solution)/shard_map/ppermute | solution.py:178
  (167 shorter events, 52.1 us)
Async XLA Ops:
  2.6 63.4 %collective-permute-start.1 = (bf16[2,128,1024]{2,1,0:T(8,128)(2,1)}, bf16[2,128,1024]{2,1,0:T(8,128)(2,1)}, u32[]{:S(2)}, u32[]{:S(2)}) collective-permute-start(bf16[2,128,1024]{2,1,0:T(8,128)(2,1)} %pad_maximum_fusion.2), channel_id=1, source_target_pairs={{0,8},{8,16},{16,24},{24,28},{28,20},{20,12},{12,4},{4,0},{1,9},{9... | collective-permute-start | bytes 1572872 | tf_op jit(solution)/shard_map/ppermute | solution.py:132
  5.7 62.5 %collective-permute-start = (bf16[2,128,1024]{2,1,0:T(8,128)(2,1)}, bf16[2,128,1024]{2,1,0:T(8,128)(2,1)}, u32[]{:S(2)}, u32[]{:S(2)}) collective-permute-start(bf16[2,128,1024]{2,1,0:T(8,128)(2,1)} %pad_maximum_fusion.2), channel_id=1, source_target_pairs={{8,0},{16,8},{24,16},{28,24},{20,28},{12,20},{4,12},{0,4},{9,1},{1... | collective-permute-start | bytes 1572872 | tf_op jit(solution)/shard_map/ppermute | solution.py:133
  5.7 62.5 %collective-permute-start.2 = (bf16[1,352,1024]{2,1,0:T(8,128)(2,1)}, bf16[1,352,1024]{2,1,0:T(8,128)(2,1)S(1)}, u32[]{:S(2)}, u32[]{:S(2)}) collective-permute-start(bf16[1,352,1024]{2,1,0:T(8,128)(2,1)} %bitcast.132), channel_id=1, source_target_pairs={{2,0},{0,2},{3,1},{1,3},{6,4},{4,6},{7,5},{5,7},{10,8},{8,10},{11,... | collective-permute-start | bytes 2162696 | tf_op jit(solution)/shard_map/ppermute | solution.py:106
  7.6 70.5 %collective-permute-start.5 = (bf16[1,352,1024]{2,1,0:T(8,128)(2,1)}, bf16[1,352,1024]{2,1,0:T(8,128)(2,1)S(1)}, u32[]{:S(2)}, u32[]{:S(2)}) collective-permute-start(bf16[1,352,1024]{2,1,0:T(8,128)(2,1)} %bitcast.133), channel_id=1, source_target_pairs={{1,0},{0,1},{3,2},{2,3},{5,4},{4,5},{7,6},{6,7},{9,8},{8,9},{11,10... | collective-permute-start | bytes 2162696 | tf_op jit(solution)/shard_map/ppermute | solution.py:106
  7.6 66.6 %collective-permute-start.3 = (bf16[1,352,1024]{2,1,0:T(8,128)(2,1)}, bf16[1,352,1024]{2,1,0:T(8,128)(2,1)}, u32[]{:S(2)}, u32[]{:S(2)}) collective-permute-start(bf16[1,352,1024]{2,1,0:T(8,128)(2,1)} %bitcast.138), channel_id=1, source_target_pairs={{2,0},{0,2},{3,1},{1,3},{6,4},{4,6},{7,5},{5,7},{10,8},{8,10},{11,... | collective-permute-start | bytes 2162696 | tf_op jit(solution)/shard_map/ppermute | solution.py:106
  66.1 12.0 %collective-permute-start.4 = (bf16[1,352,1024]{2,1,0:T(8,128)(2,1)S(1)}, bf16[1,352,1024]{2,1,0:T(8,128)(2,1)}, u32[]{:S(2)}, u32[]{:S(2)}) collective-permute-start(bf16[1,352,1024]{2,1,0:T(8,128)(2,1)S(1)} %copy-done.9), channel_id=1, source_target_pairs={{2,0},{0,2},{3,1},{1,3},{6,4},{4,6},{7,5},{5,7},{10,8},{8,10},{11,... | collective-permute-start | bytes 2162696 | tf_op jit(solution)/shard_map/ppermute | solution.py:106
  68.2 10.4 %collective-permute-start.12 = (bf16[2,128,1024]{2,1,0:T(8,128)(2,1)}, bf16[2,128,1024]{2,1,0:T(8,128)(2,1)}, u32[]{:S(2)}, u32[]{:S(2)}) collective-permute-start(bf16[2,128,1024]{2,1,0:T(8,128)(2,1)} %collective-permute-done.1), channel_id=1, source_target_pairs={{0,8},{8,16},{16,24},{24,28},{28,20},{20,12},{12,4},{4,0},{1,9},{9... | collective-permute-start | bytes 1572872 | tf_op jit(solution)/shard_map/ppermute | solution.py:132
  68.2 10.5 %collective-permute-start.11 = (bf16[2,128,1024]{2,1,0:T(8,128)(2,1)}, bf16[2,128,1024]{2,1,0:T(8,128)(2,1)}, u32[]{:S(2)}, u32[]{:S(2)}) collective-permute-start(bf16[2,128,1024]{2,1,0:T(8,128)(2,1)} %collective-permute-done), channel_id=1, source_target_pairs={{8,0},{16,8},{24,16},{28,24},{20,28},{12,20},{4,12},{0,4},{9,1},{1... | collective-permute-start | bytes 1572872 | tf_op jit(solution)/shard_map/ppermute | solution.py:133
  81.7 25.9 %collective-permute-start.14 = (bf16[2,128,1024]{2,1,0:T(8,128)(2,1)}, bf16[2,128,1024]{2,1,0:T(8,128)(2,1)S(1)}, u32[]{:S(2)}, u32[]{:S(2)}) collective-permute-start(bf16[2,128,1024]{2,1,0:T(8,128)(2,1)} %collective-permute-done.12), channel_id=1, source_target_pairs={{0,8},{8,16},{16,24},{24,28},{28,20},{20,12},{12,4},{4,0},{1,9},{9... | collective-permute-start | bytes 1572872 | tf_op jit(solution)/shard_map/ppermute | solution.py:132
  81.8 25.9 %collective-permute-start.13 = (bf16[2,128,1024]{2,1,0:T(8,128)(2,1)}, bf16[2,128,1024]{2,1,0:T(8,128)(2,1)S(1)}, u32[]{:S(2)}, u32[]{:S(2)}) collective-permute-start(bf16[2,128,1024]{2,1,0:T(8,128)(2,1)} %collective-permute-done.11), channel_id=1, source_target_pairs={{8,0},{16,8},{24,16},{28,24},{20,28},{12,20},{4,12},{0,4},{9,1},{1... | collective-permute-start | bytes 1572872 | tf_op jit(solution)/shard_map/ppermute | solution.py:133
  136.0 21.1 %collective-permute-start.17 = (bf16[64,1024]{1,0:T(8,128)(2,1)}, bf16[64,1024]{1,0:T(8,128)(2,1)}, u32[]{:S(2)}, u32[]{:S(2)}) collective-permute-start(bf16[64,1024]{1,0:T(8,128)(2,1)} %get-tuple-element.61), channel_id=1, source_target_pairs={{0,8},{8,16},{16,24},{24,28},{28,20},{20,12},{12,4},{4,0},{1,9},{9... | collective-permute-start | bytes 393224 | tf_op jit(solution)/shard_map/ppermute | solution.py:162
  137.7 19.3 %collective-permute-start.21 = (bf16[64,1024]{1,0:T(8,128)(2,1)}, bf16[64,1024]{1,0:T(8,128)(2,1)}, u32[]{:S(2)}, u32[]{:S(2)}) collective-permute-start(bf16[64,1024]{1,0:T(8,128)(2,1)} %get-tuple-element.62), channel_id=1, source_target_pairs={{8,0},{16,8},{24,16},{28,24},{20,28},{12,20},{4,12},{0,4},{9,1},{1... | collective-permute-start | bytes 393224 | tf_op jit(solution)/shard_map/ppermute | solution.py:163
  144.5 11.6 %all-to-all-start = ((f32[8,128,2]{1,2,0:T(2,128)}), f32[8,128,2]{1,2,0:T(2,128)S(1)}, u32[]{:S(2)}, u32[]{:S(2)}) async-start(f32[8,128,2]{1,2,0:T(2,128)} %broadcast_select_fusion), calls=%async_computation | async-start | bytes 16384 | tf_op jit(solution)/shard_map/all_to_all | solution.py:185
  150.3 11.0 %collective-permute-start.25 = (bf16[64,1024]{1,0:T(8,128)(2,1)}, bf16[64,1024]{1,0:T(8,128)(2,1)}, u32[]{:S(2)}, u32[]{:S(2)}) collective-permute-start(bf16[64,1024]{1,0:T(8,128)(2,1)} %get-tuple-element.59), channel_id=1, source_target_pairs={{0,8},{8,16},{16,24},{24,28},{28,20},{20,12},{12,4},{4,0},{1,9},{9... | collective-permute-start | bytes 393224 | tf_op jit(solution)/shard_map/ppermute | solution.py:162
  152.3 9.0 %collective-permute-start.29 = (bf16[64,1024]{1,0:T(8,128)(2,1)}, bf16[64,1024]{1,0:T(8,128)(2,1)}, u32[]{:S(2)}, u32[]{:S(2)}) collective-permute-start(bf16[64,1024]{1,0:T(8,128)(2,1)} %get-tuple-element.60), channel_id=1, source_target_pairs={{8,0},{16,8},{24,16},{28,24},{20,28},{12,20},{4,12},{0,4},{9,1},{1... | collective-permute-start | bytes 393224 | tf_op jit(solution)/shard_map/ppermute | solution.py:163
  159.1 9.3 %collective-permute-start.18 = (bf16[128,1024]{1,0:T(8,128)(2,1)S(1)}, bf16[128,1024]{1,0:T(8,128)(2,1)S(1)}, u32[]{:S(2)}, u32[]{:S(2)}) collective-permute-start(bf16[128,1024]{1,0:T(8,128)(2,1)S(1)} %pad_maximum_fusion.7), channel_id=1, source_target_pairs={{0,8},{8,16},{16,24},{24,28},{28,20},{20,12},{12,4},{4,0},{1,9},{9... | collective-permute-start | bytes 786440 | tf_op jit(solution)/shard_map/ppermute | solution.py:177
  159.7 9.3 %collective-permute-start.22 = (bf16[128,1024]{1,0:T(8,128)(2,1)S(1)}, bf16[128,1024]{1,0:T(8,128)(2,1)S(1)}, u32[]{:S(2)}, u32[]{:S(2)}) collective-permute-start(bf16[128,1024]{1,0:T(8,128)(2,1)S(1)} %pad_maximum_fusion.8), channel_id=1, source_target_pairs={{8,0},{16,8},{24,16},{28,24},{20,28},{12,20},{4,12},{0,4},{9,1},{1... | collective-permute-start | bytes 786440 | tf_op jit(solution)/shard_map/ppermute | solution.py:178
  162.4 11.7 %collective-permute-start.26 = (bf16[128,1024]{1,0:T(8,128)(2,1)S(1)}, bf16[128,1024]{1,0:T(8,128)(2,1)S(1)}, u32[]{:S(2)}, u32[]{:S(2)}) collective-permute-start(bf16[128,1024]{1,0:T(8,128)(2,1)S(1)} %pad_maximum_fusion.9), channel_id=1, source_target_pairs={{0,8},{8,16},{16,24},{24,28},{28,20},{20,12},{12,4},{4,0},{1,9},{9... | collective-permute-start | bytes 786440 | tf_op jit(solution)/shard_map/ppermute | solution.py:177
  162.9 11.7 %collective-permute-start.30 = (bf16[128,1024]{1,0:T(8,128)(2,1)S(1)}, bf16[128,1024]{1,0:T(8,128)(2,1)S(1)}, u32[]{:S(2)}, u32[]{:S(2)}) collective-permute-start(bf16[128,1024]{1,0:T(8,128)(2,1)S(1)} %pad_maximum_fusion.10), channel_id=1, source_target_pairs={{8,0},{16,8},{24,16},{28,24},{20,28},{12,20},{4,12},{0,4},{9,1},{1... | collective-permute-start | bytes 786440 | tf_op jit(solution)/shard_map/ppermute | solution.py:178
  169.1 10.6 %collective-permute-start.19 = (bf16[128,1024]{1,0:T(8,128)(2,1)S(1)}, bf16[128,1024]{1,0:T(8,128)(2,1)S(1)}, u32[]{:S(2)}, u32[]{:S(2)}) collective-permute-start(bf16[128,1024]{1,0:T(8,128)(2,1)S(1)} %get-tuple-element.37), channel_id=1, source_target_pairs={{0,8},{8,16},{16,24},{24,28},{28,20},{20,12},{12,4},{4,0},{1,9},{9... | collective-permute-start | bytes 786440 | tf_op jit(solution)/shard_map/ppermute | solution.py:177
  169.8 10.4 %collective-permute-start.23 = (bf16[128,1024]{1,0:T(8,128)(2,1)S(1)}, bf16[128,1024]{1,0:T(8,128)(2,1)S(1)}, u32[]{:S(2)}, u32[]{:S(2)}) collective-permute-start(bf16[128,1024]{1,0:T(8,128)(2,1)S(1)} %get-tuple-element.38), channel_id=1, source_target_pairs={{8,0},{16,8},{24,16},{28,24},{20,28},{12,20},{4,12},{0,4},{9,1},{1... | collective-permute-start | bytes 786440 | tf_op jit(solution)/shard_map/ppermute | solution.py:178
  174.7 10.6 %collective-permute-start.27 = (bf16[128,1024]{1,0:T(8,128)(2,1)S(1)}, bf16[128,1024]{1,0:T(8,128)(2,1)S(1)}, u32[]{:S(2)}, u32[]{:S(2)}) collective-permute-start(bf16[128,1024]{1,0:T(8,128)(2,1)S(1)} %get-tuple-element.33), channel_id=1, source_target_pairs={{0,8},{8,16},{16,24},{24,28},{28,20},{20,12},{12,4},{4,0},{1,9},{9... | collective-permute-start | bytes 786440 | tf_op jit(solution)/shard_map/ppermute | solution.py:177
  175.4 10.4 %collective-permute-start.31 = (bf16[128,1024]{1,0:T(8,128)(2,1)S(1)}, bf16[128,1024]{1,0:T(8,128)(2,1)S(1)}, u32[]{:S(2)}, u32[]{:S(2)}) collective-permute-start(bf16[128,1024]{1,0:T(8,128)(2,1)S(1)} %get-tuple-element.34), channel_id=1, source_target_pairs={{8,0},{16,8},{24,16},{28,24},{20,28},{12,20},{4,12},{0,4},{9,1},{1... | collective-permute-start | bytes 786440 | tf_op jit(solution)/shard_map/ppermute | solution.py:178
  180.4 9.3 %collective-permute-start.24 = (bf16[128,1024]{1,0:T(8,128)(2,1)S(1)}, bf16[128,1024]{1,0:T(8,128)(2,1)S(1)}, u32[]{:S(2)}, u32[]{:S(2)}) collective-permute-start(bf16[128,1024]{1,0:T(8,128)(2,1)S(1)} %get-tuple-element.32), channel_id=1, source_target_pairs={{8,0},{16,8},{24,16},{28,24},{20,28},{12,20},{4,12},{0,4},{9,1},{1... | collective-permute-start | bytes 786440 | tf_op jit(solution)/shard_map/ppermute | solution.py:178
  (33 other events, 432.6 us)

commit v2 on v0

v2 whole, which is shorter than its diff:
```python
import functools

import jax
import jax.numpy as jnp
from jax import lax
from jax.experimental import pallas as pl
from jax.experimental.pallas import tpu as pltpu
from jax.sharding import PartitionSpec as P

NT = (((1,), (1,)), ((), ()))
NN = (((1,), (0,)), ((), ()))


def dot(a, b, dims):
    return lax.dot_general(a, b, dims, preferred_element_type=jnp.float32)


def part_kernel(layout, blocks, has_prior, is_last, *refs):
    held = len(layout)
    arrays = sum(len(of_expert) for of_expert in layout)
    block_refs, gate_ref, refs = refs[:blocks], refs[blocks], refs[blocks + 1 :]
    weight_refs, refs = refs[:arrays], refs[arrays:]
    prior, refs = (refs[:3], refs[3:]) if has_prior else ((), refs)
    results, (token_buf, weight_buf, mixed_buf, back_buf, grad_buf, token_sem, weight_sem, sum_sem) = refs[:3], refs[3:]
    tokens = block_refs[0].shape[1]
    rows, hidden = token_buf.shape[1], weight_buf.shape[1]
    share = hidden // held

    def weight_copies(kind):
        copies, index = [], 0
        for e, of_expert in enumerate(layout):
            at = e * share
            for units in of_expert:
                source = weight_refs[index].at[pl.ds(kind * units, units)]
                target = weight_buf.at[kind, pl.ds(at, units)]
                copies.append(pltpu.make_async_copy(source, target, weight_sem.at[kind, index]))
                at, index = at + units, index + 1
        return copies

    def token_copies(which):
        return [
            pltpu.make_async_copy(
                block_refs[b].at[which], token_buf.at[which, pl.ds(b * tokens, tokens)], token_sem.at[which, b]
            )
            for b in range(blocks)
        ]

    sums = (mixed_buf, back_buf, grad_buf)
    prior_copies = [pltpu.make_async_copy(prior[i], sums[i], sum_sem.at[i]) for i in range(len(prior))]

    def start(copies):
        for copy in copies:
            copy.start()

    def wait(copies):
        for copy in copies:
            copy.wait()

    def hand_on(i, value):
        if has_prior:
            wait(prior_copies[i : i + 1])
            value = value + sums[i][...]
        if is_last:
            results[i][...] = value
            return []
        sums[i][...] = value
        copy = pltpu.make_async_copy(sums[i], results[i], sum_sem.at[i])
        copy.start()
        return [copy]

    start(token_copies(0) + weight_copies(0) + weight_copies(1) + token_copies(1) + weight_copies(2) + prior_copies)
    unit = lax.broadcasted_iota(jnp.int32, (rows, hidden), 1)
    gate = jnp.broadcast_to(gate_ref[:, 0:1], (rows, hidden))
    for e in range(1, held):
        gate = jnp.where(unit >= e * share, gate_ref[:, e : e + 1], gate)
    wait(token_copies(0) + weight_copies(0))
    gate_val = dot(token_buf[0], weight_buf[0], NT)
    wait(weight_copies(1))
    up_val = dot(token_buf[0], weight_buf[1], NT)
    wait(token_copies(1) + weight_copies(2))
    d_out = dot(token_buf[1], weight_buf[2], NT)
    sig = jax.nn.sigmoid(gate_val)
    silu = gate_val * sig
    act = silu * up_val
    d_act = gate * d_out
    d_gate = (d_act * up_val * (sig + silu * (1.0 - sig))).astype(jnp.bfloat16)
    d_up = (d_act * silu).astype(jnp.bfloat16)
    mixed = dot((gate * act).astype(jnp.bfloat16), weight_buf[2], NN)
    leaving = hand_on(0, mixed)
    product = act * d_out
    column = lax.broadcasted_iota(jnp.int32, grad_buf.shape, 1)
    gate_grads = jnp.zeros(grad_buf.shape, jnp.float32)
    for e in range(held):
        mine = (unit >= e * share) & (unit < (e + 1) * share)
        total = jnp.sum(jnp.where(mine, product, 0.0), axis=1, keepdims=True)
        gate_grads = jnp.where(column == e, total, gate_grads)
    leaving += hand_on(2, gate_grads)
    back = dot(d_gate, weight_buf[0], NN) + dot(d_up, weight_buf[1], NN)
    leaving += hand_on(1, back)
    wait(leaving)


def experts_part(blocks, gate, part, prior, is_last):
    tokens, width = blocks[0].shape[1:]
    rows, held = len(blocks) * tokens, len(part)
    layout = [[w.shape[0] // 3 for w in of_expert] for of_expert in part]
    hidden = held * sum(layout[0])
    flat = [w for of_expert in part for w in of_expert]
    vmem, hbm = pl.BlockSpec(memory_space=pltpu.VMEM), pl.BlockSpec(memory_space=pltpu.HBM)
    sums = [(rows, width), (rows, width), (rows, 128)]
    return pl.pallas_call(
        functools.partial(part_kernel, layout, len(blocks), bool(prior), is_last),
        out_shape=tuple(jax.ShapeDtypeStruct(shape, jnp.float32) for shape in sums),
        in_specs=[hbm] * len(blocks) + [vmem] + [hbm] * (len(flat) + len(prior)),
        out_specs=(vmem if is_last else hbm,) * 3,
        scratch_shapes=[
            pltpu.VMEM((2, rows, width), jnp.bfloat16),
            pltpu.VMEM((3, hidden, width), jnp.bfloat16),
            *(pltpu.VMEM(shape, jnp.float32) for shape in sums),
            pltpu.SemaphoreType.DMA((2, len(blocks))),
            pltpu.SemaphoreType.DMA((3, len(flat))),
            pltpu.SemaphoreType.DMA((3,)),
        ],
        compiler_params=pltpu.CompilerParams(vmem_limit_bytes=32 << 20),
        cost_estimate=pl.CostEstimate(
            flops=12 * rows * width * hidden,
            bytes_accessed=6 * hidden * width + 12 * rows * width,
            transcendentals=rows * hidden,
        ),
    )(*blocks, gate, *flat, *prior)


def ring_order(n):
    return [0, 2, 4, 6, 7, 5, 3, 1] if n == 8 else list(range(n))


def after(a, *others):
    return lax.optimization_barrier((a, *others))[0]


def local(hidden_rows, out_grad, gates, routes, w_gate, w_up, w_down):
    tokens, width = hidden_rows.shape
    n, n_dp, n_seq = lax.axis_size("expert"), lax.axis_size("dp"), lax.axis_size("seq")
    here = w_gate.shape[0]
    held = n_seq * here
    experts = n * held
    order = ring_order(n)
    fw = [(order[i], order[(i + 1) % n]) for i in range(n)]
    bw = [(b, a) for a, b in fw]
    me, my_seq = lax.axis_index("expert"), lax.axis_index("seq")
    few = n <= 8
    reach, far, even, half = (n - 1) // 2, n // 2, n % 2 == 0, tokens // 2

    def shifted(a, axis, size, by):
        return lax.ppermute(a, axis, [((i + by) % size, i) for i in range(size)])

    def around(a, way):
        return lax.ppermute(a, "expert", way)

    names = jnp.arange(experts, dtype=jnp.int32)
    chosen = routes.T[None] == names[:, None, None]
    dense = jnp.sum(jnp.where(chosen, gates.T[None], 0.0), axis=1)
    gates_by_chip = lax.all_to_all(dense.reshape(n, held, tokens), "expert", split_axis=0, concat_axis=0, tiled=True)

    units = w_down.shape[1]
    cuts = [0, units // 256 * 256, units] if few and units > 256 and units % 256 else [0, units]
    kinds = [jnp.swapaxes(w_gate, 1, 2), jnp.swapaxes(w_up, 1, 2), w_down]
    own = [
        [jnp.concatenate([w[i, low:high] for w in kinds]) for low, high in zip(cuts, cuts[1:])] for i in range(here)
    ]

    def by_core(share):
        return share + [[shifted(w, "seq", n_seq, r) for w in e] for r in range(1, n_seq) for e in share]

    first = by_core(own)
    groups = [[0, 1, -1]] + [[s, -s] for s in range(2, reach + 1)] + ([[far]] if even else [])

    found = [d % n for group in groups for d in group]
    chips = [[order[(order.index(i) + d) % n] for d in found] for i in range(n)]
    mine = me == jnp.arange(n, dtype=jnp.int32)
    chip_at = jnp.sum(jnp.where(mine[:, None], jnp.array(chips, jnp.int32), 0), axis=0)
    at_chip = chip_at[:, None] == jnp.arange(n, dtype=jnp.int32)
    slots = [[((c + e // here) % n_seq) * here + e % here for e in range(held)] for c in range(n_seq)]
    slot_of = jnp.sum(
        jnp.where((my_seq == jnp.arange(n_seq, dtype=jnp.int32))[:, None], jnp.array(slots, jnp.int32), 0), axis=0
    )
    in_slot = slot_of[:, None] == jnp.arange(held, dtype=jnp.int32)
    picked = at_chip[:, None, :, None] & in_slot[None, :, None, :]
    gate_rows = jnp.sum(jnp.where(picked[..., None], gates_by_chip[None, None], 0.0), axis=(2, 3))
    gate_rows = gate_rows.transpose(0, 2, 1).reshape(n * tokens, held)
    starts = [sum(len(group) for group in groups[:g]) * tokens for g in range(len(groups) + 1)]
    gate_in = [gate_rows[a:b] for a, b in zip(starts, starts[1:])]
    done = [() for _ in groups]
    last = []

    def work(g, part, is_last, *wait_for):
        gate = after(gate_in[g], *last, *wait_for)
        done[g] = experts_part([arrived[d] for d in groups[g]], gate, part, done[g], is_last)
        last[:] = [done[g][2]]

    arrived = {0: jnp.stack([hidden_rows, out_grad])}
    for s in range(1, reach + 1):
        ahead, behind = arrived[1 - s], arrived[s - 1]
        if few and s > 2:
            work(s - 3, first, False)
            ahead, behind = after(ahead, *last), after(behind, *last)
        arrived[-s], arrived[s] = around(ahead, fw), around(behind, bw)
    if few and reach > 1:
        work(reach - 2, first, False)
    if even:
        top = around(after(arrived[1 - far][:, :half], *last), fw)
        low = around(after(arrived[far - 1][:, half:], *last), bw)
        arrived[far] = jnp.concatenate([top, low], axis=1)

    others = []
    for r in range(1, n_dp):
        share = []
        for e in own:
            sent = [w if c == 0 else after(w, arrived[1][0, :1]) for c, w in enumerate(e)]
            share.append([after(shifted(w, "dp", n_dp, r), *last) for w in sent])
        others.append(by_core(share))
    rest = [[w for share in others for w in share[e]] for e in range(held)]
    whole = [first[e] + rest[e] for e in range(held)]
    if few:
        work(reach - 1, first, False)

    def finish(g, *wait_for):
        work(g, rest if done[g] else whole, True, *wait_for)
        mixed, back, _ = done[g]
        return [(mixed[i * tokens : (i + 1) * tokens], back[i * tokens : (i + 1) * tokens]) for i in range(len(groups[g]))]

    def rounded(a):
        return a.astype(jnp.bfloat16)

    def plus(part, travelled):
        return part + travelled.astype(jnp.float32)

    came_fw = came_bw = None
    before = []
    if even:
        ((mixed, back),) = finish(len(groups) - 1)
        came_fw = [around(rounded(a[:half]), fw) for a in (mixed, back)]
        came_bw = [around(rounded(a[half:]), bw) for a in (mixed, back)]
    for s in range(reach, 0, -1):
        sums = finish(s - 1, *before)
        parts_fw, parts_bw = sums[-2:]
        if came_fw is None:
            out_fw, out_bw = [rounded(a) for a in parts_fw], [rounded(a) for a in parts_bw]
        elif came_fw[0].shape[0] < tokens:
            out_fw = [rounded(jnp.concatenate([plus(a[:half], t), a[half:]])) for a, t in zip(parts_fw, came_fw)]
            out_bw = [rounded(jnp.concatenate([a[:half], plus(a[half:], t)])) for a, t in zip(parts_bw, came_bw)]
        else:
            out_fw = [rounded(plus(a, t)) for a, t in zip(parts_fw, came_fw)]
            out_bw = [rounded(plus(a, t)) for a, t in zip(parts_bw, came_bw)]
        before = [] if came_fw is None else [came_fw[0], came_bw[0]]
        came_fw, came_bw = [around(a, fw) for a in out_fw], [around(a, bw) for a in out_bw]
    mixed, grad_rows = [rounded(plus(plus(a, f), b)) for a, f, b in zip(sums[0], came_fw, came_bw)]

    grads = jnp.concatenate([results[2] for results in done])[:, :held].T.reshape(held, n, tokens)
    to_chip = jnp.sum(jnp.where(picked[..., None], grads.transpose(1, 0, 2)[:, :, None, None], 0.0), axis=(0, 1))
    to_chip = after(to_chip, *out_fw, *out_bw)
    by_expert = lax.all_to_all(to_chip, "expert", split_axis=0, concat_axis=0, tiled=True).reshape(experts, tokens)
    grad_gates = jnp.sum(jnp.where(chosen, by_expert[:, None, :], 0.0), axis=0).T
    return (mixed, grad_rows, grad_gates)


def solution(mesh):
    tokens = P(("groups", "expert", "dp", "seq"), None)
    in_specs = (tokens,) * 4 + (P(("expert", "seq"), None, "dp"),) * 2 + (P(("expert", "seq"), "dp", None),)
    return jax.shard_map(local, mesh=mesh, in_specs=in_specs, out_specs=(tokens,) * 3, check_vma=False)
```

time: 242 us -> 141 us (0.58)
  the two profiles are of different devices: /device:TPU:13 before, /device:TPU:0 now
where the time goes in v2:
time: 141 us; the launch traced here: 140 us
  Pallas kernels  50.2 us (36%)
  starting transfers between devices  39.6 us (28%)
  waiting for transfers between devices  27.6 us (20%)
  other arithmetic  12.8 us (9%)
  local copies, waits for them, and re-layouts  8.97 us (6%)
    pallas_call x7, Pallas kernels, experts_part(): pl.pallas_call(functools.partial(part_kernel, layout, len(blocks), bool(p...  50.2 us
    ppermute x24, starting transfers between devices, around(): return lax.ppermute(a, 'expert', way)  26.1 us
    ppermute x6, waiting for transfers between devices, shifted(): return lax.ppermute(a, axis, [((i + by) % size, i) for i in range(size)])  12.9 us
    convert_element_type x6, other arithmetic, rounded(): return a.astype(jnp.bfloat16)  8.33 us
    ppermute x24, waiting for transfers between devices, around(): return lax.ppermute(a, 'expert', way)  6.31 us
    all_to_all x1, starting transfers between devices, local(): lax.all_to_all(dense.reshape(n, held, tokens), 'expert', split_axis=0, co...  5.83 us
    all_to_all x1, waiting for transfers between devices, local(): lax.all_to_all(to_chip, 'expert', split_axis=0, concat_axis=0, tiled=True)  4.65 us
    all_to_all x1, starting transfers between devices, local(): lax.all_to_all(to_chip, 'expert', split_axis=0, concat_axis=0, tiled=True)  4.49 us
  transfers between devices with their start and end apart: 32, of which 8 were waited for; matrix products, arithmetic and copies ran while one was open for 13% of the time, Pallas kernels for 30%

profile of v2, /device:TPU:0, one launch (start us, length us, event | category | flops | bytes accessed | tf_op | source)
XLA Modules:
  0.0 140.3 jit_solution(15828176070654404767)
XLA Ops:
  1.9 3.1 %collective-permute-start.1 = (bf16[2,128,1024]{2,1,0:T(8,128)(2,1)S(1)}, bf16[2,128,1024]{2,1,0:T(8,128)(2,1)}, u32[]{:S(2)}, u32[]{:S(2)}) collective-permute-start(bf16[2,128,1024]{2,1,0:T(8,128)(2,1)S(1)} %pad_maximum_fusion.5.refs_0_), channel_id=1, source_target_pairs={{0,8},{8,16},{16,24},{24,28},{28,20},{20,12},{12,4},{4,0},{1,9},{9... | collective-permute-start | bytes 1572872 | tf_op jit(solution)/shard_map/ppermute | solution.py:158
  6.3 2.0 %collective-permute-start.10 = (bf16[768,1024]{1,0:T(8,128)(2,1)S(1)}, bf16[768,1024]{1,0:T(8,128)(2,1)}, u32[]{:S(2)}, u32[]{:S(2)}) collective-permute-start(bf16[768,1024]{1,0:T(8,128)(2,1)S(1)} %pad_maximum_fusion.refs_4_.refs_3_.refs_2_), channel_id=1, source_target_pairs={{2,0},{0,2},{3,1},{1,3},{6,4},{4,6},{7,5},{5,7},{10,8},{8,10},{11,... | collective-permute-start | bytes 4718600 | tf_op jit(solution)/shard_map/ppermute | solution.py:155
  8.9 5.8 %all-to-all-start = ((f32[8,2,128]{2,1,0:T(2,128)}), f32[8,2,128]{2,1,0:T(2,128)S(1)}, u32[]{:S(2)}, u32[]{:S(2)}) async-start(f32[8,2,128]{2,1,0:T(2,128)} %bitcast.4), calls=%async_computation | async-start | bytes 16384 | tf_op jit(solution)/shard_map/all_to_all | solution.py:163
  17.5 3.8 %all-to-all-done = f32[8,2,128]{2,1,0:T(2,128)S(1)} async-done(((f32[8,2,128]{2,1,0:T(2,128)}), f32[8,2,128]{2,1,0:T(2,128)S(1)}, u32[]{:S(2)}, u32[]{:S(2)}) %all-to-all-start) | async-done | bytes 8224 | tf_op jit(solution)/shard_map/all_to_all | solution.py:163
  24.0 1.5 %collective-permute-start.2 = (bf16[2,128,1024]{2,1,0:T(8,128)(2,1)}, bf16[2,128,1024]{2,1,0:T(8,128)(2,1)S(1)}, u32[]{:S(2)}, u32[]{:S(2)}) collective-permute-start(bf16[2,128,1024]{2,1,0:T(8,128)(2,1)} %collective-permute-done.refs_1_), channel_id=1, source_target_pairs={{8,0},{16,8},{24,16},{28,24},{20,28},{12,20},{4,12},{0,4},{9,1},{1... | collective-permute-start | bytes 1572872 | tf_op jit(solution)/shard_map/ppermute | solution.py:158
  26.5 8.0 %shard_map.112 = (f32[384,1024]{1,0:T(8,128)S(1)}, f32[384,1024]{1,0:T(8,128)S(1)}, f32[384,128]{1,0:T(8,128)S(1)}) custom-call(bf16[2,128,1024]{2,1,0:T(8,128)(2,1)S(1)} %pad_maximum_fusion.5.refs_0_, bf16[2,128,1024]{2,1,0:T(8,128)(2,1)} %collective-permute-done.refs_1_, bf16[2,128,1024]{2,1,0:T(8,128)(2,1)} %collective-permute-done.1.refs_2_, ...), custom_call_target="tpu_custom_call" | custom-call | flops 3321888768 | bytes 9043968 | tf_op jit(solution)/shard_map/pallas_call | solution.py:111
  34.5 2.1 %collective-permute-done.3.refs_1_ = bf16[2,128,1024]{2,1,0:T(8,128)(2,1)S(1)} collective-permute-done((bf16[2,128,1024]{2,1,0:T(8,128)(2,1)}, bf16[2,128,1024]{2,1,0:T(8,128)(2,1)S(1)}, u32[]{:S(2)}, u32[]{:S(2)}) %collective-permute-start.3) | collective-permute-done | bytes 524320 | tf_op jit(solution)/shard_map/ppermute | solution.py:158
  36.8 6.2 %shard_map.113 = (f32[256,1024]{1,0:T(8,128)S(1)}, f32[256,1024]{1,0:T(8,128)S(1)}, f32[256,128]{1,0:T(8,128)S(1)}) custom-call(bf16[2,128,1024]{2,1,0:T(8,128)(2,1)S(1)} %collective-permute-done.2.refs_0_, bf16[2,128,1024]{2,1,0:T(8,128)(2,1)S(1)} %collective-permute-done.3.refs_1_, f32[256,2]{1,0:T(8,128)S(1)} %bitcast.34, ...), custom_call_target="tpu_custom_call" | custom-call | flops 2214592512 | bytes 7471104 | tf_op jit(solution)/shard_map/pallas_call | solution.py:111
  44.0 1.5 %collective-permute-start.6 = (bf16[2,128,1024]{2,1,0:T(8,128)(2,1)S(1)}, bf16[2,128,1024]{2,1,0:T(8,128)(2,1)S(1)}, u32[]{:S(2)}, u32[]{:S(2)}) collective-permute-start(bf16[2,128,1024]{2,1,0:T(8,128)(2,1)S(1)} %collective-permute-done.2.refs_0_), channel_id=1, source_target_pairs={{8,0},{16,8},{24,16},{28,24},{20,28},{12,20},{4,12},{0,4},{9,1},{1... | collective-permute-start | bytes 1572872 | tf_op jit(solution)/shard_map/ppermute | solution.py:158
  46.0 12.9 %collective-permute-done.11.refs_5_.refs_4_ = bf16[288,1024]{1,0:T(8,128)(2,1)S(1)} collective-permute-done((bf16[288,1024]{1,0:T(8,128)(2,1)S(1)}, bf16[288,1024]{1,0:T(8,128)(2,1)S(1)}, u32[]{:S(2)}, u32[]{:S(2)}) %collective-permute-start.11) | collective-permute-done | bytes 589856 | tf_op jit(solution)/shard_map/ppermute | solution.py:155
  62.2 6.2 %shard_map.114 = (f32[256,1024]{1,0:T(8,128)S(1)}, f32[256,1024]{1,0:T(8,128)S(1)}, f32[256,128]{1,0:T(8,128)S(1)}) custom-call(bf16[2,128,1024]{2,1,0:T(8,128)(2,1)S(1)} %collective-permute-done.6.refs_0_, bf16[2,128,1024]{2,1,0:T(8,128)(2,1)S(1)} %collective-permute-done.7.refs_1_, f32[256,2]{1,0:T(8,128)S(1)} %bitcast.36, ...), custom_call_target="tpu_custom_call" | custom-call | flops 2214592512 | bytes 7471104 | tf_op jit(solution)/shard_map/pallas_call | solution.py:111
  68.5 8.3 %shard_map.115 = (f32[128,1024]{1,0:T(8,128)S(1)}, f32[128,1024]{1,0:T(8,128)S(1)}, f32[128,128]{1,0:T(8,128)S(1)}) custom-call(bf16[2,128,1024]{2,1,0:T(8,128)(2,1)S(1)} %pad_maximum_fusion.6.refs_0_, f32[128,2]{1,0:T(8,128)S(1)} %slice_bitcast_fusion.6.refs_1_, bf16[768,1024]{1,0:T(8,128)(2,1)S(1)} %pad_maximum_fusion.refs_4_.refs_3_.refs_2_, ...), custom_call_target="tpu_custom_call" | custom-call | flops 2214592512 | bytes 10223616 | tf_op jit(solution)/shard_map/pallas_call | solution.py:111
  81.1 6.6 %shard_map.116 = (f32[256,1024]{1,0:T(8,128)S(1)}, f32[256,1024]{1,0:T(8,128)S(1)}, f32[256,128]{1,0:T(8,128)S(1)}) custom-call(bf16[2,128,1024]{2,1,0:T(8,128)(2,1)S(1)} %collective-permute-done.6.refs_0_, bf16[2,128,1024]{2,1,0:T(8,128)(2,1)S(1)} %collective-permute-done.7.refs_1_, f32[256,2]{1,0:T(8,128)S(1)} %bitcast.37, ...), custom_call_target="tpu_custom_call" | custom-call | flops 2214592512 | bytes 7471104 | tf_op jit(solution)/shard_map/pallas_call | solution.py:111
  88.0 1.6 %collective-permute-start.17 = (bf16[128,1024]{1,0:T(8,128)(2,1)S(1)}, bf16[128,1024]{1,0:T(8,128)(2,1)S(1)}, u32[]{:S(2)}, u32[]{:S(2)}) collective-permute-start(bf16[128,1024]{1,0:T(8,128)(2,1)S(1)} %pad_maximum_fusion.8), channel_id=1, source_target_pairs={{8,0},{16,8},{24,16},{28,24},{20,28},{12,20},{4,12},{0,4},{9,1},{1... | collective-permute-start | bytes 786440 | tf_op jit(solution)/shard_map/ppermute | solution.py:158
  90.3 1.6 %collective-permute-start.27 = (bf16[128,1024]{1,0:T(8,128)(2,1)S(1)}, bf16[128,1024]{1,0:T(8,128)(2,1)S(1)}, u32[]{:S(2)}, u32[]{:S(2)}) collective-permute-start(bf16[128,1024]{1,0:T(8,128)(2,1)S(1)} %pad_maximum_fusion.10), channel_id=1, source_target_pairs={{8,0},{16,8},{24,16},{28,24},{20,28},{12,20},{4,12},{0,4},{9,1},{1... | collective-permute-start | bytes 786440 | tf_op jit(solution)/shard_map/ppermute | solution.py:158
  92.6 6.6 %shard_map.117 = (f32[256,1024]{1,0:T(8,128)S(1)}, f32[256,1024]{1,0:T(8,128)S(1)}, f32[256,128]{1,0:T(8,128)S(1)}) custom-call(bf16[2,128,1024]{2,1,0:T(8,128)(2,1)S(1)} %collective-permute-done.2.refs_0_, bf16[2,128,1024]{2,1,0:T(8,128)(2,1)S(1)} %collective-permute-done.3.refs_1_, f32[256,2]{1,0:T(8,128)S(1)} %bitcast.35, ...), custom_call_target="tpu_custom_call" | custom-call | flops 2214592512 | bytes 7471104 | tf_op jit(solution)/shard_map/pallas_call | solution.py:111
  102.1 8.4 %shard_map.118 = (f32[384,1024]{1,0:T(8,128)S(1)}, f32[384,1024]{1,0:T(8,128)S(1)}, f32[384,128]{1,0:T(8,128)S(1)}) custom-call(bf16[2,128,1024]{2,1,0:T(8,128)(2,1)S(1)} %copy-done.1, bf16[2,128,1024]{2,1,0:T(8,128)(2,1)} %collective-permute-done.refs_1_, bf16[2,128,1024]{2,1,0:T(8,128)(2,1)} %collective-permute-done.1.refs_2_, f32[384,2]{1,0:T(8,128)S(1)} %bitcast.33, ...), custom_call_target="tpu_custom_call" | custom-call | flops 3321888768 | bytes 9043968 | tf_op jit(solution)/shard_map/pallas_call | solution.py:111
  115.7 2.0 %add_convert_fusion.8 = (bf16[128,1024]{1,0:T(8,128)(2,1)}, bf16[128,1024]{1,0:T(8,128)(2,1)}) fusion(bf16[128,1024]{1,0:T(8,128)(2,1)} %collective-permute-done.18, f32[384,1024]{1,0:T(8,128)S(1)} %get-tuple-element.63, bf16[128,1024]{1,0:T(8,128)(2,1)} %collective-permute-done.20), kind=kLoop, calls=%fused_computation.17 | loop fusion | flops 786432 | bytes 2097152 | tf_op jit(solution)/shard_map/convert_element_type | solution.py:233
  119.7 2.7 %collective-permute-done.24 = bf16[128,1024]{1,0:T(8,128)(2,1)S(1)} collective-permute-done((bf16[128,1024]{1,0:T(8,128)(2,1)}, bf16[128,1024]{1,0:T(8,128)(2,1)S(1)}, u32[]{:S(2)}, u32[]{:S(2)}) %collective-permute-start.24) | collective-permute-done | bytes 262176 | tf_op jit(solution)/shard_map/ppermute | solution.py:158
  124.9 4.5 %all-to-all-start.1 = ((f32[8,2,128]{2,1,0:T(2,128)}), f32[8,2,128]{2,1,0:T(2,128)S(1)}, u32[]{:S(2)}, u32[]{:S(2)}) async-start(f32[8,2,128]{2,1,0:T(2,128)} %copy.23), calls=%async_computation.1 | async-start | bytes 16384 | tf_op jit(solution)/shard_map/all_to_all | solution.py:262
  129.4 2.0 %collective-permute-start.25 = (bf16[128,1024]{1,0:T(8,128)(2,1)}, bf16[128,1024]{1,0:T(8,128)(2,1)}, u32[]{:S(2)}, u32[]{:S(2)}) collective-permute-start(bf16[128,1024]{1,0:T(8,128)(2,1)} %get-tuple-element.71), channel_id=1, source_target_pairs={{0,8},{8,16},{16,24},{24,28},{28,20},{20,12},{12,4},{4,0},{1,9},{9... | collective-permute-start | bytes 786440 | tf_op jit(solution)/shard_map/ppermute | solution.py:158
  131.5 4.6 %all-to-all-done.1 = f32[8,2,128]{2,1,0:T(2,128)S(1)} async-done(((f32[8,2,128]{2,1,0:T(2,128)}), f32[8,2,128]{2,1,0:T(2,128)S(1)}, u32[]{:S(2)}, u32[]{:S(2)}) %all-to-all-start.1) | async-done | bytes 8224 | tf_op jit(solution)/shard_map/all_to_all | solution.py:262
  136.7 1.8 %add_convert_fusion.5 = bf16[128,1024]{1,0:T(8,128)(2,1)} fusion(bf16[128,1024]{1,0:T(8,128)(2,1)} %collective-permute-done.21, bf16[128,1024]{1,0:T(8,128)(2,1)S(1)} %collective-permute-done.19, f32[384,1024]{1,0:T(8,128)S(1)} %get-tuple-element.63), kind=kLoop, calls=%fused_computation.14 | loop fusion | flops 655360 | bytes 1310720 | tf_op jit(solution)/shard_map/convert_element_type | solution.py:233
  138.5 1.8 %add_convert_fusion = bf16[128,1024]{1,0:T(8,128)(2,1)} fusion(bf16[128,1024]{1,0:T(8,128)(2,1)} %collective-permute-done.29, bf16[128,1024]{1,0:T(8,128)(2,1)} %collective-permute-done.25, f32[384,1024]{1,0:T(8,128)S(1)} %get-tuple-element.65), kind=kLoop, calls=%fused_computation.9 | loop fusion | flops 655360 | bytes 1310720 | tf_op jit(solution)/shard_map/convert_element_type | solution.py:233
  (112 shorter events, 33.6 us)
Async XLA Ops:
  1.9 21.6 %collective-permute-start.1 = (bf16[2,128,1024]{2,1,0:T(8,128)(2,1)S(1)}, bf16[2,128,1024]{2,1,0:T(8,128)(2,1)}, u32[]{:S(2)}, u32[]{:S(2)}) collective-permute-start(bf16[2,128,1024]{2,1,0:T(8,128)(2,1)S(1)} %pad_maximum_fusion.5.refs_0_), channel_id=1, source_target_pairs={{0,8},{8,16},{16,24},{24,28},{28,20},{20,12},{12,4},{4,0},{1,9},{9... | collective-permute-start | bytes 1572872 | tf_op jit(solution)/shard_map/ppermute | solution.py:158
  4.9 19.1 %collective-permute-start = (bf16[2,128,1024]{2,1,0:T(8,128)(2,1)S(1)}, bf16[2,128,1024]{2,1,0:T(8,128)(2,1)}, u32[]{:S(2)}, u32[]{:S(2)}) collective-permute-start(bf16[2,128,1024]{2,1,0:T(8,128)(2,1)S(1)} %pad_maximum_fusion.5.refs_0_), channel_id=1, source_target_pairs={{8,0},{16,8},{24,16},{28,24},{20,28},{12,20},{4,12},{0,4},{9,1},{1... | collective-permute-start | bytes 1572872 | tf_op jit(solution)/shard_map/ppermute | solution.py:158
  6.3 36.8 %collective-permute-start.10 = (bf16[768,1024]{1,0:T(8,128)(2,1)S(1)}, bf16[768,1024]{1,0:T(8,128)(2,1)}, u32[]{:S(2)}, u32[]{:S(2)}) collective-permute-start(bf16[768,1024]{1,0:T(8,128)(2,1)S(1)} %pad_maximum_fusion.refs_4_.refs_3_.refs_2_), channel_id=1, source_target_pairs={{2,0},{0,2},{3,1},{1,3},{6,4},{4,6},{7,5},{5,7},{10,8},{8,10},{11,... | collective-permute-start | bytes 4718600 | tf_op jit(solution)/shard_map/ppermute | solution.py:155
  8.3 18.2 %collective-permute-start.4 = (bf16[768,1024]{1,0:T(8,128)(2,1)S(1)}, bf16[768,1024]{1,0:T(8,128)(2,1)}, u32[]{:S(2)}, u32[]{:S(2)}) collective-permute-start(bf16[768,1024]{1,0:T(8,128)(2,1)S(1)} %pad_maximum_fusion.refs_4_.refs_3_.refs_2_), channel_id=1, source_target_pairs={{1,0},{0,1},{3,2},{2,3},{5,4},{4,5},{7,6},{6,7},{9,8},{8,9},{11,10... | collective-permute-start | bytes 4718600 | tf_op jit(solution)/shard_map/ppermute | solution.py:155
  8.9 12.4 %all-to-all-start = ((f32[8,2,128]{2,1,0:T(2,128)}), f32[8,2,128]{2,1,0:T(2,128)S(1)}, u32[]{:S(2)}, u32[]{:S(2)}) async-start(f32[8,2,128]{2,1,0:T(2,128)} %bitcast.4), calls=%async_computation | async-start | bytes 16384 | tf_op jit(solution)/shard_map/all_to_all | solution.py:163
  16.8 9.7 %collective-permute-start.5 = (bf16[288,1024]{1,0:T(8,128)(2,1)S(1)}, bf16[288,1024]{1,0:T(8,128)(2,1)S(1)}, u32[]{:S(2)}, u32[]{:S(2)}) collective-permute-start(bf16[288,1024]{1,0:T(8,128)(2,1)S(1)} %pad_maximum_fusion.1.refs_5_.refs_4_.refs_3_), channel_id=1, source_target_pairs={{1,0},{0,1},{3,2},{2,3},{5,4},{4,5},{7,6},{6,7},{9,8},{8,9},{11,10... | collective-permute-start | bytes 1769480 | tf_op jit(solution)/shard_map/ppermute | solution.py:155
  23.4 13.2 %collective-permute-start.3 = (bf16[2,128,1024]{2,1,0:T(8,128)(2,1)}, bf16[2,128,1024]{2,1,0:T(8,128)(2,1)S(1)}, u32[]{:S(2)}, u32[]{:S(2)}) collective-permute-start(bf16[2,128,1024]{2,1,0:T(8,128)(2,1)} %collective-permute-done.1.refs_2_), channel_id=1, source_target_pairs={{0,8},{8,16},{16,24},{24,28},{28,20},{20,12},{12,4},{4,0},{1,9},{9... | collective-permute-start | bytes 1572872 | tf_op jit(solution)/shard_map/ppermute | solution.py:158
  24.0 12.8 %collective-permute-start.2 = (bf16[2,128,1024]{2,1,0:T(8,128)(2,1)}, bf16[2,128,1024]{2,1,0:T(8,128)(2,1)S(1)}, u32[]{:S(2)}, u32[]{:S(2)}) collective-permute-start(bf16[2,128,1024]{2,1,0:T(8,128)(2,1)} %collective-permute-done.refs_1_), channel_id=1, source_target_pairs={{8,0},{16,8},{24,16},{28,24},{20,28},{12,20},{4,12},{0,4},{9,1},{1... | collective-permute-start | bytes 1572872 | tf_op jit(solution)/shard_map/ppermute | solution.py:158
  43.1 25.4 %collective-permute-start.12 = (bf16[768,1024]{1,0:T(8,128)(2,1)}, bf16[768,1024]{1,0:T(8,128)(2,1)S(1)}, u32[]{:S(2)}, u32[]{:S(2)}) collective-permute-start(bf16[768,1024]{1,0:T(8,128)(2,1)} %collective-permute-done.10.refs_4_.refs_3_), channel_id=1, source_target_pairs={{1,0},{0,1},{3,2},{2,3},{5,4},{4,5},{7,6},{6,7},{9,8},{8,9},{11,10... | collective-permute-start | bytes 4718600 | tf_op jit(solution)/shard_map/ppermute | solution.py:155
  43.2 15.7 %collective-permute-start.11 = (bf16[288,1024]{1,0:T(8,128)(2,1)S(1)}, bf16[288,1024]{1,0:T(8,128)(2,1)S(1)}, u32[]{:S(2)}, u32[]{:S(2)}) collective-permute-start(bf16[288,1024]{1,0:T(8,128)(2,1)S(1)} %pad_maximum_fusion.1.refs_5_.refs_4_.refs_3_), channel_id=1, source_target_pairs={{2,0},{0,2},{3,1},{1,3},{6,4},{4,6},{7,5},{5,7},{10,8},{8,10},{11,... | collective-permute-start | bytes 1769480 | tf_op jit(solution)/shard_map/ppermute | solution.py:155
  44.0 14.9 %collective-permute-start.6 = (bf16[2,128,1024]{2,1,0:T(8,128)(2,1)S(1)}, bf16[2,128,1024]{2,1,0:T(8,128)(2,1)S(1)}, u32[]{:S(2)}, u32[]{:S(2)}) collective-permute-start(bf16[2,128,1024]{2,1,0:T(8,128)(2,1)S(1)} %collective-permute-done.2.refs_0_), channel_id=1, source_target_pairs={{8,0},{16,8},{24,16},{28,24},{20,28},{12,20},{4,12},{0,4},{9,1},{1... | collective-permute-start | bytes 1572872 | tf_op jit(solution)/shard_map/ppermute | solution.py:158
  45.5 13.8 %collective-permute-start.7 = (bf16[2,128,1024]{2,1,0:T(8,128)(2,1)S(1)}, bf16[2,128,1024]{2,1,0:T(8,128)(2,1)S(1)}, u32[]{:S(2)}, u32[]{:S(2)}) collective-permute-start(bf16[2,128,1024]{2,1,0:T(8,128)(2,1)S(1)} %collective-permute-done.3.refs_1_), channel_id=1, source_target_pairs={{0,8},{8,16},{16,24},{24,28},{28,20},{20,12},{12,4},{4,0},{1,9},{9... | collective-permute-start | bytes 1572872 | tf_op jit(solution)/shard_map/ppermute | solution.py:158
  58.9 9.6 %collective-permute-start.13 = (bf16[288,1024]{1,0:T(8,128)(2,1)S(1)}, bf16[288,1024]{1,0:T(8,128)(2,1)S(1)}, u32[]{:S(2)}, u32[]{:S(2)}) collective-permute-start(bf16[288,1024]{1,0:T(8,128)(2,1)S(1)} %collective-permute-done.11.refs_5_.refs_4_), channel_id=1, source_target_pairs={{1,0},{0,1},{3,2},{2,3},{5,4},{4,5},{7,6},{6,7},{9,8},{8,9},{11,10... | collective-permute-start | bytes 1769480 | tf_op jit(solution)/shard_map/ppermute | solution.py:155
  76.9 11.0 %collective-permute-start.14 = (bf16[64,1024]{1,0:T(8,128)(2,1)S(1)}, bf16[64,1024]{1,0:T(8,128)(2,1)S(1)}, u32[]{:S(2)}, u32[]{:S(2)}) collective-permute-start(bf16[64,1024]{1,0:T(8,128)(2,1)S(1)} %get-tuple-element.91), channel_id=1, source_target_pairs={{0,8},{8,16},{16,24},{24,28},{28,20},{20,12},{12,4},{4,0},{1,9},{9... | collective-permute-start | bytes 393224 | tf_op jit(solution)/shard_map/ppermute | solution.py:158
  79.0 11.1 %collective-permute-start.22 = (bf16[64,1024]{1,0:T(8,128)(2,1)S(1)}, bf16[64,1024]{1,0:T(8,128)(2,1)S(1)}, u32[]{:S(2)}, u32[]{:S(2)}) collective-permute-start(bf16[64,1024]{1,0:T(8,128)(2,1)S(1)} %get-tuple-element.89), channel_id=1, source_target_pairs={{0,8},{8,16},{16,24},{24,28},{28,20},{20,12},{12,4},{4,0},{1,9},{9... | collective-permute-start | bytes 393224 | tf_op jit(solution)/shard_map/ppermute | solution.py:158
  80.5 9.6 %collective-permute-start.26 = (bf16[64,1024]{1,0:T(8,128)(2,1)S(1)}, bf16[64,1024]{1,0:T(8,128)(2,1)S(1)}, u32[]{:S(2)}, u32[]{:S(2)}) collective-permute-start(bf16[64,1024]{1,0:T(8,128)(2,1)S(1)} %get-tuple-element.90), channel_id=1, source_target_pairs={{8,0},{16,8},{24,16},{28,24},{20,28},{12,20},{4,12},{0,4},{9,1},{1... | collective-permute-start | bytes 393224 | tf_op jit(solution)/shard_map/ppermute | solution.py:158
  88.0 11.2 %collective-permute-start.17 = (bf16[128,1024]{1,0:T(8,128)(2,1)S(1)}, bf16[128,1024]{1,0:T(8,128)(2,1)S(1)}, u32[]{:S(2)}, u32[]{:S(2)}) collective-permute-start(bf16[128,1024]{1,0:T(8,128)(2,1)S(1)} %pad_maximum_fusion.8), channel_id=1, source_target_pairs={{8,0},{16,8},{24,16},{28,24},{20,28},{12,20},{4,12},{0,4},{9,1},{1... | collective-permute-start | bytes 786440 | tf_op jit(solution)/shard_map/ppermute | solution.py:158
  90.3 20.3 %collective-permute-start.27 = (bf16[128,1024]{1,0:T(8,128)(2,1)S(1)}, bf16[128,1024]{1,0:T(8,128)(2,1)S(1)}, u32[]{:S(2)}, u32[]{:S(2)}) collective-permute-start(bf16[128,1024]{1,0:T(8,128)(2,1)S(1)} %pad_maximum_fusion.10), channel_id=1, source_target_pairs={{8,0},{16,8},{24,16},{28,24},{20,28},{12,20},{4,12},{0,4},{9,1},{1... | collective-permute-start | bytes 786440 | tf_op jit(solution)/shard_map/ppermute | solution.py:158
  91.9 18.6 %collective-permute-start.23 = (bf16[128,1024]{1,0:T(8,128)(2,1)S(1)}, bf16[128,1024]{1,0:T(8,128)(2,1)S(1)}, u32[]{:S(2)}, u32[]{:S(2)}) collective-permute-start(bf16[128,1024]{1,0:T(8,128)(2,1)S(1)} %pad_maximum_fusion.9), channel_id=1, source_target_pairs={{0,8},{8,16},{16,24},{24,28},{28,20},{20,12},{12,4},{4,0},{1,9},{9... | collective-permute-start | bytes 786440 | tf_op jit(solution)/shard_map/ppermute | solution.py:158
  100.1 15.6 %collective-permute-start.18 = (bf16[128,1024]{1,0:T(8,128)(2,1)}, bf16[128,1024]{1,0:T(8,128)(2,1)}, u32[]{:S(2)}, u32[]{:S(2)}) collective-permute-start(bf16[128,1024]{1,0:T(8,128)(2,1)} %get-tuple-element.79), channel_id=1, source_target_pairs={{0,8},{8,16},{16,24},{24,28},{28,20},{20,12},{12,4},{4,0},{1,9},{9... | collective-permute-start | bytes 786440 | tf_op jit(solution)/shard_map/ppermute | solution.py:158
  101.5 14.2 %collective-permute-start.20 = (bf16[128,1024]{1,0:T(8,128)(2,1)S(1)}, bf16[128,1024]{1,0:T(8,128)(2,1)}, u32[]{:S(2)}, u32[]{:S(2)}) collective-permute-start(bf16[128,1024]{1,0:T(8,128)(2,1)S(1)} %get-tuple-element.80), channel_id=1, source_target_pairs={{8,0},{16,8},{24,16},{28,24},{20,28},{12,20},{4,12},{0,4},{9,1},{1... | collective-permute-start | bytes 786440 | tf_op jit(solution)/shard_map/ppermute | solution.py:158
  117.7 19.0 %collective-permute-start.19 = (bf16[128,1024]{1,0:T(8,128)(2,1)}, bf16[128,1024]{1,0:T(8,128)(2,1)S(1)}, u32[]{:S(2)}, u32[]{:S(2)}) collective-permute-start(bf16[128,1024]{1,0:T(8,128)(2,1)} %get-tuple-element.73), channel_id=1, source_target_pairs={{0,8},{8,16},{16,24},{24,28},{28,20},{20,12},{12,4},{4,0},{1,9},{9... | collective-permute-start | bytes 786440 | tf_op jit(solution)/shard_map/ppermute | solution.py:158
  119.2 17.6 %collective-permute-start.21 = (bf16[128,1024]{1,0:T(8,128)(2,1)}, bf16[128,1024]{1,0:T(8,128)(2,1)}, u32[]{:S(2)}, u32[]{:S(2)}) collective-permute-start(bf16[128,1024]{1,0:T(8,128)(2,1)} %get-tuple-element.74), channel_id=1, source_target_pairs={{8,0},{16,8},{24,16},{28,24},{20,28},{12,20},{4,12},{0,4},{9,1},{1... | collective-permute-start | bytes 786440 | tf_op jit(solution)/shard_map/ppermute | solution.py:158
  124.9 11.2 %all-to-all-start.1 = ((f32[8,2,128]{2,1,0:T(2,128)}), f32[8,2,128]{2,1,0:T(2,128)S(1)}, u32[]{:S(2)}, u32[]{:S(2)}) async-start(f32[8,2,128]{2,1,0:T(2,128)} %copy.23), calls=%async_computation.1 | async-start | bytes 16384 | tf_op jit(solution)/shard_map/all_to_all | solution.py:262
  (16 other events, 134.6 us)

commit v3 on v2

v3 whole, which is shorter than its diff:
```python
import functools

import jax
import jax.numpy as jnp
from jax import lax
from jax.experimental import pallas as pl
from jax.experimental.pallas import tpu as pltpu
from jax.sharding import PartitionSpec as P

NT = (((1,), (1,)), ((), ()))
NN = (((1,), (0,)), ((), ()))


def dot(a, b, dims):
    return lax.dot_general(a, b, dims, preferred_element_type=jnp.float32)


def part_kernel(layout, arrays, blocks, tokens, lines, prior_row, is_last, *refs):
    has_prior = prior_row is not None
    expert_ref, block_refs, refs = refs[0], refs[1 : blocks + 1], refs[blocks + 1 :]
    weight_refs, refs = refs[:arrays], refs[arrays:]
    prior, refs = (refs[:3], refs[3:]) if has_prior else ((), refs)
    results, refs = (refs[:1], refs[1:]) if is_last else (refs[:3], refs[3:])
    token_buf, name_buf, gate_buf, mixed_buf, back_buf, grad_buf, token_sem, sum_sem = refs
    rows, width = mixed_buf.shape
    extra, held = name_buf.shape[1], expert_ref.shape[0]

    per_row = width // tokens
    line = lax.broadcasted_iota(jnp.int32, (extra, width), 0)
    spot = lax.broadcasted_iota(jnp.int32, (extra, width), 1) // tokens

    def token_copies(which):
        return [
            pltpu.make_async_copy(
                block_refs[b].at[pl.ds(which * tokens, tokens)],
                token_buf.at[which, pl.ds(b * tokens, tokens)],
                token_sem.at[which, b],
            )
            for b in range(blocks)
        ]

    name_copies = [
        pltpu.make_async_copy(block_refs[b].at[pl.ds(2 * tokens, extra)], name_buf.at[b], token_sem.at[2, b])
        for b in range(blocks)
    ]

    sums = (mixed_buf, back_buf, grad_buf)
    prior_copies = [pltpu.make_async_copy(prior[i].at[pl.ds(prior_row, rows)], sums[i], sum_sem.at[i]) for i in range(len(prior))]

    def start(copies):
        for copy in copies:
            copy.start()

    def wait(copies):
        for copy in copies:
            copy.wait()

    def spread(i, value):
        for b in range(blocks):
            at, of_block = b * (2 * tokens + extra), value[b * tokens : (b + 1) * tokens]
            if i < 2:
                results[0][at + i * tokens : at + (i + 1) * tokens, :] = of_block
                continue
            by_slot, out = of_block.T, jnp.zeros((extra, width), jnp.float32)
            for e in range(held):
                left, name = jnp.concatenate([by_slot[e : e + 1]] * per_row, axis=1), expert_ref[e]
                for third in range(3):
                    piece = left.astype(jnp.bfloat16).astype(jnp.float32)
                    mine = (spot == name % per_row) & (line == third * lines + name // per_row)
                    out = jnp.where(mine, piece, out)
                    left = left - piece
            results[0][at + 2 * tokens : at + 2 * tokens + extra, :] = out

    def hand_on(i, value):
        if has_prior:
            wait(prior_copies[i : i + 1])
            value = value + sums[i][...]
        if is_last:
            spread(i, value)
            return []
        sums[i][...] = value
        copy = pltpu.make_async_copy(sums[i], results[i], sum_sem.at[i])
        copy.start()
        return [copy]

    start(name_copies + token_copies(0) + token_copies(1) + prior_copies)
    slot = lax.broadcasted_iota(jnp.int32, (8, tokens), 0)
    wait(name_copies)
    for b in range(blocks):
        gates = jnp.zeros((8, tokens), jnp.float32)
        held_gates = name_buf[b].astype(jnp.float32)
        for e in range(held):
            name = expert_ref[e]
            mine = (spot == name % per_row) & (line < 3 * lines) & (line % lines == name // per_row)
            found = jnp.sum(jnp.where(mine, held_gates, 0.0), axis=0, keepdims=True)
            found = sum(found[:, i * tokens : (i + 1) * tokens] for i in range(per_row))
            gates = jnp.where(slot == e, found, gates)
        gate_buf[b * tokens : (b + 1) * tokens, 0:8] = gates.T
    column = lax.broadcasted_iota(jnp.int32, grad_buf.shape, 1)
    gate_grads = jnp.zeros(grad_buf.shape, jnp.float32)
    wait(token_copies(0) + token_copies(1))
    mixed = back = 0.0
    for e, units, places in layout:
        w_gate, w_up, w_down = [weight_refs[index][pl.ds(first, units)] for index, first in places]
        gate = gate_buf[:, e : e + 1]
        gate_val = dot(token_buf[0], w_gate, NT)
        up_val = dot(token_buf[0], w_up, NT)
        d_out = dot(token_buf[1], w_down, NT)
        sig = jax.nn.sigmoid(gate_val)
        silu = gate_val * sig
        act = silu * up_val
        d_act = gate * d_out
        d_gate = (d_act * up_val * (sig + silu * (1.0 - sig))).astype(jnp.bfloat16)
        d_up = (d_act * silu).astype(jnp.bfloat16)
        mixed = mixed + dot((gate * act).astype(jnp.bfloat16), w_down, NN)
        total = jnp.sum(act * d_out, axis=1, keepdims=True)
        gate_grads = gate_grads + jnp.where(column == e, total, 0.0)
        back = back + dot(d_gate, w_gate, NN) + dot(d_up, w_up, NN)
    leaving = hand_on(0, mixed)
    leaving += hand_on(2, gate_grads)
    leaving += hand_on(1, back)
    wait(leaving)


def experts_part(blocks, experts_here, lines, tokens, part, prior, prior_row, is_last):
    width = blocks[0].shape[1]
    rows = len(blocks) * tokens
    flat, layout = [], []
    for e, units, places in part:
        known = []
        for array, first in places:
            if not any(array is a for a in flat):
                flat.append(array)
            known.append(([array is a for a in flat].index(True), first))
        layout.append((e, units, known))
    hidden = sum(units for _, units, _ in part)
    vmem, hbm = pl.BlockSpec(memory_space=pltpu.VMEM), pl.BlockSpec(memory_space=pltpu.HBM)
    sums, out = [(rows, width), (rows, width), (rows, 128)], [(len(blocks) * blocks[0].shape[0], width)]
    return pl.pallas_call(
        functools.partial(part_kernel, layout, len(flat), len(blocks), tokens, lines, prior_row if prior else None, is_last),
        out_shape=tuple(jax.ShapeDtypeStruct(shape, jnp.float32) for shape in (out if is_last else sums)),
        in_specs=[pl.BlockSpec(memory_space=pltpu.SMEM)] + [hbm] * len(blocks) + [vmem] * len(flat) + [hbm] * len(prior),
        out_specs=(vmem,) if is_last else (hbm,) * 3,
        scratch_shapes=[
            pltpu.VMEM((2, rows, width), jnp.bfloat16),
            pltpu.VMEM((len(blocks), blocks[0].shape[0] - 2 * tokens, width), jnp.bfloat16),
            pltpu.VMEM((rows, 128), jnp.float32),
            *(pltpu.VMEM(shape, jnp.float32) for shape in sums),
            pltpu.SemaphoreType.DMA((3, len(blocks))),
            pltpu.SemaphoreType.DMA((3,)),
        ],
        compiler_params=pltpu.CompilerParams(vmem_limit_bytes=24 << 20),
        cost_estimate=pl.CostEstimate(
            flops=120 * rows * width * hidden,
            bytes_accessed=60 * hidden * width + 120 * rows * width,
            transcendentals=rows * hidden,
        ),
    )(experts_here, *blocks, *flat, *prior)


def gate_rows(dense, width):
    pieces, left = [], dense.reshape(-1, width)
    for _ in range(3):
        piece = lax.reduce_precision(left, 8, 7)
        pieces.append(piece)
        left = left - piece
    rows = jnp.concatenate(pieces).astype(jnp.bfloat16)
    return jnp.pad(rows, ((0, -rows.shape[0] % 16), (0, 0)))


def ring_order(n):
    return [0, 2, 4, 6, 7, 5, 3, 1] if n == 8 else list(range(n))


def after(a, *others):
    return lax.optimization_barrier((a, *others))[0]


def local(hidden_rows, out_grad, gates, routes, w_gate, w_up, w_down):
    tokens, width = hidden_rows.shape
    n, n_dp, n_seq = lax.axis_size("expert"), lax.axis_size("dp"), lax.axis_size("seq")
    here = w_gate.shape[0]
    held = n_seq * here
    experts = n * held
    order = ring_order(n)
    fw = [(order[i], order[(i + 1) % n]) for i in range(n)]
    bw = [(b, a) for a, b in fw]
    me, my_seq = lax.axis_index("expert"), lax.axis_index("seq")
    few = n <= 8
    reach, far, even, half = (n - 1) // 2, n // 2, n % 2 == 0, tokens // 2

    def shifted(a, axis, size, by):
        return lax.ppermute(a, axis, [((i + by) % size, i) for i in range(size)])

    def around(a, way):
        return lax.ppermute(a, "expert", way)

    names = jnp.arange(experts, dtype=jnp.int32)
    chosen = routes.T[None] == names[:, None, None]
    dense = jnp.sum(jnp.where(chosen, gates.T[None], 0.0), axis=1)

    units = w_down.shape[1]
    own = [[w[i] for w in (jnp.swapaxes(w_gate, 1, 2), jnp.swapaxes(w_up, 1, 2), w_down)] for i in range(here)]

    def listed(arrays, slot):
        return (slot, units, tuple((w, 0) for w in arrays))

    gate_up = [jnp.concatenate(w[:2]) for w in own]

    def packed(both, down, slot):
        return (slot, units, ((both, 0), (both, units), (down, 0)))

    first = [listed(w, i) for i, w in enumerate(own)]
    groups = [[0, 1, -1]] + [[s, -s] for s in range(2, reach + 1)] + ([[far]] if even else [])

    slots = [[((c + e // here) % n_seq) * here + e % here for e in range(held)] for c in range(n_seq)]
    slot_of = jnp.sum(
        jnp.where((my_seq == jnp.arange(n_seq, dtype=jnp.int32))[:, None], jnp.array(slots, jnp.int32), 0), axis=0
    )
    experts_here = me * held + slot_of
    lines = experts * tokens // width
    done = [() for _ in groups]
    last = []

    def work(g, part, is_last, *wait_for, skip=0, take=None):
        named = after(experts_here, *last, *wait_for)
        some = groups[g][skip:take]
        got = experts_part(
            [arrived[d] for d in some], named, lines, tokens, part, done[g], skip * tokens, is_last
        )
        last[:] = [got[-1] if not is_last else got[0][:1]]
        return got

    def top_half(a):
        return jnp.concatenate([a[:half], a[tokens : tokens + half], a[2 * tokens :]])

    def low_half(a):
        return jnp.concatenate([a[half:tokens], a[tokens + half : 2 * tokens]])

    arrived = {0: jnp.concatenate([hidden_rows, out_grad, gate_rows(dense, width)])}
    arrived[-1], arrived[1] = around(arrived[0], fw), around(arrived[0], bw)
    for r in range(1, n_seq):
        for i in range(here):
            down = after(own[i][2], arrived[1][:1]) if few else own[i][2]
            first.append(packed(shifted(gate_up[i], "seq", n_seq, r), shifted(down, "seq", n_seq, r), r * here + i))
    for s in range(2, reach + 1):
        ahead, behind = arrived[1 - s], arrived[s - 1]
        if few and s > 2:
            done[s - 3] = work(s - 3, first, False)
            ahead, behind = after(ahead, *last), after(behind, *last)
        arrived[-s], arrived[s] = around(ahead, fw), around(behind, bw)
    if few and reach > 1:
        done[reach - 2] = work(reach - 2, first, False)
    end = []
    if even:
        ahead, behind = after(arrived[1 - far], *last), after(arrived[far - 1], *last)
        top, low = around(top_half(ahead), fw), around(low_half(behind), bw)
        end = [top[:1], low[:1]]
        arrived[far] = jnp.concatenate([top[:half], low[:half], top[half:tokens], low[half:], top[tokens:]])

    rest = []
    for r in range(1, n_dp):
        for i in range(here):
            down, both = shifted(own[i][2], "dp", n_dp, r), shifted(gate_up[i], "dp", n_dp, r)
            rest.append(packed(both, down, i))
            down, both = after(down, *last, arrived[reach][:1]), after(both, *last, *end)
            for q in range(1, n_seq):
                rest.append(packed(shifted(both, "seq", n_seq, q), shifted(down, "seq", n_seq, q), q * here + i))

    if few:
        done[reach - 1] = work(reach - 1, first, False)

    def finish(g, *wait_for, skip=0, take=None):
        (sums,) = work(g, rest if done[g] else first + rest, True, *wait_for, skip=skip, take=take)
        size = sums.shape[0] // len(groups[g][skip:take])
        return [sums[i * size : (i + 1) * size] for i in range(len(groups[g][skip:take]))]

    def rounded(a):
        return a.astype(jnp.bfloat16)

    def plus(part, travelled):
        return part + travelled.astype(jnp.float32)

    def plus_top(a, t):
        return jnp.concatenate(
            [
                plus(a[:half], t[:half]),
                a[half:tokens],
                plus(a[tokens : tokens + half], t[half:tokens]),
                a[tokens + half : 2 * tokens],
                plus(a[2 * tokens :], t[tokens:]),
            ]
        )

    def plus_low(a, t):
        return jnp.concatenate(
            [
                a[:half],
                plus(a[half:tokens], t[:half]),
                a[tokens : tokens + half],
                plus(a[tokens + half : 2 * tokens], t[half:]),
                a[2 * tokens :],
            ]
        )

    came = None
    if even:
        (sums,) = finish(len(groups) - 1)
        came = around(rounded(top_half(sums)), fw), around(rounded(low_half(sums)), bw)
    before = []
    for s in range(reach, 0, -1):
        sums_fw, sums_bw = finish(s - 1, *before, skip=int(s == 1))
        if came is None:
            out = rounded(sums_fw), rounded(sums_bw)
        elif even and s == reach:
            out = rounded(plus_top(sums_fw, came[0])), rounded(plus_low(sums_bw, came[1]))
        else:
            out = rounded(plus(sums_fw, came[0])), rounded(plus(sums_bw, came[1]))
        before = [] if came is None else [a[:1] for a in came]
        came = around(out[0], fw), around(out[1], bw)
    (own_sums,) = finish(0, *[a[:1] for a in out], take=1)
    total = plus(plus(own_sums, came[0]), came[1])
    mixed, grad_rows = rounded(total[:tokens]), rounded(total[tokens : 2 * tokens])

    thirds = total[2 * tokens : 2 * tokens + 3 * lines].reshape(3, lines, width)
    by_expert = (thirds[0] + thirds[1] + thirds[2]).reshape(experts, tokens)
    grad_gates = jnp.sum(jnp.where(chosen, by_expert[:, None, :], 0.0), axis=0).T
    return (mixed, grad_rows, grad_gates)


def solution(mesh):
    tokens = P(("groups", "expert", "dp", "seq"), None)
    in_specs = (tokens,) * 4 + (P(("expert", "seq"), None, "dp"),) * 2 + (P(("expert", "seq"), "dp", None),)
    return jax.shard_map(local, mesh=mesh, in_specs=in_specs, out_specs=(tokens,) * 3, check_vma=False)
```

time: 141 us -> 125 us (0.89)
  starting transfers between devices: 39.6 us -> 22.7 us
  waiting for transfers between devices: 27.6 us -> 43.9 us
  local copies, waits for them, and re-layouts: 8.97 us -> 1.05 us
  other arithmetic: 12.8 us -> 5.99 us
    ppermute x24 -> x16, waiting for transfers between devices: 6.31 us -> 32.4 us  [around(): return lax.ppermute(a, 'expert', way)]
    all_to_all x2 -> x0, starting transfers between devices: 10.3 us -> none  [the longest x1 5.83 us: local(): lax.all_to_all(dense.reshape(n, held, tokens), 'expert', split_axis=0, co...]
    all_to_all x2 -> x0, waiting for transfers between devices: 8.4 us -> none  [the longest x1 4.65 us: local(): lax.all_to_all(to_chip, 'expert', split_axis=0, concat_axis=0, tiled=True)]
    ppermute x24 -> x16, starting transfers between devices: 26.1 us -> 18.1 us  [around(): return lax.ppermute(a, 'expert', way)]
    convert_element_type x6 -> x2, other arithmetic: 8.33 us -> 0.79 us  [rounded(): return a.astype(jnp.bfloat16)]
    squeeze x4 -> x0, local copies, waits for them, and re-layouts: 3.14 us -> none  [local(): w[i, low:high]]
    concatenate x8, other arithmetic: 1.1 us -> 3.82 us  [the longest x1 2.64 us: local(): gate_up = [jnp.concatenate(w[:2]) for w in own]]
    slice x9 -> x6, local copies, waits for them, and re-layouts: 2.88 us -> 0.91 us  [the longest x1 0.82 us: local(): total[tokens:2 * tokens]]
  transfers between devices with their start and end apart: 32 -> 22, of which waited for: 8 -> 10; matrix products, arithmetic and copies ran while one was open for 13% -> 1% of each run, Pallas kernels for 30% -> 34%
where the time goes in v3:
time: 125 us; the launch traced here: 124 us
  Pallas kernels  49.4 us (40%)
  waiting for transfers between devices  43.9 us (35%)
  starting transfers between devices  22.7 us (18%)
  other arithmetic  5.99 us (5%)
    pallas_call x8, Pallas kernels, experts_part(): pl.pallas_call(functools.partial(part_kernel, layout, len(flat), len(bloc...  49.4 us
    ppermute x16, waiting for transfers between devices, around(): return lax.ppermute(a, 'expert', way)  32.4 us
    ppermute x16, starting transfers between devices, around(): return lax.ppermute(a, 'expert', way)  18.1 us
    ppermute x6, waiting for transfers between devices, shifted(): return lax.ppermute(a, axis, [((i + by) % size, i) for i in range(size)])  11.6 us
    ppermute x6, starting transfers between devices, shifted(): return lax.ppermute(a, axis, [((i + by) % size, i) for i in range(size)])  4.67 us
    concatenate x1, other arithmetic, local(): gate_up = [jnp.concatenate(w[:2]) for w in own]  2.64 us
  transfers between devices with their start and end apart: 22, of which 10 were waited for; matrix products, arithmetic and copies ran while one was open for 1% of the time, Pallas kernels for 34%

profile of v3, /device:TPU:0, one launch (start us, length us, event | category | flops | bytes accessed | tf_op | source)
XLA Modules:
  0.0 124.1 jit_solution(3203156712306821162)
XLA Ops:
  0.7 2.6 %pad_maximum_fusion = bf16[704,1024]{1,0:T(8,128)(2,1)} fusion(bf16[352,1024]{1,0:T(8,128)(2,1)} %bitcast.10, bf16[352,1024]{1,0:T(8,128)(2,1)} %bitcast.15), kind=kLoop, calls=%fused_computation | loop fusion | flops 2883584 | bytes 2883584 | tf_op jit(solution)/shard_map/concatenate | solution.py:208
  5.0 3.1 %collective-permute-start.3 = (bf16[272,1024]{1,0:T(8,128)(2,1)S(1)}, bf16[272,1024]{1,0:T(8,128)(2,1)}, u32[]{:S(2)}, u32[]{:S(2)}) collective-permute-start(bf16[272,1024]{1,0:T(8,128)(2,1)S(1)} %pad_maximum_fusion.1.refs_1_), channel_id=1, source_target_pairs={{0,8},{8,16},{16,24},{24,28},{28,20},{20,12},{12,4},{4,0},{1,9},{9... | collective-permute-start | bytes 1671176 | tf_op jit(solution)/shard_map/ppermute | solution.py:196
  8.1 1.9 %collective-permute-start.1 = (bf16[352,1024]{1,0:T(8,128)(2,1)}, bf16[352,1024]{1,0:T(8,128)(2,1)}, u32[]{:S(2)}, u32[]{:S(2)}) collective-permute-start(bf16[352,1024]{1,0:T(8,128)(2,1)} %bitcast.6.refs_6_.refs_5_.refs_4_), channel_id=1, source_target_pairs={{2,0},{0,2},{3,1},{1,3},{6,4},{4,6},{7,5},{5,7},{10,8},{8,10},{11,... | collective-permute-start | bytes 2162696 | tf_op jit(solution)/shard_map/ppermute | solution.py:193
  10.1 10.9 %collective-permute-done.3.refs_3_.refs_2_ = bf16[272,1024]{1,0:T(8,128)(2,1)} collective-permute-done((bf16[272,1024]{1,0:T(8,128)(2,1)S(1)}, bf16[272,1024]{1,0:T(8,128)(2,1)}, u32[]{:S(2)}, u32[]{:S(2)}) %collective-permute-start.3) | collective-permute-done | bytes 557088 | tf_op jit(solution)/shard_map/ppermute | solution.py:196
  21.0 1.7 %collective-permute-start = (bf16[704,1024]{1,0:T(8,128)(2,1)}, bf16[704,1024]{1,0:T(8,128)(2,1)S(1)}, u32[]{:S(2)}, u32[]{:S(2)}) collective-permute-start(bf16[704,1024]{1,0:T(8,128)(2,1)} %pad_maximum_fusion), channel_id=1, source_target_pairs={{2,0},{0,2},{3,1},{1,3},{6,4},{4,6},{7,5},{5,7},{10,8},{8,10},{11,... | collective-permute-start | bytes 4325384 | tf_op jit(solution)/shard_map/ppermute | solution.py:193
  24.7 8.6 %shard_map.103 = (f32[384,1024]{1,0:T(8,128)S(1)}, f32[384,1024]{1,0:T(8,128)S(1)}, f32[384,128]{1,0:T(8,128)S(1)}) custom-call(s32[2]{0:T(128)S(1)} %broadcast_add_fusion.refs_0_, bf16[272,1024]{1,0:T(8,128)(2,1)S(1)} %pad_maximum_fusion.1.refs_1_, bf16[272,1024]{1,0:T(8,128)(2,1)} %collective-permute-done.2.refs_2_.refs_1_, ...), custom_call_target="tpu_custom_call" | custom-call | flops 33218887680 | bytes 90439680 | tf_op jit(solution)/shard_map/pallas_call | solution.py:139
  33.3 3.0 %collective-permute-done.7.refs_2_ = bf16[272,1024]{1,0:T(8,128)(2,1)S(1)} collective-permute-done((bf16[272,1024]{1,0:T(8,128)(2,1)}, bf16[272,1024]{1,0:T(8,128)(2,1)S(1)}, u32[]{:S(2)}, u32[]{:S(2)}) %collective-permute-start.7) | collective-permute-done | bytes 557088 | tf_op jit(solution)/shard_map/ppermute | solution.py:196
  39.7 5.7 %shard_map.104 = (f32[256,1024]{1,0:T(8,128)S(1)}, f32[256,1024]{1,0:T(8,128)S(1)}, f32[256,128]{1,0:T(8,128)S(1)}) custom-call(s32[2]{0:T(128)S(1)} %broadcast_add_fusion.refs_0_, bf16[272,1024]{1,0:T(8,128)(2,1)S(1)} %collective-permute-done.6.refs_1_, bf16[272,1024]{1,0:T(8,128)(2,1)S(1)} %collective-permute-done.7.refs_2_, ...), custom_call_target="tpu_custom_call" | custom-call | flops 22145925120 | bytes 74711040 | tf_op jit(solution)/shard_map/pallas_call | solution.py:139
  45.5 11.5 %collective-permute-done.refs_2_.refs_3_.refs_7_ = bf16[704,1024]{1,0:T(8,128)(2,1)S(1)} collective-permute-done((bf16[704,1024]{1,0:T(8,128)(2,1)}, bf16[704,1024]{1,0:T(8,128)(2,1)S(1)}, u32[]{:S(2)}, u32[]{:S(2)}) %collective-permute-start) | collective-permute-done | bytes 1441824 | tf_op jit(solution)/shard_map/ppermute | solution.py:193
  57.6 1.7 %collective-permute-start.13 = (bf16[128,1024]{1,0:T(8,128)(2,1)S(1)}, bf16[128,1024]{1,0:T(8,128)(2,1)S(1)}, u32[]{:S(2)}, u32[]{:S(2)}) collective-permute-start(bf16[128,1024]{1,0:T(8,128)(2,1)S(1)} %pad_maximum_fusion.4), channel_id=1, source_target_pairs={{8,0},{16,8},{24,16},{28,24},{20,28},{12,20},{4,12},{0,4},{9,1},{1... | collective-permute-start | bytes 786440 | tf_op jit(solution)/shard_map/ppermute | solution.py:196
  59.9 5.7 %shard_map.108 = (f32[256,1024]{1,0:T(8,128)S(1)}, f32[256,1024]{1,0:T(8,128)S(1)}, f32[256,128]{1,0:T(8,128)S(1)}) custom-call(s32[2]{0:T(128)S(1)} %broadcast_add_fusion.refs_0_, bf16[272,1024]{1,0:T(8,128)(2,1)S(1)} %collective-permute-done.10.refs_1_, bf16[272,1024]{1,0:T(8,128)(2,1)S(1)} %collective-permute-done.11.refs_2_, ...), custom_call_target="tpu_custom_call" | custom-call | flops 22145925120 | bytes 74711040 | tf_op jit(solution)/shard_map/pallas_call | solution.py:139
  65.7 2.5 %collective-permute-done.12 = bf16[144,1024]{1,0:T(8,128)(2,1)S(1)} collective-permute-done((bf16[144,1024]{1,0:T(8,128)(2,1)S(1)}, bf16[144,1024]{1,0:T(8,128)(2,1)S(1)}, u32[]{:S(2)}, u32[]{:S(2)}) %collective-permute-start.12) | collective-permute-done | bytes 294944 | tf_op jit(solution)/shard_map/ppermute | solution.py:196
  68.3 6.8 %shard_map.110 = f32[272,1024]{1,0:T(8,128)S(1)} custom-call(s32[2]{0:T(128)S(1)} %broadcast_add_fusion.refs_0_, bf16[272,1024]{1,0:T(8,128)(2,1)S(1)} %slice_dynamic-update-slice_fusion.9.refs_1_, bf16[352,1024]{1,0:T(8,128)(2,1)S(1)} %bitcast.19, bf16[352,1024]{1,0:T(8,128)(2,1)S(1)} %bitcast.14, bf16[352,1024]{1,0:T(8,128)(2,1)} %bitcast.6.refs_6_.refs_5_.refs_4_, ...), custom_call_target="tpu_custom_call" | custom-call | flops 22145925120 | bytes 102236160 | tf_op jit(solution)/shard_map/pallas_call | solution.py:139
  75.3 1.6 %collective-permute-start.18 = (bf16[128,1024]{1,0:T(8,128)(2,1)S(1)}, bf16[128,1024]{1,0:T(8,128)(2,1)S(1)}, u32[]{:S(2)}, u32[]{:S(2)}) collective-permute-start(bf16[128,1024]{1,0:T(8,128)(2,1)S(1)} %pad_maximum_fusion.5), channel_id=1, source_target_pairs={{8,0},{16,8},{24,16},{28,24},{20,28},{12,20},{4,12},{0,4},{9,1},{1... | collective-permute-start | bytes 786440 | tf_op jit(solution)/shard_map/ppermute | solution.py:196
  77.5 5.8 %shard_map.109 = f32[544,1024]{1,0:T(8,128)S(1)} custom-call(s32[2]{0:T(128)S(1)} %broadcast_add_fusion.refs_0_, bf16[272,1024]{1,0:T(8,128)(2,1)S(1)} %collective-permute-done.10.refs_1_, bf16[272,1024]{1,0:T(8,128)(2,1)S(1)} %collective-permute-done.11.refs_2_, bf16[704,1024]{1,0:T(8,128)(2,1)S(1)} %collective-permute-done.refs_2_.refs_3_.refs_7_, ...), custom_call_target="tpu_custom_call" | custom-call | flops 22145925120 | bytes 74711040 | tf_op jit(solution)/shard_map/pallas_call | solution.py:139
  84.7 1.6 %collective-permute-start.19 = (bf16[272,1024]{1,0:T(8,128)(2,1)S(1)}, bf16[272,1024]{1,0:T(8,128)(2,1)S(1)}, u32[]{:S(2)}, u32[]{:S(2)}) collective-permute-start(bf16[272,1024]{1,0:T(8,128)(2,1)S(1)} %slice_dynamic-update-slice_fusion.8), channel_id=1, source_target_pairs={{8,0},{16,8},{24,16},{28,24},{20,28},{12,20},{4,12},{0,4},{9,1},{1... | collective-permute-start | bytes 1671176 | tf_op jit(solution)/shard_map/ppermute | solution.py:196
  87.1 5.8 %shard_map.107 = f32[544,1024]{1,0:T(8,128)S(1)} custom-call(s32[2]{0:T(128)S(1)} %broadcast_add_fusion.refs_0_, bf16[272,1024]{1,0:T(8,128)(2,1)S(1)} %collective-permute-done.6.refs_1_, bf16[272,1024]{1,0:T(8,128)(2,1)S(1)} %collective-permute-done.7.refs_2_, bf16[704,1024]{1,0:T(8,128)(2,1)S(1)} %collective-permute-done.refs_2_.refs_3_.refs_7_, ...), custom_call_target="tpu_custom_call" | custom-call | flops 22145925120 | bytes 74711040 | tf_op jit(solution)/shard_map/pallas_call | solution.py:139
  92.9 4.1 %collective-permute-done.19 = bf16[272,1024]{1,0:T(8,128)(2,1)S(1)} collective-permute-done((bf16[272,1024]{1,0:T(8,128)(2,1)S(1)}, bf16[272,1024]{1,0:T(8,128)(2,1)S(1)}, u32[]{:S(2)}, u32[]{:S(2)}) %collective-permute-start.19) | collective-permute-done | bytes 557088 | tf_op jit(solution)/shard_map/ppermute | solution.py:196
  96.9 2.0 %collective-permute-done.15 = bf16[272,1024]{1,0:T(8,128)(2,1)S(1)} collective-permute-done((bf16[272,1024]{1,0:T(8,128)(2,1)S(1)}, bf16[272,1024]{1,0:T(8,128)(2,1)S(1)}, u32[]{:S(2)}, u32[]{:S(2)}) %collective-permute-start.15) | collective-permute-done | bytes 557088 | tf_op jit(solution)/shard_map/ppermute | solution.py:196
  99.9 1.6 %collective-permute-start.20 = (bf16[272,1024]{1,0:T(8,128)(2,1)S(1)}, bf16[272,1024]{1,0:T(8,128)(2,1)S(1)}, u32[]{:S(2)}, u32[]{:S(2)}) collective-permute-start(bf16[272,1024]{1,0:T(8,128)(2,1)S(1)} %get-tuple-element.44), channel_id=1, source_target_pairs={{8,0},{16,8},{24,16},{28,24},{20,28},{12,20},{4,12},{0,4},{9,1},{1... | collective-permute-start | bytes 1671176 | tf_op jit(solution)/shard_map/ppermute | solution.py:196
  101.4 6.4 %shard_map.106 = f32[544,1024]{1,0:T(8,128)S(1)} custom-call(s32[2]{0:T(128)S(1)} %broadcast_add_fusion.refs_0_, bf16[272,1024]{1,0:T(8,128)(2,1)} %collective-permute-done.2.refs_2_.refs_1_, bf16[272,1024]{1,0:T(8,128)(2,1)} %collective-permute-done.3.refs_3_.refs_2_, bf16[704,1024]{1,0:T(8,128)(2,1)S(1)} %collective-permute-done.refs_2_.refs_3_.refs_7_, ...), custom_call_target="tpu_custom_call" | custom-call | flops 22145925120 | bytes 74711040 | tf_op jit(solution)/shard_map/pallas_call | solution.py:139
  107.8 3.9 %collective-permute-done.16 = bf16[272,1024]{1,0:T(8,128)(2,1)S(1)} collective-permute-done((bf16[272,1024]{1,0:T(8,128)(2,1)S(1)}, bf16[272,1024]{1,0:T(8,128)(2,1)S(1)}, u32[]{:S(2)}, u32[]{:S(2)}) %collective-permute-start.16) | collective-permute-done | bytes 557088 | tf_op jit(solution)/shard_map/ppermute | solution.py:196
  114.2 4.6 %shard_map.105 = f32[272,1024]{1,0:T(8,128)S(1)} custom-call(s32[2]{0:T(128)S(1)} %broadcast_add_fusion.refs_0_, bf16[272,1024]{1,0:T(8,128)(2,1)S(1)} %pad_maximum_fusion.1.refs_1_, bf16[704,1024]{1,0:T(8,128)(2,1)S(1)} %collective-permute-done.refs_2_.refs_3_.refs_7_, bf16[352,1024]{1,0:T(8,128)(2,1)} %collective-permute-done.1.refs_3_.refs_4_.refs_8_, ...), custom_call_target="tpu_custom_call" | custom-call | flops 11072962560 | bytes 58982400 | tf_op jit(solution)/shard_map/pallas_call | solution.py:139
  118.8 3.6 %collective-permute-done.17 = bf16[272,1024]{1,0:T(8,128)(2,1)S(1)} collective-permute-done((bf16[272,1024]{1,0:T(8,128)(2,1)S(1)}, bf16[272,1024]{1,0:T(8,128)(2,1)S(1)}, u32[]{:S(2)}, u32[]{:S(2)}) %collective-permute-start.17) | collective-permute-done | bytes 557088 | tf_op jit(solution)/shard_map/ppermute | solution.py:196
  (79 shorter events, 16.2 us)
Async XLA Ops:
  0.7 24.1 %copy-start.1 = (bf16[1,1024,352]{1,2,0:T(8,128)(2,1)S(1)}, bf16[1,1024,352]{1,2,0:T(8,128)(2,1)}, u32[]{:S(2)}) copy-start(bf16[1,1024,352]{1,2,0:T(8,128)(2,1)} %param.12) | copy-start | bytes 2162692
  3.3 21.4 %copy-start = (bf16[1,1024,352]{1,2,0:T(8,128)(2,1)S(1)}, bf16[1,1024,352]{1,2,0:T(8,128)(2,1)}, u32[]{:S(2)}) copy-start(bf16[1,1024,352]{1,2,0:T(8,128)(2,1)} %param.13) | copy-start | bytes 2162692
  3.3 21.4 %collective-permute-start.4 = (bf16[704,1024]{1,0:T(8,128)(2,1)}, bf16[704,1024]{1,0:T(8,128)(2,1)S(1)}, u32[]{:S(2)}, u32[]{:S(2)}) collective-permute-start(bf16[704,1024]{1,0:T(8,128)(2,1)} %pad_maximum_fusion), channel_id=1, source_target_pairs={{1,0},{0,1},{3,2},{2,3},{5,4},{4,5},{7,6},{6,7},{9,8},{8,9},{11,10... | collective-permute-start | bytes 4325384 | tf_op jit(solution)/shard_map/ppermute | solution.py:193
  3.8 20.5 %collective-permute-start.5 = (bf16[352,1024]{1,0:T(8,128)(2,1)}, bf16[352,1024]{1,0:T(8,128)(2,1)}, u32[]{:S(2)}, u32[]{:S(2)}) collective-permute-start(bf16[352,1024]{1,0:T(8,128)(2,1)} %bitcast.6.refs_6_.refs_5_.refs_4_), channel_id=1, source_target_pairs={{1,0},{0,1},{3,2},{2,3},{5,4},{4,5},{7,6},{6,7},{9,8},{8,9},{11,10... | collective-permute-start | bytes 2162696 | tf_op jit(solution)/shard_map/ppermute | solution.py:193
  5.0 16.0 %collective-permute-start.3 = (bf16[272,1024]{1,0:T(8,128)(2,1)S(1)}, bf16[272,1024]{1,0:T(8,128)(2,1)}, u32[]{:S(2)}, u32[]{:S(2)}) collective-permute-start(bf16[272,1024]{1,0:T(8,128)(2,1)S(1)} %pad_maximum_fusion.1.refs_1_), channel_id=1, source_target_pairs={{0,8},{8,16},{16,24},{24,28},{28,20},{20,12},{12,4},{4,0},{1,9},{9... | collective-permute-start | bytes 1671176 | tf_op jit(solution)/shard_map/ppermute | solution.py:196
  8.0 14.6 %collective-permute-start.2 = (bf16[272,1024]{1,0:T(8,128)(2,1)S(1)}, bf16[272,1024]{1,0:T(8,128)(2,1)}, u32[]{:S(2)}, u32[]{:S(2)}) collective-permute-start(bf16[272,1024]{1,0:T(8,128)(2,1)S(1)} %pad_maximum_fusion.1.refs_1_), channel_id=1, source_target_pairs={{8,0},{16,8},{24,16},{28,24},{20,28},{12,20},{4,12},{0,4},{9,1},{1... | collective-permute-start | bytes 1671176 | tf_op jit(solution)/shard_map/ppermute | solution.py:196
  8.1 37.4 %collective-permute-start.1 = (bf16[352,1024]{1,0:T(8,128)(2,1)}, bf16[352,1024]{1,0:T(8,128)(2,1)}, u32[]{:S(2)}, u32[]{:S(2)}) collective-permute-start(bf16[352,1024]{1,0:T(8,128)(2,1)} %bitcast.6.refs_6_.refs_5_.refs_4_), channel_id=1, source_target_pairs={{2,0},{0,2},{3,1},{1,3},{6,4},{4,6},{7,5},{5,7},{10,8},{8,10},{11,... | collective-permute-start | bytes 2162696 | tf_op jit(solution)/shard_map/ppermute | solution.py:193
  21.0 36.0 %collective-permute-start = (bf16[704,1024]{1,0:T(8,128)(2,1)}, bf16[704,1024]{1,0:T(8,128)(2,1)S(1)}, u32[]{:S(2)}, u32[]{:S(2)}) collective-permute-start(bf16[704,1024]{1,0:T(8,128)(2,1)} %pad_maximum_fusion), channel_id=1, source_target_pairs={{2,0},{0,2},{3,1},{1,3},{6,4},{4,6},{7,5},{5,7},{10,8},{8,10},{11,... | collective-permute-start | bytes 4325384 | tf_op jit(solution)/shard_map/ppermute | solution.py:193
  22.7 13.7 %collective-permute-start.7 = (bf16[272,1024]{1,0:T(8,128)(2,1)}, bf16[272,1024]{1,0:T(8,128)(2,1)S(1)}, u32[]{:S(2)}, u32[]{:S(2)}) collective-permute-start(bf16[272,1024]{1,0:T(8,128)(2,1)} %collective-permute-done.3.refs_3_.refs_2_), channel_id=1, source_target_pairs={{0,8},{8,16},{16,24},{24,28},{28,20},{20,12},{12,4},{4,0},{1,9},{9... | collective-permute-start | bytes 1671176 | tf_op jit(solution)/shard_map/ppermute | solution.py:196
  24.3 13.4 %collective-permute-start.6 = (bf16[272,1024]{1,0:T(8,128)(2,1)}, bf16[272,1024]{1,0:T(8,128)(2,1)S(1)}, u32[]{:S(2)}, u32[]{:S(2)}) collective-permute-start(bf16[272,1024]{1,0:T(8,128)(2,1)} %collective-permute-done.2.refs_2_.refs_1_), channel_id=1, source_target_pairs={{8,0},{16,8},{24,16},{28,24},{20,28},{12,20},{4,12},{0,4},{9,1},{1... | collective-permute-start | bytes 1671176 | tf_op jit(solution)/shard_map/ppermute | solution.py:196
  37.7 19.9 %collective-permute-start.10 = (bf16[272,1024]{1,0:T(8,128)(2,1)S(1)}, bf16[272,1024]{1,0:T(8,128)(2,1)S(1)}, u32[]{:S(2)}, u32[]{:S(2)}) collective-permute-start(bf16[272,1024]{1,0:T(8,128)(2,1)S(1)} %collective-permute-done.6.refs_1_), channel_id=1, source_target_pairs={{8,0},{16,8},{24,16},{28,24},{20,28},{12,20},{4,12},{0,4},{9,1},{1... | collective-permute-start | bytes 1671176 | tf_op jit(solution)/shard_map/ppermute | solution.py:196
  38.1 19.4 %collective-permute-start.11 = (bf16[272,1024]{1,0:T(8,128)(2,1)S(1)}, bf16[272,1024]{1,0:T(8,128)(2,1)S(1)}, u32[]{:S(2)}, u32[]{:S(2)}) collective-permute-start(bf16[272,1024]{1,0:T(8,128)(2,1)S(1)} %collective-permute-done.7.refs_2_), channel_id=1, source_target_pairs={{0,8},{8,16},{16,24},{24,28},{28,20},{20,12},{12,4},{4,0},{1,9},{9... | collective-permute-start | bytes 1671176 | tf_op jit(solution)/shard_map/ppermute | solution.py:196
  57.0 11.3 %collective-permute-start.9 = (bf16[352,1024]{1,0:T(8,128)(2,1)}, bf16[352,1024]{1,0:T(8,128)(2,1)S(1)}, u32[]{:S(2)}, u32[]{:S(2)}) collective-permute-start(bf16[352,1024]{1,0:T(8,128)(2,1)} %collective-permute-done.1.refs_3_.refs_4_.refs_8_), channel_id=1, source_target_pairs={{1,0},{0,1},{3,2},{2,3},{5,4},{4,5},{7,6},{6,7},{9,8},{8,9},{11,10... | collective-permute-start | bytes 2162696 | tf_op jit(solution)/shard_map/ppermute | solution.py:193
  57.0 11.3 %collective-permute-start.8 = (bf16[704,1024]{1,0:T(8,128)(2,1)S(1)}, bf16[704,1024]{1,0:T(8,128)(2,1)S(1)}, u32[]{:S(2)}, u32[]{:S(2)}) collective-permute-start(bf16[704,1024]{1,0:T(8,128)(2,1)S(1)} %collective-permute-done.refs_2_.refs_3_.refs_7_), channel_id=1, source_target_pairs={{1,0},{0,1},{3,2},{2,3},{5,4},{4,5},{7,6},{6,7},{9,8},{8,9},{11,10... | collective-permute-start | bytes 4325384 | tf_op jit(solution)/shard_map/ppermute | solution.py:193
  57.6 10.6 %collective-permute-start.13 = (bf16[128,1024]{1,0:T(8,128)(2,1)S(1)}, bf16[128,1024]{1,0:T(8,128)(2,1)S(1)}, u32[]{:S(2)}, u32[]{:S(2)}) collective-permute-start(bf16[128,1024]{1,0:T(8,128)(2,1)S(1)} %pad_maximum_fusion.4), channel_id=1, source_target_pairs={{8,0},{16,8},{24,16},{28,24},{20,28},{12,20},{4,12},{0,4},{9,1},{1... | collective-permute-start | bytes 786440 | tf_op jit(solution)/shard_map/ppermute | solution.py:196
  59.4 8.9 %collective-permute-start.12 = (bf16[144,1024]{1,0:T(8,128)(2,1)S(1)}, bf16[144,1024]{1,0:T(8,128)(2,1)S(1)}, u32[]{:S(2)}, u32[]{:S(2)}) collective-permute-start(bf16[144,1024]{1,0:T(8,128)(2,1)S(1)} %pad_maximum_fusion.2), channel_id=1, source_target_pairs={{0,8},{8,16},{16,24},{24,28},{28,20},{20,12},{12,4},{4,0},{1,9},{9... | collective-permute-start | bytes 884744 | tf_op jit(solution)/shard_map/ppermute | solution.py:196
  75.3 8.2 %collective-permute-start.18 = (bf16[128,1024]{1,0:T(8,128)(2,1)S(1)}, bf16[128,1024]{1,0:T(8,128)(2,1)S(1)}, u32[]{:S(2)}, u32[]{:S(2)}) collective-permute-start(bf16[128,1024]{1,0:T(8,128)(2,1)S(1)} %pad_maximum_fusion.5), channel_id=1, source_target_pairs={{8,0},{16,8},{24,16},{28,24},{20,28},{12,20},{4,12},{0,4},{9,1},{1... | collective-permute-start | bytes 786440 | tf_op jit(solution)/shard_map/ppermute | solution.py:196
  77.0 7.5 %collective-permute-start.14 = (bf16[144,1024]{1,0:T(8,128)(2,1)S(1)}, bf16[144,1024]{1,0:T(8,128)(2,1)S(1)}, u32[]{:S(2)}, u32[]{:S(2)}) collective-permute-start(bf16[144,1024]{1,0:T(8,128)(2,1)S(1)} %pad_maximum_fusion.3), channel_id=1, source_target_pairs={{0,8},{8,16},{16,24},{24,28},{28,20},{20,12},{12,4},{4,0},{1,9},{9... | collective-permute-start | bytes 884744 | tf_op jit(solution)/shard_map/ppermute | solution.py:196
  84.7 12.2 %collective-permute-start.19 = (bf16[272,1024]{1,0:T(8,128)(2,1)S(1)}, bf16[272,1024]{1,0:T(8,128)(2,1)S(1)}, u32[]{:S(2)}, u32[]{:S(2)}) collective-permute-start(bf16[272,1024]{1,0:T(8,128)(2,1)S(1)} %slice_dynamic-update-slice_fusion.8), channel_id=1, source_target_pairs={{8,0},{16,8},{24,16},{28,24},{20,28},{12,20},{4,12},{0,4},{9,1},{1... | collective-permute-start | bytes 1671176 | tf_op jit(solution)/shard_map/ppermute | solution.py:196
  86.3 12.6 %collective-permute-start.15 = (bf16[272,1024]{1,0:T(8,128)(2,1)S(1)}, bf16[272,1024]{1,0:T(8,128)(2,1)S(1)}, u32[]{:S(2)}, u32[]{:S(2)}) collective-permute-start(bf16[272,1024]{1,0:T(8,128)(2,1)S(1)} %fusion.18), channel_id=1, source_target_pairs={{0,8},{8,16},{16,24},{24,28},{28,20},{20,12},{12,4},{4,0},{1,9},{9... | collective-permute-start | bytes 1671176 | tf_op jit(solution)/shard_map/ppermute | solution.py:196
  99.3 12.4 %collective-permute-start.16 = (bf16[272,1024]{1,0:T(8,128)(2,1)S(1)}, bf16[272,1024]{1,0:T(8,128)(2,1)S(1)}, u32[]{:S(2)}, u32[]{:S(2)}) collective-permute-start(bf16[272,1024]{1,0:T(8,128)(2,1)S(1)} %get-tuple-element.43), channel_id=1, source_target_pairs={{0,8},{8,16},{16,24},{24,28},{28,20},{20,12},{12,4},{4,0},{1,9},{9... | collective-permute-start | bytes 1671176 | tf_op jit(solution)/shard_map/ppermute | solution.py:196
  99.9 11.9 %collective-permute-start.20 = (bf16[272,1024]{1,0:T(8,128)(2,1)S(1)}, bf16[272,1024]{1,0:T(8,128)(2,1)S(1)}, u32[]{:S(2)}, u32[]{:S(2)}) collective-permute-start(bf16[272,1024]{1,0:T(8,128)(2,1)S(1)} %get-tuple-element.44), channel_id=1, source_target_pairs={{8,0},{16,8},{24,16},{28,24},{20,28},{12,20},{4,12},{0,4},{9,1},{1... | collective-permute-start | bytes 1671176 | tf_op jit(solution)/shard_map/ppermute | solution.py:196
  112.1 10.2 %collective-permute-start.17 = (bf16[272,1024]{1,0:T(8,128)(2,1)S(1)}, bf16[272,1024]{1,0:T(8,128)(2,1)S(1)}, u32[]{:S(2)}, u32[]{:S(2)}) collective-permute-start(bf16[272,1024]{1,0:T(8,128)(2,1)S(1)} %get-tuple-element.41), channel_id=1, source_target_pairs={{0,8},{8,16},{16,24},{24,28},{28,20},{20,12},{12,4},{4,0},{1,9},{9... | collective-permute-start | bytes 1671176 | tf_op jit(solution)/shard_map/ppermute | solution.py:196
  112.6 9.7 %collective-permute-start.21 = (bf16[272,1024]{1,0:T(8,128)(2,1)S(1)}, bf16[272,1024]{1,0:T(8,128)(2,1)S(1)}, u32[]{:S(2)}, u32[]{:S(2)}) collective-permute-start(bf16[272,1024]{1,0:T(8,128)(2,1)S(1)} %get-tuple-element.42), channel_id=1, source_target_pairs={{8,0},{16,8},{24,16},{28,24},{20,28},{12,20},{4,12},{0,4},{9,1},{1... | collective-permute-start | bytes 1671176 | tf_op jit(solution)/shard_map/ppermute | solution.py:196
  (4 other events, 17.8 us)

commit v4 on v3

--- a/solution.py
+++ b/solution.py
@@ -205,12 +205,14 @@
     def listed(arrays, slot):
         return (slot, units, tuple((w, 0) for w in arrays))
 
-    gate_up = [jnp.concatenate(w[:2]) for w in own]
-
-    def packed(both, down, slot):
-        return (slot, units, ((both, 0), (both, units), (down, 0)))
-
     first = [listed(w, i) for i, w in enumerate(own)]
+    to_dp = [list(w) for w in own]
+    for r in range(1, n_seq):
+        for i in range(here):
+            gate, up = shifted(own[i][0], "seq", n_seq, r), shifted(own[i][1], "seq", n_seq, r)
+            gate, up, down, *to_dp[i][:2] = lax.optimization_barrier((gate, up, own[i][2], *to_dp[i][:2]))
+            first.append(listed([gate, up, shifted(down, "seq", n_seq, r)], r * here + i))
+
     groups = [[0, 1, -1]] + [[s, -s] for s in range(2, reach + 1)] + ([[far]] if even else [])
 
     slots = [[((c + e // here) % n_seq) * here + e % here for e in range(held)] for c in range(n_seq)]
@@ -237,12 +239,12 @@
     def low_half(a):
         return jnp.concatenate([a[half:tokens], a[tokens + half : 2 * tokens]])
 
+    shares = [
+        [shifted(w, "dp", n_dp, r) for w in to_dp[i][::-1]][::-1] for r in range(1, n_dp) for i in range(here)
+    ]
+
     arrived = {0: jnp.concatenate([hidden_rows, out_grad, gate_rows(dense, width)])}
     arrived[-1], arrived[1] = around(arrived[0], fw), around(arrived[0], bw)
-    for r in range(1, n_seq):
-        for i in range(here):
-            down = after(own[i][2], arrived[1][:1]) if few else own[i][2]
-            first.append(packed(shifted(gate_up[i], "seq", n_seq, r), shifted(down, "seq", n_seq, r), r * here + i))
     for s in range(2, reach + 1):
         ahead, behind = arrived[1 - s], arrived[s - 1]
         if few and s > 2:
@@ -251,22 +253,20 @@
         arrived[-s], arrived[s] = around(ahead, fw), around(behind, bw)
     if few and reach > 1:
         done[reach - 2] = work(reach - 2, first, False)
-    end = []
+    tied = lax.optimization_barrier((arrived[-reach], arrived[reach], [(w[0], w[2]) for w in shares]))
+    arrived[-reach], arrived[reach], early = tied
+    late = [w[1] for w in shares]
     if even:
         ahead, behind = after(arrived[1 - far], *last), after(arrived[far - 1], *last)
         top, low = around(top_half(ahead), fw), around(low_half(behind), bw)
-        end = [top[:1], low[:1]]
+        top, low, late = lax.optimization_barrier((top, low, late))
         arrived[far] = jnp.concatenate([top[:half], low[:half], top[half:tokens], low[half:], top[tokens:]])
-
     rest = []
-    for r in range(1, n_dp):
-        for i in range(here):
-            down, both = shifted(own[i][2], "dp", n_dp, r), shifted(gate_up[i], "dp", n_dp, r)
-            rest.append(packed(both, down, i))
-            down, both = after(down, *last, arrived[reach][:1]), after(both, *last, *end)
-            for q in range(1, n_seq):
-                rest.append(packed(shifted(both, "seq", n_seq, q), shifted(down, "seq", n_seq, q), q * here + i))
-
+    for k, ((gate, down), up) in enumerate(zip(early, late)):
+        share = [gate, up, down]
+        rest.append(listed(share, k % here))
+        for q in range(1, n_seq):
+            rest.append(listed([shifted(w, "seq", n_seq, q) for w in share], q * here + k % here))
     if few:
         done[reach - 1] = work(reach - 1, first, False)
 
@@ -282,47 +282,37 @@
         return part + travelled.astype(jnp.float32)
 
     def plus_top(a, t):
-        return jnp.concatenate(
-            [
-                plus(a[:half], t[:half]),
-                a[half:tokens],
-                plus(a[tokens : tokens + half], t[half:tokens]),
-                a[tokens + half : 2 * tokens],
-                plus(a[2 * tokens :], t[tokens:]),
-            ]
-        )
+        return jnp.concatenate([plus(a[:half], t[:half]), a[half:tokens], plus(a[tokens:], t[half:])])
 
     def plus_low(a, t):
-        return jnp.concatenate(
-            [
-                a[:half],
-                plus(a[half:tokens], t[:half]),
-                a[tokens : tokens + half],
-                plus(a[tokens + half : 2 * tokens], t[half:]),
-                a[2 * tokens :],
-            ]
-        )
+        return jnp.concatenate([a[:half], plus(a[half:tokens], t), a[tokens:]])
+
+    def two(a):
+        return [a[:tokens], a[tokens:]]
 
     came = None
     if even:
         (sums,) = finish(len(groups) - 1)
-        came = around(rounded(top_half(sums)), fw), around(rounded(low_half(sums)), bw)
+        tops = [rounded(jnp.concatenate([a[:half], a[tokens:]])) for a in two(sums)]
+        lows = [rounded(a[half:tokens]) for a in two(sums)]
+        came = [(around(a, fw), around(b, bw)) for a, b in zip(tops, lows)]
     before = []
     for s in range(reach, 0, -1):
         sums_fw, sums_bw = finish(s - 1, *before, skip=int(s == 1))
+        parts = list(zip(two(sums_fw), two(sums_bw)))
         if came is None:
-            out = rounded(sums_fw), rounded(sums_bw)
+            out = [(rounded(a), rounded(b)) for a, b in parts]
         elif even and s == reach:
-            out = rounded(plus_top(sums_fw, came[0])), rounded(plus_low(sums_bw, came[1]))
+            out = [(rounded(plus_top(a, t)), rounded(plus_low(b, u))) for (a, b), (t, u) in zip(parts, came)]
         else:
-            out = rounded(plus(sums_fw, came[0])), rounded(plus(sums_bw, came[1]))
-        before = [] if came is None else [a[:1] for a in came]
-        came = around(out[0], fw), around(out[1], bw)
-    (own_sums,) = finish(0, *[a[:1] for a in out], take=1)
-    total = plus(plus(own_sums, came[0]), came[1])
-    mixed, grad_rows = rounded(total[:tokens]), rounded(total[tokens : 2 * tokens])
-
-    thirds = total[2 * tokens : 2 * tokens + 3 * lines].reshape(3, lines, width)
+            out = [(rounded(plus(a, t)), rounded(plus(b, u))) for (a, b), (t, u) in zip(parts, came)]
+        before = [] if came is None else [a[:1] for pair in came for a in pair]
+        came = [(around(a, fw), around(b, bw)) for a, b in out]
+    (own_sums,) = finish(0, *[a[:1] for pair in out for a in pair], take=1)
+    mixed, total = [plus(plus(a, t), u) for a, (t, u) in zip(two(own_sums), came)]
+    mixed, grad_rows, total = rounded(mixed), rounded(total[:tokens]), total[tokens:]
+
+    thirds = total[: 3 * lines].reshape(3, lines, width)
     by_expert = (thirds[0] + thirds[1] + thirds[2]).reshape(experts, tokens)
     grad_gates = jnp.sum(jnp.where(chosen, by_expert[:, None, :], 0.0), axis=0).T
     return (mixed, grad_rows, grad_gates)

time: 125 us -> 121 us (0.968)
  waiting for transfers between devices: 43.9 us -> 34.8 us
  starting transfers between devices: 22.7 us -> 31.7 us
  Pallas kernels: 49.4 us -> 43.8 us
  local copies, waits for them, and re-layouts: 1.05 us -> 4.27 us
    ppermute x16 -> x24, starting transfers between devices: 18.1 us -> 26.2 us  [around(): return lax.ppermute(a, 'expert', way)]
    ppermute x6 -> x9, waiting for transfers between devices: 11.6 us -> 4.33 us  [shifted(): return lax.ppermute(a, axis, [((i + by) % size, i) for i in range(size)])]
    pallas_call x8, Pallas kernels: 49.4 us -> 43.8 us  [experts_part(): pl.pallas_call(functools.partial(part_kernel, layout, len(flat), len(bloc...]
    unnamed x19 -> x18, local copies, waits for them, and re-layouts: 0.11 us -> 3.39 us
    concatenate x1 -> x3, other arithmetic: 2.64 us -> 0.05 us  [the longest x2 0.04 us: plus_low(): return jnp.concatenate([a[:half], plus(a[half:tokens], t), a[tokens:]])]
    ppermute x16 -> x24, waiting for transfers between devices: 32.4 us -> 30.4 us  [around(): return lax.ppermute(a, 'expert', way)]
    ppermute x6 -> x9, starting transfers between devices: 4.67 us -> 5.53 us  [shifted(): return lax.ppermute(a, axis, [((i + by) % size, i) for i in range(size)])]
  transfers between devices with their start and end apart: 22 -> 33, of which waited for: 10 -> 16; matrix products, arithmetic and copies ran while one was open for 1% -> 4% of each run, Pallas kernels for 34% -> 31%
where the time goes in v4:
time: 121 us
  Pallas kernels  43.8 us (36%)
  waiting for transfers between devices  34.8 us (29%)
  starting transfers between devices  31.7 us (26%)
  other arithmetic  5.36 us (4%)
  local copies, waits for them, and re-layouts  4.27 us (4%)
    pallas_call x8, Pallas kernels, experts_part(): pl.pallas_call(functools.partial(part_kernel, layout, len(flat), len(bloc...  43.8 us
    ppermute x24, waiting for transfers between devices, around(): return lax.ppermute(a, 'expert', way)  30.4 us
    ppermute x24, starting transfers between devices, around(): return lax.ppermute(a, 'expert', way)  26.2 us
    ppermute x9, starting transfers between devices, shifted(): return lax.ppermute(a, axis, [((i + by) % size, i) for i in range(size)])  5.53 us
    ppermute x9, waiting for transfers between devices, shifted(): return lax.ppermute(a, axis, [((i + by) % size, i) for i in range(size)])  4.33 us
    unnamed x18, local copies, waits for them, and re-layouts  3.39 us
  transfers between devices with their start and end apart: 33, of which 16 were waited for; matrix products, arithmetic and copies ran while one was open for 4% of the time, Pallas kernels for 31%

profile of v4, /device:TPU:0, one launch (start us, length us, event | category | flops | bytes accessed | tf_op | source)
XLA Modules:
  0.0 120.9 jit_solution(16360139117983649395)
XLA Ops:
  5.7 2.7 %collective-permute-start.2 = (bf16[272,1024]{1,0:T(8,128)(2,1)S(1)}, bf16[272,1024]{1,0:T(8,128)(2,1)}, u32[]{:S(2)}, u32[]{:S(2)}) collective-permute-start(bf16[272,1024]{1,0:T(8,128)(2,1)S(1)} %pad_maximum_fusion.refs_1_), channel_id=1, source_target_pairs={{8,0},{16,8},{24,16},{28,24},{20,28},{12,20},{4,12},{0,4},{9,1},{1... | collective-permute-start | bytes 1671176 | tf_op jit(solution)/shard_map/ppermute | solution.py:196
  8.5 1.9 %collective-permute-start.10 = (bf16[352,1024]{1,0:T(8,128)(2,1)}, bf16[352,1024]{1,0:T(8,128)(2,1)S(1)}, u32[]{:S(2)}, u32[]{:S(2)}) collective-permute-start(bf16[352,1024]{1,0:T(8,128)(2,1)} %bitcast.23), channel_id=1, source_target_pairs={{2,0},{0,2},{3,1},{1,3},{6,4},{4,6},{7,5},{5,7},{10,8},{8,10},{11,... | collective-permute-start | bytes 2162696 | tf_op jit(solution)/shard_map/ppermute | solution.py:193
  11.2 10.5 %collective-permute-done.2.refs_2_.refs_1_ = bf16[272,1024]{1,0:T(8,128)(2,1)} collective-permute-done((bf16[272,1024]{1,0:T(8,128)(2,1)S(1)}, bf16[272,1024]{1,0:T(8,128)(2,1)}, u32[]{:S(2)}, u32[]{:S(2)}) %collective-permute-start.2) | collective-permute-done | bytes 557088 | tf_op jit(solution)/shard_map/ppermute | solution.py:196
  21.7 1.7 %collective-permute-start.7 = (bf16[272,1024]{1,0:T(8,128)(2,1)}, bf16[272,1024]{1,0:T(8,128)(2,1)S(1)}, u32[]{:S(2)}, u32[]{:S(2)}) collective-permute-start(bf16[272,1024]{1,0:T(8,128)(2,1)} %collective-permute-done.2.refs_2_.refs_1_), channel_id=1, source_target_pairs={{8,0},{16,8},{24,16},{28,24},{20,28},{12,20},{4,12},{0,4},{9,1},{1... | collective-permute-start | bytes 1671176 | tf_op jit(solution)/shard_map/ppermute | solution.py:196
  23.7 1.7 %collective-permute-start.9 = (bf16[352,1024]{1,0:T(8,128)(2,1)}, bf16[352,1024]{1,0:T(8,128)(2,1)S(1)}, u32[]{:S(2)}, u32[]{:S(2)}) collective-permute-start(bf16[352,1024]{1,0:T(8,128)(2,1)} %bitcast.11), channel_id=1, source_target_pairs={{2,0},{0,2},{3,1},{1,3},{6,4},{4,6},{7,5},{5,7},{10,8},{8,10},{11,... | collective-permute-start | bytes 2162696 | tf_op jit(solution)/shard_map/ppermute | solution.py:193
  29.1 7.9 %shard_map.103 = (f32[384,1024]{1,0:T(8,128)S(1)}, f32[384,1024]{1,0:T(8,128)S(1)}, f32[384,128]{1,0:T(8,128)S(1)}) custom-call(s32[2]{0:T(128)S(1)} %broadcast_add_fusion.refs_0_, bf16[272,1024]{1,0:T(8,128)(2,1)S(1)} %pad_maximum_fusion.refs_1_, bf16[272,1024]{1,0:T(8,128)(2,1)} %collective-permute-done.2.refs_2_.refs_1_, ...), custom_call_target="tpu_custom_call" | custom-call | flops 33218887680 | bytes 90439680 | tf_op jit(solution)/shard_map/pallas_call | solution.py:139
  39.4 5.0 %shard_map.104 = (f32[256,1024]{1,0:T(8,128)S(1)}, f32[256,1024]{1,0:T(8,128)S(1)}, f32[256,128]{1,0:T(8,128)S(1)}) custom-call(s32[2]{0:T(128)S(1)} %broadcast_add_fusion.refs_0_, bf16[272,1024]{1,0:T(8,128)(2,1)S(1)} %collective-permute-done.7.refs_1_, bf16[272,1024]{1,0:T(8,128)(2,1)S(1)} %collective-permute-done.1.refs_2_, ...), custom_call_target="tpu_custom_call" | custom-call | flops 22145925120 | bytes 74711040 | tf_op jit(solution)/shard_map/pallas_call | solution.py:139
  44.4 5.9 %collective-permute-done.6.refs_2_ = bf16[272,1024]{1,0:T(8,128)(2,1)S(1)} collective-permute-done((bf16[272,1024]{1,0:T(8,128)(2,1)S(1)}, bf16[272,1024]{1,0:T(8,128)(2,1)S(1)}, u32[]{:S(2)}, u32[]{:S(2)}) %collective-permute-start.6) | collective-permute-done | bytes 557088 | tf_op jit(solution)/shard_map/ppermute | solution.py:196
  52.8 1.7 %collective-permute-start.11 = (bf16[144,1024]{1,0:T(8,128)(2,1)S(1)}, bf16[144,1024]{1,0:T(8,128)(2,1)S(1)}, u32[]{:S(2)}, u32[]{:S(2)}) collective-permute-start(bf16[144,1024]{1,0:T(8,128)(2,1)S(1)} %pad_maximum_fusion.1), channel_id=1, source_target_pairs={{0,8},{8,16},{16,24},{24,28},{28,20},{20,12},{12,4},{4,0},{1,9},{9... | collective-permute-start | bytes 884744 | tf_op jit(solution)/shard_map/ppermute | solution.py:196
  54.5 5.0 %shard_map.108 = (f32[256,1024]{1,0:T(8,128)S(1)}, f32[256,1024]{1,0:T(8,128)S(1)}, f32[256,128]{1,0:T(8,128)S(1)}) custom-call(s32[2]{0:T(128)S(1)} %broadcast_add_fusion.refs_0_, bf16[272,1024]{1,0:T(8,128)(2,1)S(1)} %collective-permute-done.8.refs_1_, bf16[272,1024]{1,0:T(8,128)(2,1)S(1)} %collective-permute-done.6.refs_2_, ...), custom_call_target="tpu_custom_call" | custom-call | flops 22145925120 | bytes 74711040 | tf_op jit(solution)/shard_map/pallas_call | solution.py:139
  61.9 2.1 %collective-permute-done.15.refs_6_.refs_7_.refs_12_ = bf16[352,1024]{1,0:T(8,128)(2,1)S(1)} collective-permute-done((bf16[352,1024]{1,0:T(8,128)(2,1)S(1)}, bf16[352,1024]{1,0:T(8,128)(2,1)S(1)}, u32[]{:S(2)}, u32[]{:S(2)}) %collective-permute-start.15) | collective-permute-done | bytes 720928 | tf_op jit(solution)/shard_map/ppermute | solution.py:193
  64.0 5.8 %shard_map.110 = f32[272,1024]{1,0:T(8,128)S(1)} custom-call(s32[2]{0:T(128)S(1)} %broadcast_add_fusion.refs_0_, bf16[272,1024]{1,0:T(8,128)(2,1)S(1)} %slice_dynamic-update-slice_fusion.4.refs_1_, bf16[352,1024]{1,0:T(8,128)(2,1)S(1)} %bitcast.15, bf16[352,1024]{1,0:T(8,128)(2,1)S(1)} %bitcast.21, bf16[352,1024]{1,0:T(8,128)(2,1)S(1)} %bitcast.27, ...), custom_call_target="tpu_custom_call" | custom-call | flops 22145925120 | bytes 102236160 | tf_op jit(solution)/shard_map/pallas_call | solution.py:139
  69.9 1.6 %collective-permute-start.29 = (bf16[64,1024]{1,0:T(8,128)(2,1)S(1)}, bf16[64,1024]{1,0:T(8,128)(2,1)S(1)}, u32[]{:S(2)}, u32[]{:S(2)}) collective-permute-start(bf16[64,1024]{1,0:T(8,128)(2,1)S(1)} %get-tuple-element.76), channel_id=1, source_target_pairs={{8,0},{16,8},{24,16},{28,24},{20,28},{12,20},{4,12},{0,4},{9,1},{1... | collective-permute-start | bytes 393224 | tf_op jit(solution)/shard_map/ppermute | solution.py:196
  71.6 1.6 %collective-permute-start.21 = (bf16[64,1024]{1,0:T(8,128)(2,1)S(1)}, bf16[64,1024]{1,0:T(8,128)(2,1)S(1)}, u32[]{:S(2)}, u32[]{:S(2)}) collective-permute-start(bf16[64,1024]{1,0:T(8,128)(2,1)S(1)} %get-tuple-element.77), channel_id=1, source_target_pairs={{8,0},{16,8},{24,16},{28,24},{20,28},{12,20},{4,12},{0,4},{9,1},{1... | collective-permute-start | bytes 393224 | tf_op jit(solution)/shard_map/ppermute | solution.py:196
  74.1 5.2 %shard_map.109 = f32[544,1024]{1,0:T(8,128)S(1)} custom-call(s32[2]{0:T(128)S(1)} %broadcast_add_fusion.refs_0_, bf16[272,1024]{1,0:T(8,128)(2,1)S(1)} %collective-permute-done.8.refs_1_, bf16[272,1024]{1,0:T(8,128)(2,1)S(1)} %collective-permute-done.6.refs_2_, bf16[352,1024]{1,0:T(8,128)(2,1)S(1)} %collective-permute-done.9.refs_2_.refs_3_.refs_8_, ...), custom_call_target="tpu_custom_call" | custom-call | flops 22145925120 | bytes 74711040 | tf_op jit(solution)/shard_map/pallas_call | solution.py:139
  79.6 2.1 %collective-permute-done.25 = bf16[80,1024]{1,0:T(8,128)(2,1)S(1)} collective-permute-done((bf16[80,1024]{1,0:T(8,128)(2,1)S(1)}, bf16[80,1024]{1,0:T(8,128)(2,1)S(1)}, u32[]{:S(2)}, u32[]{:S(2)}) %collective-permute-start.25) | collective-permute-done | bytes 163872 | tf_op jit(solution)/shard_map/ppermute | solution.py:196
  82.6 1.6 %collective-permute-start.22 = (bf16[128,1024]{1,0:T(8,128)(2,1)S(1)}, bf16[128,1024]{1,0:T(8,128)(2,1)S(1)}, u32[]{:S(2)}, u32[]{:S(2)}) collective-permute-start(bf16[128,1024]{1,0:T(8,128)(2,1)S(1)} %pad_maximum_fusion.6), channel_id=1, source_target_pairs={{8,0},{16,8},{24,16},{28,24},{20,28},{12,20},{4,12},{0,4},{9,1},{1... | collective-permute-start | bytes 786440 | tf_op jit(solution)/shard_map/ppermute | solution.py:196
  84.2 1.6 %collective-permute-start.30 = (bf16[144,1024]{1,0:T(8,128)(2,1)S(1)}, bf16[144,1024]{1,0:T(8,128)(2,1)S(1)}, u32[]{:S(2)}, u32[]{:S(2)}) collective-permute-start(bf16[144,1024]{1,0:T(8,128)(2,1)S(1)} %pad_maximum_fusion.3), channel_id=1, source_target_pairs={{8,0},{16,8},{24,16},{28,24},{20,28},{12,20},{4,12},{0,4},{9,1},{1... | collective-permute-start | bytes 884744 | tf_op jit(solution)/shard_map/ppermute | solution.py:196
  86.4 5.2 %shard_map.107 = f32[544,1024]{1,0:T(8,128)S(1)} custom-call(s32[2]{0:T(128)S(1)} %broadcast_add_fusion.refs_0_, bf16[272,1024]{1,0:T(8,128)(2,1)S(1)} %collective-permute-done.7.refs_1_, bf16[272,1024]{1,0:T(8,128)(2,1)S(1)} %collective-permute-done.1.refs_2_, bf16[352,1024]{1,0:T(8,128)(2,1)S(1)} %collective-permute-done.9.refs_2_.refs_3_.refs_8_, ...), custom_call_target="tpu_custom_call" | custom-call | flops 22145925120 | bytes 74711040 | tf_op jit(solution)/shard_map/pallas_call | solution.py:139
  92.6 1.5 %collective-permute-start.23 = (bf16[128,1024]{1,0:T(8,128)(2,1)S(1)}, bf16[128,1024]{1,0:T(8,128)(2,1)S(1)}, u32[]{:S(2)}, u32[]{:S(2)}) collective-permute-start(bf16[128,1024]{1,0:T(8,128)(2,1)S(1)} %get-tuple-element.70), channel_id=1, source_target_pairs={{8,0},{16,8},{24,16},{28,24},{20,28},{12,20},{4,12},{0,4},{9,1},{1... | collective-permute-start | bytes 786440 | tf_op jit(solution)/shard_map/ppermute | solution.py:196
  94.1 4.1 %collective-permute-done.30 = bf16[144,1024]{1,0:T(8,128)(2,1)S(1)} collective-permute-done((bf16[144,1024]{1,0:T(8,128)(2,1)S(1)}, bf16[144,1024]{1,0:T(8,128)(2,1)S(1)}, u32[]{:S(2)}, u32[]{:S(2)}) %collective-permute-start.30) | collective-permute-done | bytes 294944 | tf_op jit(solution)/shard_map/ppermute | solution.py:196
  100.4 5.8 %shard_map.106 = f32[544,1024]{1,0:T(8,128)S(1)} custom-call(s32[2]{0:T(128)S(1)} %broadcast_add_fusion.refs_0_, bf16[272,1024]{1,0:T(8,128)(2,1)} %collective-permute-done.2.refs_2_.refs_1_, bf16[272,1024]{1,0:T(8,128)(2,1)} %collective-permute-done.refs_3_.refs_2_, bf16[352,1024]{1,0:T(8,128)(2,1)S(1)} %collective-permute-done.9.refs_2_.refs_3_.refs_8_, ...), custom_call_target="tpu_custom_call" | custom-call | flops 22145925120 | bytes 74711040 | tf_op jit(solution)/shard_map/pallas_call | solution.py:139
  112.4 4.0 %shard_map.105 = f32[272,1024]{1,0:T(8,128)S(1)} custom-call(s32[2]{0:T(128)S(1)} %broadcast_add_fusion.refs_0_, bf16[272,1024]{1,0:T(8,128)(2,1)S(1)} %pad_maximum_fusion.refs_1_, bf16[352,1024]{1,0:T(8,128)(2,1)S(1)} %collective-permute-done.9.refs_2_.refs_3_.refs_8_, bf16[352,1024]{1,0:T(8,128)(2,1)S(1)} %collective-permute-done.13.refs_3_.refs_4_.refs_9_, ...), custom_call_target="tpu_custom_call" | custom-call | flops 11072962560 | bytes 58982400 | tf_op jit(solution)/shard_map/pallas_call | solution.py:139
  117.3 1.9 %collective-permute-done.28 = bf16[144,1024]{1,0:T(8,128)(2,1)S(1)} collective-permute-done((bf16[144,1024]{1,0:T(8,128)(2,1)S(1)}, bf16[144,1024]{1,0:T(8,128)(2,1)S(1)}, u32[]{:S(2)}, u32[]{:S(2)}) %collective-permute-start.28) | collective-permute-done | bytes 294944 | tf_op jit(solution)/shard_map/ppermute | solution.py:196
  (105 shorter events, 32.0 us)
Async XLA Ops:
  4.2 21.2 %collective-permute-start.5 = (bf16[352,1024]{1,0:T(8,128)(2,1)}, bf16[352,1024]{1,0:T(8,128)(2,1)S(1)}, u32[]{:S(2)}, u32[]{:S(2)}) collective-permute-start(bf16[352,1024]{1,0:T(8,128)(2,1)} %bitcast.22), channel_id=1, source_target_pairs={{1,0},{0,1},{3,2},{2,3},{5,4},{4,5},{7,6},{6,7},{9,8},{8,9},{11,10... | collective-permute-start | bytes 2162696 | tf_op jit(solution)/shard_map/ppermute | solution.py:193
  5.7 16.0 %collective-permute-start.2 = (bf16[272,1024]{1,0:T(8,128)(2,1)S(1)}, bf16[272,1024]{1,0:T(8,128)(2,1)}, u32[]{:S(2)}, u32[]{:S(2)}) collective-permute-start(bf16[272,1024]{1,0:T(8,128)(2,1)S(1)} %pad_maximum_fusion.refs_1_), channel_id=1, source_target_pairs={{8,0},{16,8},{24,16},{28,24},{20,28},{12,20},{4,12},{0,4},{9,1},{1... | collective-permute-start | bytes 1671176 | tf_op jit(solution)/shard_map/ppermute | solution.py:196
  8.4 15.0 %collective-permute-start = (bf16[272,1024]{1,0:T(8,128)(2,1)S(1)}, bf16[272,1024]{1,0:T(8,128)(2,1)}, u32[]{:S(2)}, u32[]{:S(2)}) collective-permute-start(bf16[272,1024]{1,0:T(8,128)(2,1)S(1)} %pad_maximum_fusion.refs_1_), channel_id=1, source_target_pairs={{0,8},{8,16},{16,24},{24,28},{28,20},{20,12},{12,4},{4,0},{1,9},{9... | collective-permute-start | bytes 1671176 | tf_op jit(solution)/shard_map/ppermute | solution.py:196
  8.5 35.9 %collective-permute-start.10 = (bf16[352,1024]{1,0:T(8,128)(2,1)}, bf16[352,1024]{1,0:T(8,128)(2,1)S(1)}, u32[]{:S(2)}, u32[]{:S(2)}) collective-permute-start(bf16[352,1024]{1,0:T(8,128)(2,1)} %bitcast.23), channel_id=1, source_target_pairs={{2,0},{0,2},{3,1},{1,3},{6,4},{4,6},{7,5},{5,7},{10,8},{8,10},{11,... | collective-permute-start | bytes 2162696 | tf_op jit(solution)/shard_map/ppermute | solution.py:193
  21.7 15.3 %collective-permute-start.7 = (bf16[272,1024]{1,0:T(8,128)(2,1)}, bf16[272,1024]{1,0:T(8,128)(2,1)S(1)}, u32[]{:S(2)}, u32[]{:S(2)}) collective-permute-start(bf16[272,1024]{1,0:T(8,128)(2,1)} %collective-permute-done.2.refs_2_.refs_1_), channel_id=1, source_target_pairs={{8,0},{16,8},{24,16},{28,24},{20,28},{12,20},{4,12},{0,4},{9,1},{1... | collective-permute-start | bytes 1671176 | tf_op jit(solution)/shard_map/ppermute | solution.py:196
  23.4 14.0 %collective-permute-start.1 = (bf16[272,1024]{1,0:T(8,128)(2,1)}, bf16[272,1024]{1,0:T(8,128)(2,1)S(1)}, u32[]{:S(2)}, u32[]{:S(2)}) collective-permute-start(bf16[272,1024]{1,0:T(8,128)(2,1)} %collective-permute-done.refs_3_.refs_2_), channel_id=1, source_target_pairs={{0,8},{8,16},{16,24},{24,28},{28,20},{20,12},{12,4},{4,0},{1,9},{9... | collective-permute-start | bytes 1671176 | tf_op jit(solution)/shard_map/ppermute | solution.py:196
  23.7 20.7 %collective-permute-start.9 = (bf16[352,1024]{1,0:T(8,128)(2,1)}, bf16[352,1024]{1,0:T(8,128)(2,1)S(1)}, u32[]{:S(2)}, u32[]{:S(2)}) collective-permute-start(bf16[352,1024]{1,0:T(8,128)(2,1)} %bitcast.11), channel_id=1, source_target_pairs={{2,0},{0,2},{3,1},{1,3},{6,4},{4,6},{7,5},{5,7},{10,8},{8,10},{11,... | collective-permute-start | bytes 2162696 | tf_op jit(solution)/shard_map/ppermute | solution.py:193
  25.4 34.0 %collective-permute-start.13 = (bf16[352,1024]{1,0:T(8,128)(2,1)}, bf16[352,1024]{1,0:T(8,128)(2,1)S(1)}, u32[]{:S(2)}, u32[]{:S(2)}) collective-permute-start(bf16[352,1024]{1,0:T(8,128)(2,1)} %bitcast.17), channel_id=1, source_target_pairs={{2,0},{0,2},{3,1},{1,3},{6,4},{4,6},{7,5},{5,7},{10,8},{8,10},{11,... | collective-permute-start | bytes 2162696 | tf_op jit(solution)/shard_map/ppermute | solution.py:193
  37.4 12.9 %collective-permute-start.6 = (bf16[272,1024]{1,0:T(8,128)(2,1)S(1)}, bf16[272,1024]{1,0:T(8,128)(2,1)S(1)}, u32[]{:S(2)}, u32[]{:S(2)}) collective-permute-start(bf16[272,1024]{1,0:T(8,128)(2,1)S(1)} %collective-permute-done.1.refs_2_), channel_id=1, source_target_pairs={{0,8},{8,16},{16,24},{24,28},{28,20},{20,12},{12,4},{4,0},{1,9},{9... | collective-permute-start | bytes 1671176 | tf_op jit(solution)/shard_map/ppermute | solution.py:196
  38.8 12.7 %collective-permute-start.8 = (bf16[272,1024]{1,0:T(8,128)(2,1)S(1)}, bf16[272,1024]{1,0:T(8,128)(2,1)S(1)}, u32[]{:S(2)}, u32[]{:S(2)}) collective-permute-start(bf16[272,1024]{1,0:T(8,128)(2,1)S(1)} %collective-permute-done.7.refs_1_), channel_id=1, source_target_pairs={{8,0},{16,8},{24,16},{28,24},{20,28},{12,20},{4,12},{0,4},{9,1},{1... | collective-permute-start | bytes 1671176 | tf_op jit(solution)/shard_map/ppermute | solution.py:196
  51.5 10.4 %collective-permute-start.14 = (bf16[352,1024]{1,0:T(8,128)(2,1)S(1)}, bf16[352,1024]{1,0:T(8,128)(2,1)S(1)}, u32[]{:S(2)}, u32[]{:S(2)}) collective-permute-start(bf16[352,1024]{1,0:T(8,128)(2,1)S(1)} %collective-permute-done.9.refs_2_.refs_3_.refs_8_), channel_id=1, source_target_pairs={{1,0},{0,1},{3,2},{2,3},{5,4},{4,5},{7,6},{6,7},{9,8},{8,9},{11,10... | collective-permute-start | bytes 2162696 | tf_op jit(solution)/shard_map/ppermute | solution.py:193
  51.6 10.3 %collective-permute-start.16 = (bf16[352,1024]{1,0:T(8,128)(2,1)S(1)}, bf16[352,1024]{1,0:T(8,128)(2,1)S(1)}, u32[]{:S(2)}, u32[]{:S(2)}) collective-permute-start(bf16[352,1024]{1,0:T(8,128)(2,1)S(1)} %collective-permute-done.10.refs_4_.refs_5_.refs_10_), channel_id=1, source_target_pairs={{1,0},{0,1},{3,2},{2,3},{5,4},{4,5},{7,6},{6,7},{9,8},{8,9},{11,10... | collective-permute-start | bytes 2162696 | tf_op jit(solution)/shard_map/ppermute | solution.py:193
  52.8 8.9 %collective-permute-start.11 = (bf16[144,1024]{1,0:T(8,128)(2,1)S(1)}, bf16[144,1024]{1,0:T(8,128)(2,1)S(1)}, u32[]{:S(2)}, u32[]{:S(2)}) collective-permute-start(bf16[144,1024]{1,0:T(8,128)(2,1)S(1)} %pad_maximum_fusion.1), channel_id=1, source_target_pairs={{0,8},{8,16},{16,24},{24,28},{28,20},{20,12},{12,4},{4,0},{1,9},{9... | collective-permute-start | bytes 884744 | tf_op jit(solution)/shard_map/ppermute | solution.py:196
  69.9 9.6 %collective-permute-start.29 = (bf16[64,1024]{1,0:T(8,128)(2,1)S(1)}, bf16[64,1024]{1,0:T(8,128)(2,1)S(1)}, u32[]{:S(2)}, u32[]{:S(2)}) collective-permute-start(bf16[64,1024]{1,0:T(8,128)(2,1)S(1)} %get-tuple-element.76), channel_id=1, source_target_pairs={{8,0},{16,8},{24,16},{28,24},{20,28},{12,20},{4,12},{0,4},{9,1},{1... | collective-permute-start | bytes 393224 | tf_op jit(solution)/shard_map/ppermute | solution.py:196
  81.8 9.8 %collective-permute-start.18 = (bf16[128,1024]{1,0:T(8,128)(2,1)S(1)}, bf16[128,1024]{1,0:T(8,128)(2,1)S(1)}, u32[]{:S(2)}, u32[]{:S(2)}) collective-permute-start(bf16[128,1024]{1,0:T(8,128)(2,1)S(1)} %pad_maximum_fusion.5), channel_id=1, source_target_pairs={{0,8},{8,16},{16,24},{24,28},{28,20},{20,12},{12,4},{4,0},{1,9},{9... | collective-permute-start | bytes 786440 | tf_op jit(solution)/shard_map/ppermute | solution.py:196
  82.6 9.3 %collective-permute-start.22 = (bf16[128,1024]{1,0:T(8,128)(2,1)S(1)}, bf16[128,1024]{1,0:T(8,128)(2,1)S(1)}, u32[]{:S(2)}, u32[]{:S(2)}) collective-permute-start(bf16[128,1024]{1,0:T(8,128)(2,1)S(1)} %pad_maximum_fusion.6), channel_id=1, source_target_pairs={{8,0},{16,8},{24,16},{28,24},{20,28},{12,20},{4,12},{0,4},{9,1},{1... | collective-permute-start | bytes 786440 | tf_op jit(solution)/shard_map/ppermute | solution.py:196
  84.2 14.0 %collective-permute-start.30 = (bf16[144,1024]{1,0:T(8,128)(2,1)S(1)}, bf16[144,1024]{1,0:T(8,128)(2,1)S(1)}, u32[]{:S(2)}, u32[]{:S(2)}) collective-permute-start(bf16[144,1024]{1,0:T(8,128)(2,1)S(1)} %pad_maximum_fusion.3), channel_id=1, source_target_pairs={{8,0},{16,8},{24,16},{28,24},{20,28},{12,20},{4,12},{0,4},{9,1},{1... | collective-permute-start | bytes 884744 | tf_op jit(solution)/shard_map/ppermute | solution.py:196
  85.9 12.3 %collective-permute-start.26 = (bf16[144,1024]{1,0:T(8,128)(2,1)S(1)}, bf16[144,1024]{1,0:T(8,128)(2,1)S(1)}, u32[]{:S(2)}, u32[]{:S(2)}) collective-permute-start(bf16[144,1024]{1,0:T(8,128)(2,1)S(1)} %pad_maximum_fusion.2), channel_id=1, source_target_pairs={{0,8},{8,16},{16,24},{24,28},{28,20},{20,12},{12,4},{4,0},{1,9},{9... | collective-permute-start | bytes 884744 | tf_op jit(solution)/shard_map/ppermute | solution.py:196
  92.0 14.2 %collective-permute-start.19 = (bf16[128,1024]{1,0:T(8,128)(2,1)S(1)}, bf16[128,1024]{1,0:T(8,128)(2,1)S(1)}, u32[]{:S(2)}, u32[]{:S(2)}) collective-permute-start(bf16[128,1024]{1,0:T(8,128)(2,1)S(1)} %get-tuple-element.69), channel_id=1, source_target_pairs={{0,8},{8,16},{16,24},{24,28},{28,20},{20,12},{12,4},{4,0},{1,9},{9... | collective-permute-start | bytes 786440 | tf_op jit(solution)/shard_map/ppermute | solution.py:196
  92.6 13.6 %collective-permute-start.23 = (bf16[128,1024]{1,0:T(8,128)(2,1)S(1)}, bf16[128,1024]{1,0:T(8,128)(2,1)S(1)}, u32[]{:S(2)}, u32[]{:S(2)}) collective-permute-start(bf16[128,1024]{1,0:T(8,128)(2,1)S(1)} %get-tuple-element.70), channel_id=1, source_target_pairs={{8,0},{16,8},{24,16},{28,24},{20,28},{12,20},{4,12},{0,4},{9,1},{1... | collective-permute-start | bytes 786440 | tf_op jit(solution)/shard_map/ppermute | solution.py:196
  98.4 11.2 %collective-permute-start.27 = (bf16[144,1024]{1,0:T(8,128)(2,1)S(1)}, bf16[144,1024]{1,0:T(8,128)(2,1)S(1)}, u32[]{:S(2)}, u32[]{:S(2)}) collective-permute-start(bf16[144,1024]{1,0:T(8,128)(2,1)S(1)} %get-tuple-element.61), channel_id=1, source_target_pairs={{0,8},{8,16},{16,24},{24,28},{28,20},{20,12},{12,4},{4,0},{1,9},{9... | collective-permute-start | bytes 884744 | tf_op jit(solution)/shard_map/ppermute | solution.py:196
  99.0 11.2 %collective-permute-start.31 = (bf16[144,1024]{1,0:T(8,128)(2,1)S(1)}, bf16[144,1024]{1,0:T(8,128)(2,1)S(1)}, u32[]{:S(2)}, u32[]{:S(2)}) collective-permute-start(bf16[144,1024]{1,0:T(8,128)(2,1)S(1)} %get-tuple-element.62), channel_id=1, source_target_pairs={{8,0},{16,8},{24,16},{28,24},{20,28},{12,20},{4,12},{0,4},{9,1},{1... | collective-permute-start | bytes 884744 | tf_op jit(solution)/shard_map/ppermute | solution.py:196
  106.4 10.0 %collective-permute-start.20 = (bf16[128,1024]{1,0:T(8,128)(2,1)S(1)}, bf16[128,1024]{1,0:T(8,128)(2,1)S(1)}, u32[]{:S(2)}, u32[]{:S(2)}) collective-permute-start(bf16[128,1024]{1,0:T(8,128)(2,1)S(1)} %get-tuple-element.67), channel_id=1, source_target_pairs={{0,8},{8,16},{16,24},{24,28},{28,20},{20,12},{12,4},{4,0},{1,9},{9... | collective-permute-start | bytes 786440 | tf_op jit(solution)/shard_map/ppermute | solution.py:196
  107.0 9.4 %collective-permute-start.24 = (bf16[128,1024]{1,0:T(8,128)(2,1)S(1)}, bf16[128,1024]{1,0:T(8,128)(2,1)S(1)}, u32[]{:S(2)}, u32[]{:S(2)}) collective-permute-start(bf16[128,1024]{1,0:T(8,128)(2,1)S(1)} %get-tuple-element.68), channel_id=1, source_target_pairs={{8,0},{16,8},{24,16},{28,24},{20,28},{12,20},{4,12},{0,4},{9,1},{1... | collective-permute-start | bytes 786440 | tf_op jit(solution)/shard_map/ppermute | solution.py:196
  (16 other events, 94.3 us)

commit v5 on v4

--- a/solution.py
+++ b/solution.py
@@ -15,8 +15,7 @@
     return lax.dot_general(a, b, dims, preferred_element_type=jnp.float32)
 
 
-def part_kernel(layout, arrays, blocks, tokens, lines, prior_row, is_last, *refs):
-    has_prior = prior_row is not None
+def part_kernel(layout, arrays, blocks, tokens, lines, has_prior, is_last, *refs):
     expert_ref, block_refs, refs = refs[0], refs[1 : blocks + 1], refs[blocks + 1 :]
     weight_refs, refs = refs[:arrays], refs[arrays:]
     prior, refs = (refs[:3], refs[3:]) if has_prior else ((), refs)
@@ -45,7 +44,7 @@
     ]
 
     sums = (mixed_buf, back_buf, grad_buf)
-    prior_copies = [pltpu.make_async_copy(prior[i].at[pl.ds(prior_row, rows)], sums[i], sum_sem.at[i]) for i in range(len(prior))]
+    prior_copies = [pltpu.make_async_copy(prior[i], sums[i], sum_sem.at[i]) for i in range(len(prior))]
 
     def start(copies):
         for copy in copies:
@@ -122,7 +121,7 @@
     wait(leaving)
 
 
-def experts_part(blocks, experts_here, lines, tokens, part, prior, prior_row, is_last):
+def experts_part(blocks, experts_here, lines, tokens, part, prior, is_last):
     width = blocks[0].shape[1]
     rows = len(blocks) * tokens
     flat, layout = [], []
@@ -137,7 +136,7 @@
     vmem, hbm = pl.BlockSpec(memory_space=pltpu.VMEM), pl.BlockSpec(memory_space=pltpu.HBM)
     sums, out = [(rows, width), (rows, width), (rows, 128)], [(len(blocks) * blocks[0].shape[0], width)]
     return pl.pallas_call(
-        functools.partial(part_kernel, layout, len(flat), len(blocks), tokens, lines, prior_row if prior else None, is_last),
+        functools.partial(part_kernel, layout, len(flat), len(blocks), tokens, lines, bool(prior), is_last),
         out_shape=tuple(jax.ShapeDtypeStruct(shape, jnp.float32) for shape in (out if is_last else sums)),
         in_specs=[pl.BlockSpec(memory_space=pltpu.SMEM)] + [hbm] * len(blocks) + [vmem] * len(flat) + [hbm] * len(prior),
         out_specs=(vmem,) if is_last else (hbm,) * 3,
@@ -206,14 +205,11 @@
         return (slot, units, tuple((w, 0) for w in arrays))
 
     first = [listed(w, i) for i, w in enumerate(own)]
-    to_dp = [list(w) for w in own]
     for r in range(1, n_seq):
         for i in range(here):
-            gate, up = shifted(own[i][0], "seq", n_seq, r), shifted(own[i][1], "seq", n_seq, r)
-            gate, up, down, *to_dp[i][:2] = lax.optimization_barrier((gate, up, own[i][2], *to_dp[i][:2]))
-            first.append(listed([gate, up, shifted(down, "seq", n_seq, r)], r * here + i))
-
-    groups = [[0, 1, -1]] + [[s, -s] for s in range(2, reach + 1)] + ([[far]] if even else [])
+            first.append(listed([shifted(w, "seq", n_seq, r) for w in own[i]], r * here + i))
+
+    groups = [[0]] + [[s, -s] for s in range(1, reach + 1)] + ([[far]] if even else [])
 
     slots = [[((c + e // here) % n_seq) * here + e % here for e in range(held)] for c in range(n_seq)]
     slot_of = jnp.sum(
@@ -224,11 +220,10 @@
     done = [() for _ in groups]
     last = []
 
-    def work(g, part, is_last, *wait_for, skip=0, take=None):
+    def work(g, part, is_last, *wait_for):
         named = after(experts_here, *last, *wait_for)
-        some = groups[g][skip:take]
         got = experts_part(
-            [arrived[d] for d in some], named, lines, tokens, part, done[g], skip * tokens, is_last
+            [arrived[d] for d in groups[g]], named, lines, tokens, part, done[g], is_last
         )
         last[:] = [got[-1] if not is_last else got[0][:1]]
         return got
@@ -240,19 +235,19 @@
         return jnp.concatenate([a[half:tokens], a[tokens + half : 2 * tokens]])
 
     shares = [
-        [shifted(w, "dp", n_dp, r) for w in to_dp[i][::-1]][::-1] for r in range(1, n_dp) for i in range(here)
+        [shifted(w, "dp", n_dp, r) for w in own[i][::-1]][::-1] for r in range(1, n_dp) for i in range(here)
     ]
 
     arrived = {0: jnp.concatenate([hidden_rows, out_grad, gate_rows(dense, width)])}
     arrived[-1], arrived[1] = around(arrived[0], fw), around(arrived[0], bw)
     for s in range(2, reach + 1):
         ahead, behind = arrived[1 - s], arrived[s - 1]
-        if few and s > 2:
-            done[s - 3] = work(s - 3, first, False)
+        if few:
+            done[s - 2] = work(s - 2, first, False)
             ahead, behind = after(ahead, *last), after(behind, *last)
         arrived[-s], arrived[s] = around(ahead, fw), around(behind, bw)
     if few and reach > 1:
-        done[reach - 2] = work(reach - 2, first, False)
+        done[reach - 1] = work(reach - 1, first, False)
     tied = lax.optimization_barrier((arrived[-reach], arrived[reach], [(w[0], w[2]) for w in shares]))
     arrived[-reach], arrived[reach], early = tied
     late = [w[1] for w in shares]
@@ -268,12 +263,12 @@
         for q in range(1, n_seq):
             rest.append(listed([shifted(w, "seq", n_seq, q) for w in share], q * here + k % here))
     if few:
-        done[reach - 1] = work(reach - 1, first, False)
-
-    def finish(g, *wait_for, skip=0, take=None):
-        (sums,) = work(g, rest if done[g] else first + rest, True, *wait_for, skip=skip, take=take)
-        size = sums.shape[0] // len(groups[g][skip:take])
-        return [sums[i * size : (i + 1) * size] for i in range(len(groups[g][skip:take]))]
+        done[reach] = work(reach, first, False)
+
+    def finish(g, *wait_for):
+        (sums,) = work(g, rest if done[g] else first + rest, True, *wait_for)
+        size = sums.shape[0] // len(groups[g])
+        return [sums[i * size : (i + 1) * size] for i in range(len(groups[g]))]
 
     def rounded(a):
         return a.astype(jnp.bfloat16)
@@ -293,12 +288,11 @@
     came = None
     if even:
         (sums,) = finish(len(groups) - 1)
-        tops = [rounded(jnp.concatenate([a[:half], a[tokens:]])) for a in two(sums)]
-        lows = [rounded(a[half:tokens]) for a in two(sums)]
-        came = [(around(a, fw), around(b, bw)) for a, b in zip(tops, lows)]
+        high, low = around(rounded(top_half(sums)), fw), around(rounded(low_half(sums)), bw)
+        came = [(high[:half], low[:half]), (high[half:], low[half:])]
     before = []
     for s in range(reach, 0, -1):
-        sums_fw, sums_bw = finish(s - 1, *before, skip=int(s == 1))
+        sums_fw, sums_bw = finish(s, *before)
         parts = list(zip(two(sums_fw), two(sums_bw)))
         if came is None:
             out = [(rounded(a), rounded(b)) for a, b in parts]
@@ -308,7 +302,7 @@
             out = [(rounded(plus(a, t)), rounded(plus(b, u))) for (a, b), (t, u) in zip(parts, came)]
         before = [] if came is None else [a[:1] for pair in came for a in pair]
         came = [(around(a, fw), around(b, bw)) for a, b in out]
-    (own_sums,) = finish(0, *[a[:1] for pair in out for a in pair], take=1)
+    (own_sums,) = finish(0, *[a[:1] for pair in out for a in pair])
     mixed, total = [plus(plus(a, t), u) for a, (t, u) in zip(two(own_sums), came)]
     mixed, grad_rows, total = rounded(mixed), rounded(total[:tokens]), total[tokens:]
 

time: 121 us -> 116 us (0.959)
  waiting for transfers between devices: 34.8 us -> 31.6 us
  starting transfers between devices: 31.7 us -> 29.6 us
  Pallas kernels: 43.8 us -> 45.6 us
    ppermute x9, waiting for transfers between devices: 4.33 us -> 2.11 us  [shifted(): return lax.ppermute(a, axis, [((i + by) % size, i) for i in range(size)])]
    ppermute x24 -> x22, starting transfers between devices: 26.2 us -> 24 us  [around(): return lax.ppermute(a, 'expert', way)]
    pallas_call x8 -> x9, Pallas kernels: 43.8 us -> 45.6 us  [experts_part(): pl.pallas_call(functools.partial(part_kernel, layout, len(flat), len(bloc...]
    unnamed x18 -> x16, local copies, waits for them, and re-layouts: 3.39 us -> 2.31 us
    ppermute x24 -> x22, waiting for transfers between devices: 30.4 us -> 29.5 us  [around(): return lax.ppermute(a, 'expert', way)]
  transfers between devices with their start and end apart: 33 -> 31, of which waited for: 16 -> 12; matrix products, arithmetic and copies ran while one was open for 4% -> 3% of each run, Pallas kernels for 31% -> 34%
where the time goes in v5:
time: 116 us
  Pallas kernels  45.6 us (39%)
  waiting for transfers between devices  31.6 us (27%)
  starting transfers between devices  29.6 us (26%)
  other arithmetic  4.69 us (4%)
  local copies, waits for them, and re-layouts  3.2 us (3%)
    pallas_call x9, Pallas kernels, experts_part(): pl.pallas_call(functools.partial(part_kernel, layout, len(flat), len(bloc...  45.6 us
    ppermute x22, waiting for transfers between devices, around(): return lax.ppermute(a, 'expert', way)  29.5 us
    ppermute x22, starting transfers between devices, around(): return lax.ppermute(a, 'expert', way)  24 us
    ppermute x9, starting transfers between devices, shifted(): return lax.ppermute(a, axis, [((i + by) % size, i) for i in range(size)])  5.56 us
  transfers between devices with their start and end apart: 31, of which 12 were waited for; matrix products, arithmetic and copies ran while one was open for 3% of the time, Pallas kernels for 34%

profile of v5, /device:TPU:0, one launch (start us, length us, event | category | flops | bytes accessed | tf_op | source)
XLA Modules:
  0.0 115.7 jit_solution(7799121487204108562)
XLA Ops:
  3.5 2.7 %collective-permute-start = (bf16[272,1024]{1,0:T(8,128)(2,1)S(1)}, bf16[272,1024]{1,0:T(8,128)(2,1)}, u32[]{:S(2)}, u32[]{:S(2)}) collective-permute-start(bf16[272,1024]{1,0:T(8,128)(2,1)S(1)} %pad_maximum_fusion.refs_1_), channel_id=1, source_target_pairs={{0,8},{8,16},{16,24},{24,28},{28,20},{20,12},{12,4},{4,0},{1,9},{9... | collective-permute-start | bytes 1671176 | tf_op jit(solution)/shard_map/ppermute | solution.py:195
  6.4 2.0 %collective-permute-start.9 = (bf16[352,1024]{1,0:T(8,128)(2,1)S(1)}, bf16[352,1024]{1,0:T(8,128)(2,1)S(1)}, u32[]{:S(2)}, u32[]{:S(2)}) collective-permute-start(bf16[352,1024]{1,0:T(8,128)(2,1)S(1)} %bitcast.11), channel_id=1, source_target_pairs={{2,0},{0,2},{3,1},{1,3},{6,4},{4,6},{7,5},{5,7},{10,8},{8,10},{11,... | collective-permute-start | bytes 2162696 | tf_op jit(solution)/shard_map/ppermute | solution.py:192
  8.5 1.9 %collective-permute-start.13 = (bf16[352,1024]{1,0:T(8,128)(2,1)}, bf16[352,1024]{1,0:T(8,128)(2,1)S(1)}, u32[]{:S(2)}, u32[]{:S(2)}) collective-permute-start(bf16[352,1024]{1,0:T(8,128)(2,1)} %bitcast.18), channel_id=1, source_target_pairs={{2,0},{0,2},{3,1},{1,3},{6,4},{4,6},{7,5},{5,7},{10,8},{8,10},{11,... | collective-permute-start | bytes 2162696 | tf_op jit(solution)/shard_map/ppermute | solution.py:192
  12.6 3.8 %shard_map.103 = (f32[128,1024]{1,0:T(8,128)S(1)}, f32[128,1024]{1,0:T(8,128)S(1)}, f32[128,128]{1,0:T(8,128)S(1)}) custom-call(s32[2]{0:T(128)S(1)} %broadcast_add_fusion.refs_0_, bf16[272,1024]{1,0:T(8,128)(2,1)S(1)} %pad_maximum_fusion.refs_1_, bf16[352,1024]{1,0:T(8,128)(2,1)S(1)} %bitcast.12, bf16[352,1024]{1,0:T(8,128)(2,1)S(1)} %bitcast.19, ...), custom_call_target="tpu_custom_call" | custom-call | flops 11072962560 | bytes 58982400 | tf_op jit(solution)/shard_map/pallas_call | solution.py:138
  16.5 3.0 %collective-permute-done.refs_2_ = bf16[272,1024]{1,0:T(8,128)(2,1)} collective-permute-done((bf16[272,1024]{1,0:T(8,128)(2,1)S(1)}, bf16[272,1024]{1,0:T(8,128)(2,1)}, u32[]{:S(2)}, u32[]{:S(2)}) %collective-permute-start) | collective-permute-done | bytes 557088 | tf_op jit(solution)/shard_map/ppermute | solution.py:195
  19.5 1.8 %collective-permute-start.4 = (bf16[272,1024]{1,0:T(8,128)(2,1)}, bf16[272,1024]{1,0:T(8,128)(2,1)S(1)}, u32[]{:S(2)}, u32[]{:S(2)}) collective-permute-start(bf16[272,1024]{1,0:T(8,128)(2,1)} %collective-permute-done.refs_2_), channel_id=1, source_target_pairs={{0,8},{8,16},{16,24},{24,28},{28,20},{20,12},{12,4},{4,0},{1,9},{9... | collective-permute-start | bytes 1671176 | tf_op jit(solution)/shard_map/ppermute | solution.py:195
  21.5 5.8 %shard_map.104 = (f32[256,1024]{1,0:T(8,128)S(1)}, f32[256,1024]{1,0:T(8,128)S(1)}, f32[256,128]{1,0:T(8,128)S(1)}) custom-call(s32[2]{0:T(128)S(1)} %broadcast_add_fusion.refs_0_, bf16[272,1024]{1,0:T(8,128)(2,1)} %collective-permute-done.5.refs_1_, bf16[272,1024]{1,0:T(8,128)(2,1)} %collective-permute-done.refs_2_, bf16[352,1024]{1,0:T(8,128)(2,1)S(1)} %bitcast.13, ...), custom_call_target="tpu_custom_call" | custom-call | flops 22145925120 | bytes 74711040 | tf_op jit(solution)/shard_map/pallas_call | solution.py:138
  27.4 6.7 %collective-permute-done.4.refs_2_ = bf16[272,1024]{1,0:T(8,128)(2,1)S(1)} collective-permute-done((bf16[272,1024]{1,0:T(8,128)(2,1)}, bf16[272,1024]{1,0:T(8,128)(2,1)S(1)}, u32[]{:S(2)}, u32[]{:S(2)}) %collective-permute-start.4) | collective-permute-done | bytes 557088 | tf_op jit(solution)/shard_map/ppermute | solution.py:195
  34.1 1.6 %collective-permute-start.6 = (bf16[272,1024]{1,0:T(8,128)(2,1)S(1)}, bf16[272,1024]{1,0:T(8,128)(2,1)S(1)}, u32[]{:S(2)}, u32[]{:S(2)}) collective-permute-start(bf16[272,1024]{1,0:T(8,128)(2,1)S(1)} %collective-permute-done.4.refs_2_), channel_id=1, source_target_pairs={{0,8},{8,16},{16,24},{24,28},{28,20},{20,12},{12,4},{4,0},{1,9},{9... | collective-permute-start | bytes 1671176 | tf_op jit(solution)/shard_map/ppermute | solution.py:195
  36.1 5.0 %shard_map.105 = (f32[256,1024]{1,0:T(8,128)S(1)}, f32[256,1024]{1,0:T(8,128)S(1)}, f32[256,128]{1,0:T(8,128)S(1)}) custom-call(s32[2]{0:T(128)S(1)} %broadcast_add_fusion.refs_0_, bf16[272,1024]{1,0:T(8,128)(2,1)S(1)} %collective-permute-done.7.refs_1_, bf16[272,1024]{1,0:T(8,128)(2,1)S(1)} %collective-permute-done.4.refs_2_, ...), custom_call_target="tpu_custom_call" | custom-call | flops 22145925120 | bytes 74711040 | tf_op jit(solution)/shard_map/pallas_call | solution.py:138
  41.1 6.5 %collective-permute-done.6.refs_2_ = bf16[272,1024]{1,0:T(8,128)(2,1)S(1)} collective-permute-done((bf16[272,1024]{1,0:T(8,128)(2,1)S(1)}, bf16[272,1024]{1,0:T(8,128)(2,1)S(1)}, u32[]{:S(2)}, u32[]{:S(2)}) %collective-permute-start.6) | collective-permute-done | bytes 557088 | tf_op jit(solution)/shard_map/ppermute | solution.py:195
  48.8 1.6 %collective-permute-start.11 = (bf16[144,1024]{1,0:T(8,128)(2,1)S(1)}, bf16[144,1024]{1,0:T(8,128)(2,1)S(1)}, u32[]{:S(2)}, u32[]{:S(2)}) collective-permute-start(bf16[144,1024]{1,0:T(8,128)(2,1)S(1)} %pad_maximum_fusion.1), channel_id=1, source_target_pairs={{0,8},{8,16},{16,24},{24,28},{28,20},{20,12},{12,4},{4,0},{1,9},{9... | collective-permute-start | bytes 884744 | tf_op jit(solution)/shard_map/ppermute | solution.py:195
  51.7 5.0 %shard_map.109 = (f32[256,1024]{1,0:T(8,128)S(1)}, f32[256,1024]{1,0:T(8,128)S(1)}, f32[256,128]{1,0:T(8,128)S(1)}) custom-call(s32[2]{0:T(128)S(1)} %broadcast_add_fusion.refs_0_, bf16[272,1024]{1,0:T(8,128)(2,1)S(1)} %collective-permute-done.8.refs_1_, bf16[272,1024]{1,0:T(8,128)(2,1)S(1)} %collective-permute-done.6.refs_2_, ...), custom_call_target="tpu_custom_call" | custom-call | flops 22145925120 | bytes 74711040 | tf_op jit(solution)/shard_map/pallas_call | solution.py:138
  57.2 2.1 %collective-permute-done.15.refs_6_.refs_7_.refs_12_ = bf16[352,1024]{1,0:T(8,128)(2,1)S(1)} collective-permute-done((bf16[352,1024]{1,0:T(8,128)(2,1)S(1)}, bf16[352,1024]{1,0:T(8,128)(2,1)S(1)}, u32[]{:S(2)}, u32[]{:S(2)}) %collective-permute-start.15) | collective-permute-done | bytes 720928 | tf_op jit(solution)/shard_map/ppermute | solution.py:192
  59.3 5.8 %shard_map.111 = f32[272,1024]{1,0:T(8,128)S(1)} custom-call(s32[2]{0:T(128)S(1)} %broadcast_add_fusion.refs_0_, bf16[272,1024]{1,0:T(8,128)(2,1)S(1)} %slice_dynamic-update-slice_fusion.4.refs_1_, bf16[352,1024]{1,0:T(8,128)(2,1)S(1)} %bitcast.16, bf16[352,1024]{1,0:T(8,128)(2,1)S(1)} %bitcast.23, bf16[352,1024]{1,0:T(8,128)(2,1)S(1)} %bitcast.30, ...), custom_call_target="tpu_custom_call" | custom-call | flops 22145925120 | bytes 102236160 | tf_op jit(solution)/shard_map/pallas_call | solution.py:138
  65.2 1.6 %collective-permute-start.17 = (bf16[144,1024]{1,0:T(8,128)(2,1)S(1)}, bf16[144,1024]{1,0:T(8,128)(2,1)S(1)}, u32[]{:S(2)}, u32[]{:S(2)}) collective-permute-start(bf16[144,1024]{1,0:T(8,128)(2,1)S(1)} %pad_maximum_fusion.2), channel_id=1, source_target_pairs={{0,8},{8,16},{16,24},{24,28},{28,20},{20,12},{12,4},{4,0},{1,9},{9... | collective-permute-start | bytes 884744 | tf_op jit(solution)/shard_map/ppermute | solution.py:195
  67.4 5.2 %shard_map.110 = f32[544,1024]{1,0:T(8,128)S(1)} custom-call(s32[2]{0:T(128)S(1)} %broadcast_add_fusion.refs_0_, bf16[272,1024]{1,0:T(8,128)(2,1)S(1)} %collective-permute-done.8.refs_1_, bf16[272,1024]{1,0:T(8,128)(2,1)S(1)} %collective-permute-done.6.refs_2_, bf16[352,1024]{1,0:T(8,128)(2,1)S(1)} %collective-permute-done.9.refs_2_.refs_3_.refs_8_, ...), custom_call_target="tpu_custom_call" | custom-call | flops 22145925120 | bytes 74711040 | tf_op jit(solution)/shard_map/pallas_call | solution.py:138
  72.8 2.2 %collective-permute-done.21 = bf16[128,1024]{1,0:T(8,128)(2,1)S(1)} collective-permute-done((bf16[128,1024]{1,0:T(8,128)(2,1)S(1)}, bf16[128,1024]{1,0:T(8,128)(2,1)S(1)}, u32[]{:S(2)}, u32[]{:S(2)}) %collective-permute-start.21) | collective-permute-done | bytes 262176 | tf_op jit(solution)/shard_map/ppermute | solution.py:195
  75.2 1.8 %collective-permute-start.18 = (bf16[128,1024]{1,0:T(8,128)(2,1)S(1)}, bf16[128,1024]{1,0:T(8,128)(2,1)S(1)}, u32[]{:S(2)}, u32[]{:S(2)}) collective-permute-start(bf16[128,1024]{1,0:T(8,128)(2,1)S(1)} %pad_maximum_fusion.6), channel_id=1, source_target_pairs={{0,8},{8,16},{16,24},{24,28},{28,20},{20,12},{12,4},{4,0},{1,9},{9... | collective-permute-start | bytes 786440 | tf_op jit(solution)/shard_map/ppermute | solution.py:195
  79.8 5.2 %shard_map.108 = f32[544,1024]{1,0:T(8,128)S(1)} custom-call(s32[2]{0:T(128)S(1)} %broadcast_add_fusion.refs_0_, bf16[272,1024]{1,0:T(8,128)(2,1)S(1)} %collective-permute-done.7.refs_1_, bf16[272,1024]{1,0:T(8,128)(2,1)S(1)} %collective-permute-done.4.refs_2_, bf16[352,1024]{1,0:T(8,128)(2,1)S(1)} %collective-permute-done.9.refs_2_.refs_3_.refs_8_, ...), custom_call_target="tpu_custom_call" | custom-call | flops 22145925120 | bytes 74711040 | tf_op jit(solution)/shard_map/pallas_call | solution.py:138
  88.6 2.5 %collective-permute-done.25 = bf16[144,1024]{1,0:T(8,128)(2,1)S(1)} collective-permute-done((bf16[144,1024]{1,0:T(8,128)(2,1)S(1)}, bf16[144,1024]{1,0:T(8,128)(2,1)S(1)}, u32[]{:S(2)}, u32[]{:S(2)}) %collective-permute-start.25) | collective-permute-done | bytes 294944 | tf_op jit(solution)/shard_map/ppermute | solution.py:195
  94.9 5.8 %shard_map.107 = f32[544,1024]{1,0:T(8,128)S(1)} custom-call(s32[2]{0:T(128)S(1)} %broadcast_add_fusion.refs_0_, bf16[272,1024]{1,0:T(8,128)(2,1)} %collective-permute-done.5.refs_1_, bf16[272,1024]{1,0:T(8,128)(2,1)} %collective-permute-done.refs_2_, bf16[352,1024]{1,0:T(8,128)(2,1)S(1)} %collective-permute-done.9.refs_2_.refs_3_.refs_8_, ...), custom_call_target="tpu_custom_call" | custom-call | flops 22145925120 | bytes 74711040 | tf_op jit(solution)/shard_map/pallas_call | solution.py:138
  106.9 4.0 %shard_map.106 = f32[272,1024]{1,0:T(8,128)S(1)} custom-call(s32[2]{0:T(128)S(1)} %broadcast_add_fusion.refs_0_, bf16[272,1024]{1,0:T(8,128)(2,1)S(1)} %pad_maximum_fusion.refs_1_, bf16[352,1024]{1,0:T(8,128)(2,1)S(1)} %collective-permute-done.9.refs_2_.refs_3_.refs_8_, bf16[352,1024]{1,0:T(8,128)(2,1)S(1)} %collective-permute-done.13.refs_3_.refs_4_.refs_9_, ...), custom_call_target="tpu_custom_call" | custom-call | flops 11072962560 | bytes 58982400 | tf_op jit(solution)/shard_map/pallas_call | solution.py:138
  111.7 2.5 %collective-permute-done.30 = bf16[144,1024]{1,0:T(8,128)(2,1)S(1)} collective-permute-done((bf16[144,1024]{1,0:T(8,128)(2,1)S(1)}, bf16[144,1024]{1,0:T(8,128)(2,1)S(1)}, u32[]{:S(2)}, u32[]{:S(2)}) %collective-permute-start.30) | collective-permute-done | bytes 294944 | tf_op jit(solution)/shard_map/ppermute | solution.py:195
  (102 shorter events, 28.5 us)
Async XLA Ops:
  3.5 16.0 %collective-permute-start = (bf16[272,1024]{1,0:T(8,128)(2,1)S(1)}, bf16[272,1024]{1,0:T(8,128)(2,1)}, u32[]{:S(2)}, u32[]{:S(2)}) collective-permute-start(bf16[272,1024]{1,0:T(8,128)(2,1)S(1)} %pad_maximum_fusion.refs_1_), channel_id=1, source_target_pairs={{0,8},{8,16},{16,24},{24,28},{28,20},{20,12},{12,4},{4,0},{1,9},{9... | collective-permute-start | bytes 1671176 | tf_op jit(solution)/shard_map/ppermute | solution.py:195
  6.2 15.1 %collective-permute-start.5 = (bf16[272,1024]{1,0:T(8,128)(2,1)S(1)}, bf16[272,1024]{1,0:T(8,128)(2,1)}, u32[]{:S(2)}, u32[]{:S(2)}) collective-permute-start(bf16[272,1024]{1,0:T(8,128)(2,1)S(1)} %pad_maximum_fusion.refs_1_), channel_id=1, source_target_pairs={{8,0},{16,8},{24,16},{28,24},{20,28},{12,20},{4,12},{0,4},{9,1},{1... | collective-permute-start | bytes 1671176 | tf_op jit(solution)/shard_map/ppermute | solution.py:195
  6.4 34.7 %collective-permute-start.9 = (bf16[352,1024]{1,0:T(8,128)(2,1)S(1)}, bf16[352,1024]{1,0:T(8,128)(2,1)S(1)}, u32[]{:S(2)}, u32[]{:S(2)}) collective-permute-start(bf16[352,1024]{1,0:T(8,128)(2,1)S(1)} %bitcast.11), channel_id=1, source_target_pairs={{2,0},{0,2},{3,1},{1,3},{6,4},{4,6},{7,5},{5,7},{10,8},{8,10},{11,... | collective-permute-start | bytes 2162696 | tf_op jit(solution)/shard_map/ppermute | solution.py:192
  8.4 32.7 %collective-permute-start.10 = (bf16[352,1024]{1,0:T(8,128)(2,1)}, bf16[352,1024]{1,0:T(8,128)(2,1)S(1)}, u32[]{:S(2)}, u32[]{:S(2)}) collective-permute-start(bf16[352,1024]{1,0:T(8,128)(2,1)} %bitcast.25), channel_id=1, source_target_pairs={{2,0},{0,2},{3,1},{1,3},{6,4},{4,6},{7,5},{5,7},{10,8},{8,10},{11,... | collective-permute-start | bytes 2162696 | tf_op jit(solution)/shard_map/ppermute | solution.py:192
  8.5 48.2 %collective-permute-start.13 = (bf16[352,1024]{1,0:T(8,128)(2,1)}, bf16[352,1024]{1,0:T(8,128)(2,1)S(1)}, u32[]{:S(2)}, u32[]{:S(2)}) collective-permute-start(bf16[352,1024]{1,0:T(8,128)(2,1)} %bitcast.18), channel_id=1, source_target_pairs={{2,0},{0,2},{3,1},{1,3},{6,4},{4,6},{7,5},{5,7},{10,8},{8,10},{11,... | collective-permute-start | bytes 2162696 | tf_op jit(solution)/shard_map/ppermute | solution.py:192
  19.5 14.6 %collective-permute-start.4 = (bf16[272,1024]{1,0:T(8,128)(2,1)}, bf16[272,1024]{1,0:T(8,128)(2,1)S(1)}, u32[]{:S(2)}, u32[]{:S(2)}) collective-permute-start(bf16[272,1024]{1,0:T(8,128)(2,1)} %collective-permute-done.refs_2_), channel_id=1, source_target_pairs={{0,8},{8,16},{16,24},{24,28},{28,20},{20,12},{12,4},{4,0},{1,9},{9... | collective-permute-start | bytes 1671176 | tf_op jit(solution)/shard_map/ppermute | solution.py:195
  21.3 14.4 %collective-permute-start.7 = (bf16[272,1024]{1,0:T(8,128)(2,1)}, bf16[272,1024]{1,0:T(8,128)(2,1)S(1)}, u32[]{:S(2)}, u32[]{:S(2)}) collective-permute-start(bf16[272,1024]{1,0:T(8,128)(2,1)} %collective-permute-done.5.refs_1_), channel_id=1, source_target_pairs={{8,0},{16,8},{24,16},{28,24},{20,28},{12,20},{4,12},{0,4},{9,1},{1... | collective-permute-start | bytes 1671176 | tf_op jit(solution)/shard_map/ppermute | solution.py:195
  34.1 13.5 %collective-permute-start.6 = (bf16[272,1024]{1,0:T(8,128)(2,1)S(1)}, bf16[272,1024]{1,0:T(8,128)(2,1)S(1)}, u32[]{:S(2)}, u32[]{:S(2)}) collective-permute-start(bf16[272,1024]{1,0:T(8,128)(2,1)S(1)} %collective-permute-done.4.refs_2_), channel_id=1, source_target_pairs={{0,8},{8,16},{16,24},{24,28},{28,20},{20,12},{12,4},{4,0},{1,9},{9... | collective-permute-start | bytes 1671176 | tf_op jit(solution)/shard_map/ppermute | solution.py:195
  35.7 13.0 %collective-permute-start.8 = (bf16[272,1024]{1,0:T(8,128)(2,1)S(1)}, bf16[272,1024]{1,0:T(8,128)(2,1)S(1)}, u32[]{:S(2)}, u32[]{:S(2)}) collective-permute-start(bf16[272,1024]{1,0:T(8,128)(2,1)S(1)} %collective-permute-done.7.refs_1_), channel_id=1, source_target_pairs={{8,0},{16,8},{24,16},{28,24},{20,28},{12,20},{4,12},{0,4},{9,1},{1... | collective-permute-start | bytes 1671176 | tf_op jit(solution)/shard_map/ppermute | solution.py:195
  48.8 8.3 %collective-permute-start.11 = (bf16[144,1024]{1,0:T(8,128)(2,1)S(1)}, bf16[144,1024]{1,0:T(8,128)(2,1)S(1)}, u32[]{:S(2)}, u32[]{:S(2)}) collective-permute-start(bf16[144,1024]{1,0:T(8,128)(2,1)S(1)} %pad_maximum_fusion.1), channel_id=1, source_target_pairs={{0,8},{8,16},{16,24},{24,28},{28,20},{20,12},{12,4},{4,0},{1,9},{9... | collective-permute-start | bytes 884744 | tf_op jit(solution)/shard_map/ppermute | solution.py:195
  65.2 9.8 %collective-permute-start.17 = (bf16[144,1024]{1,0:T(8,128)(2,1)S(1)}, bf16[144,1024]{1,0:T(8,128)(2,1)S(1)}, u32[]{:S(2)}, u32[]{:S(2)}) collective-permute-start(bf16[144,1024]{1,0:T(8,128)(2,1)S(1)} %pad_maximum_fusion.2), channel_id=1, source_target_pairs={{0,8},{8,16},{16,24},{24,28},{28,20},{20,12},{12,4},{4,0},{1,9},{9... | collective-permute-start | bytes 884744 | tf_op jit(solution)/shard_map/ppermute | solution.py:195
  66.9 8.1 %collective-permute-start.21 = (bf16[128,1024]{1,0:T(8,128)(2,1)S(1)}, bf16[128,1024]{1,0:T(8,128)(2,1)S(1)}, u32[]{:S(2)}, u32[]{:S(2)}) collective-permute-start(bf16[128,1024]{1,0:T(8,128)(2,1)S(1)} %pad_maximum_fusion.7), channel_id=1, source_target_pairs={{8,0},{16,8},{24,16},{28,24},{20,28},{12,20},{4,12},{0,4},{9,1},{1... | collective-permute-start | bytes 786440 | tf_op jit(solution)/shard_map/ppermute | solution.py:195
  75.2 9.8 %collective-permute-start.18 = (bf16[128,1024]{1,0:T(8,128)(2,1)S(1)}, bf16[128,1024]{1,0:T(8,128)(2,1)S(1)}, u32[]{:S(2)}, u32[]{:S(2)}) collective-permute-start(bf16[128,1024]{1,0:T(8,128)(2,1)S(1)} %pad_maximum_fusion.6), channel_id=1, source_target_pairs={{0,8},{8,16},{16,24},{24,28},{28,20},{20,12},{12,4},{4,0},{1,9},{9... | collective-permute-start | bytes 786440 | tf_op jit(solution)/shard_map/ppermute | solution.py:195
  77.0 9.3 %collective-permute-start.22 = (bf16[128,1024]{1,0:T(8,128)(2,1)S(1)}, bf16[128,1024]{1,0:T(8,128)(2,1)S(1)}, u32[]{:S(2)}, u32[]{:S(2)}) collective-permute-start(bf16[128,1024]{1,0:T(8,128)(2,1)S(1)} %pad_maximum_fusion.8), channel_id=1, source_target_pairs={{8,0},{16,8},{24,16},{28,24},{20,28},{12,20},{4,12},{0,4},{9,1},{1... | collective-permute-start | bytes 786440 | tf_op jit(solution)/shard_map/ppermute | solution.py:195
  77.6 13.4 %collective-permute-start.25 = (bf16[144,1024]{1,0:T(8,128)(2,1)S(1)}, bf16[144,1024]{1,0:T(8,128)(2,1)S(1)}, u32[]{:S(2)}, u32[]{:S(2)}) collective-permute-start(bf16[144,1024]{1,0:T(8,128)(2,1)S(1)} %pad_maximum_fusion.3), channel_id=1, source_target_pairs={{0,8},{8,16},{16,24},{24,28},{28,20},{20,12},{12,4},{4,0},{1,9},{9... | collective-permute-start | bytes 884744 | tf_op jit(solution)/shard_map/ppermute | solution.py:195
  79.2 13.4 %collective-permute-start.28 = (bf16[144,1024]{1,0:T(8,128)(2,1)S(1)}, bf16[144,1024]{1,0:T(8,128)(2,1)S(1)}, u32[]{:S(2)}, u32[]{:S(2)}) collective-permute-start(bf16[144,1024]{1,0:T(8,128)(2,1)S(1)} %pad_maximum_fusion.4), channel_id=1, source_target_pairs={{8,0},{16,8},{24,16},{28,24},{20,28},{12,20},{4,12},{0,4},{9,1},{1... | collective-permute-start | bytes 884744 | tf_op jit(solution)/shard_map/ppermute | solution.py:195
  86.5 14.2 %collective-permute-start.19 = (bf16[128,1024]{1,0:T(8,128)(2,1)S(1)}, bf16[128,1024]{1,0:T(8,128)(2,1)S(1)}, u32[]{:S(2)}, u32[]{:S(2)}) collective-permute-start(bf16[128,1024]{1,0:T(8,128)(2,1)S(1)} %get-tuple-element.73), channel_id=1, source_target_pairs={{0,8},{8,16},{16,24},{24,28},{28,20},{20,12},{12,4},{4,0},{1,9},{9... | collective-permute-start | bytes 786440 | tf_op jit(solution)/shard_map/ppermute | solution.py:195
  87.8 12.9 %collective-permute-start.23 = (bf16[128,1024]{1,0:T(8,128)(2,1)S(1)}, bf16[128,1024]{1,0:T(8,128)(2,1)S(1)}, u32[]{:S(2)}, u32[]{:S(2)}) collective-permute-start(bf16[128,1024]{1,0:T(8,128)(2,1)S(1)} %get-tuple-element.74), channel_id=1, source_target_pairs={{8,0},{16,8},{24,16},{28,24},{20,28},{12,20},{4,12},{0,4},{9,1},{1... | collective-permute-start | bytes 786440 | tf_op jit(solution)/shard_map/ppermute | solution.py:195
  92.8 10.2 %collective-permute-start.26 = (bf16[144,1024]{1,0:T(8,128)(2,1)S(1)}, bf16[144,1024]{1,0:T(8,128)(2,1)S(1)}, u32[]{:S(2)}, u32[]{:S(2)}) collective-permute-start(bf16[144,1024]{1,0:T(8,128)(2,1)S(1)} %get-tuple-element.67), channel_id=1, source_target_pairs={{0,8},{8,16},{16,24},{24,28},{28,20},{20,12},{12,4},{4,0},{1,9},{9... | collective-permute-start | bytes 884744 | tf_op jit(solution)/shard_map/ppermute | solution.py:195
  94.1 10.5 %collective-permute-start.29 = (bf16[144,1024]{1,0:T(8,128)(2,1)S(1)}, bf16[144,1024]{1,0:T(8,128)(2,1)S(1)}, u32[]{:S(2)}, u32[]{:S(2)}) collective-permute-start(bf16[144,1024]{1,0:T(8,128)(2,1)S(1)} %get-tuple-element.68), channel_id=1, source_target_pairs={{8,0},{16,8},{24,16},{28,24},{20,28},{12,20},{4,12},{0,4},{9,1},{1... | collective-permute-start | bytes 884744 | tf_op jit(solution)/shard_map/ppermute | solution.py:195
  100.9 10.0 %collective-permute-start.24 = (bf16[128,1024]{1,0:T(8,128)(2,1)S(1)}, bf16[128,1024]{1,0:T(8,128)(2,1)S(1)}, u32[]{:S(2)}, u32[]{:S(2)}) collective-permute-start(bf16[128,1024]{1,0:T(8,128)(2,1)S(1)} %get-tuple-element.72), channel_id=1, source_target_pairs={{8,0},{16,8},{24,16},{28,24},{20,28},{12,20},{4,12},{0,4},{9,1},{1... | collective-permute-start | bytes 786440 | tf_op jit(solution)/shard_map/ppermute | solution.py:195
  101.4 9.4 %collective-permute-start.20 = (bf16[128,1024]{1,0:T(8,128)(2,1)S(1)}, bf16[128,1024]{1,0:T(8,128)(2,1)S(1)}, u32[]{:S(2)}, u32[]{:S(2)}) collective-permute-start(bf16[128,1024]{1,0:T(8,128)(2,1)S(1)} %get-tuple-element.71), channel_id=1, source_target_pairs={{0,8},{8,16},{16,24},{24,28},{28,20},{20,12},{12,4},{4,0},{1,9},{9... | collective-permute-start | bytes 786440 | tf_op jit(solution)/shard_map/ppermute | solution.py:195
  104.8 9.4 %collective-permute-start.30 = (bf16[144,1024]{1,0:T(8,128)(2,1)S(1)}, bf16[144,1024]{1,0:T(8,128)(2,1)S(1)}, u32[]{:S(2)}, u32[]{:S(2)}) collective-permute-start(bf16[144,1024]{1,0:T(8,128)(2,1)S(1)} %get-tuple-element.66), channel_id=1, source_target_pairs={{8,0},{16,8},{24,16},{28,24},{20,28},{12,20},{4,12},{0,4},{9,1},{1... | collective-permute-start | bytes 884744 | tf_op jit(solution)/shard_map/ppermute | solution.py:195
  105.3 8.9 %collective-permute-start.27 = (bf16[144,1024]{1,0:T(8,128)(2,1)S(1)}, bf16[144,1024]{1,0:T(8,128)(2,1)S(1)}, u32[]{:S(2)}, u32[]{:S(2)}) collective-permute-start(bf16[144,1024]{1,0:T(8,128)(2,1)S(1)} %get-tuple-element.65), channel_id=1, source_target_pairs={{0,8},{8,16},{16,24},{24,28},{28,20},{20,12},{12,4},{4,0},{1,9},{9... | collective-permute-start | bytes 884744 | tf_op jit(solution)/shard_map/ppermute | solution.py:195
  (14 other events, 64.4 us)

commit v6 on v5

--- a/solution.py
+++ b/solution.py
@@ -248,13 +248,12 @@
         arrived[-s], arrived[s] = around(ahead, fw), around(behind, bw)
     if few and reach > 1:
         done[reach - 1] = work(reach - 1, first, False)
-    tied = lax.optimization_barrier((arrived[-reach], arrived[reach], [(w[0], w[2]) for w in shares]))
-    arrived[-reach], arrived[reach], early = tied
+    arrived[-reach], early = lax.optimization_barrier((arrived[-reach], [(w[0], w[2]) for w in shares]))
     late = [w[1] for w in shares]
     if even:
         ahead, behind = after(arrived[1 - far], *last), after(arrived[far - 1], *last)
         top, low = around(top_half(ahead), fw), around(low_half(behind), bw)
-        top, low, late = lax.optimization_barrier((top, low, late))
+        top, late = lax.optimization_barrier((top, late))
         arrived[far] = jnp.concatenate([top[:half], low[:half], top[half:tokens], low[half:], top[tokens:]])
     rest = []
     for k, ((gate, down), up) in enumerate(zip(early, late)):

time: 116 us -> 114 us (0.983)
  waiting for transfers between devices: 31.6 us -> 29.8 us
    ppermute x9, waiting for transfers between devices: 2.11 us -> 0.04 us  [shifted(): return lax.ppermute(a, axis, [((i + by) % size, i) for i in range(size)])]
  transfers between devices with their start and end apart: 31 -> 31, of which waited for: 12 -> 10; matrix products, arithmetic and copies ran while one was open for 3% -> 3% of each run, Pallas kernels for 34% -> 35%
where the time goes in v6:
time: 114 us
  Pallas kernels  45.6 us (40%)
  waiting for transfers between devices  29.8 us (26%)
  starting transfers between devices  29.6 us (26%)
  other arithmetic  4.69 us (4%)
  local copies, waits for them, and re-layouts  3.2 us (3%)
    pallas_call x9, Pallas kernels, experts_part(): pl.pallas_call(functools.partial(part_kernel, layout, len(flat), len(bloc...  45.6 us
    ppermute x22, waiting for transfers between devices, around(): return lax.ppermute(a, 'expert', way)  29.8 us
    ppermute x22, starting transfers between devices, around(): return lax.ppermute(a, 'expert', way)  24 us
    ppermute x9, starting transfers between devices, shifted(): return lax.ppermute(a, axis, [((i + by) % size, i) for i in range(size)])  5.63 us
    unnamed x16, local copies, waits for them, and re-layouts  2.31 us
  transfers between devices with their start and end apart: 31, of which 10 were waited for; matrix products, arithmetic and copies ran while one was open for 3% of the time, Pallas kernels for 35%

profile of v6, /device:TPU:0, one launch (start us, length us, event | category | flops | bytes accessed | tf_op | source)
XLA Modules:
  0.0 114.0 jit_solution(16341334809387962702)
XLA Ops:
  3.5 2.7 %collective-permute-start = (bf16[272,1024]{1,0:T(8,128)(2,1)S(1)}, bf16[272,1024]{1,0:T(8,128)(2,1)}, u32[]{:S(2)}, u32[]{:S(2)}) collective-permute-start(bf16[272,1024]{1,0:T(8,128)(2,1)S(1)} %pad_maximum_fusion.refs_1_), channel_id=1, source_target_pairs={{0,8},{8,16},{16,24},{24,28},{28,20},{20,12},{12,4},{4,0},{1,9},{9... | collective-permute-start | bytes 1671176 | tf_op jit(solution)/shard_map/ppermute | solution.py:195
  6.4 2.0 %collective-permute-start.7 = (bf16[352,1024]{1,0:T(8,128)(2,1)S(1)}, bf16[352,1024]{1,0:T(8,128)(2,1)S(1)}, u32[]{:S(2)}, u32[]{:S(2)}) collective-permute-start(bf16[352,1024]{1,0:T(8,128)(2,1)S(1)} %bitcast.11), channel_id=1, source_target_pairs={{2,0},{0,2},{3,1},{1,3},{6,4},{4,6},{7,5},{5,7},{10,8},{8,10},{11,... | collective-permute-start | bytes 2162696 | tf_op jit(solution)/shard_map/ppermute | solution.py:192
  8.5 1.9 %collective-permute-start.11 = (bf16[352,1024]{1,0:T(8,128)(2,1)}, bf16[352,1024]{1,0:T(8,128)(2,1)S(1)}, u32[]{:S(2)}, u32[]{:S(2)}) collective-permute-start(bf16[352,1024]{1,0:T(8,128)(2,1)} %bitcast.18), channel_id=1, source_target_pairs={{2,0},{0,2},{3,1},{1,3},{6,4},{4,6},{7,5},{5,7},{10,8},{8,10},{11,... | collective-permute-start | bytes 2162696 | tf_op jit(solution)/shard_map/ppermute | solution.py:192
  12.6 3.8 %shard_map.103 = (f32[128,1024]{1,0:T(8,128)S(1)}, f32[128,1024]{1,0:T(8,128)S(1)}, f32[128,128]{1,0:T(8,128)S(1)}) custom-call(s32[2]{0:T(128)S(1)} %broadcast_add_fusion.refs_0_, bf16[272,1024]{1,0:T(8,128)(2,1)S(1)} %pad_maximum_fusion.refs_1_, bf16[352,1024]{1,0:T(8,128)(2,1)S(1)} %bitcast.12, bf16[352,1024]{1,0:T(8,128)(2,1)S(1)} %bitcast.19, ...), custom_call_target="tpu_custom_call" | custom-call | flops 11072962560 | bytes 58982400 | tf_op jit(solution)/shard_map/pallas_call | solution.py:138
  16.5 3.0 %collective-permute-done.refs_2_ = bf16[272,1024]{1,0:T(8,128)(2,1)} collective-permute-done((bf16[272,1024]{1,0:T(8,128)(2,1)S(1)}, bf16[272,1024]{1,0:T(8,128)(2,1)}, u32[]{:S(2)}, u32[]{:S(2)}) %collective-permute-start) | collective-permute-done | bytes 557088 | tf_op jit(solution)/shard_map/ppermute | solution.py:195
  19.5 1.8 %collective-permute-start.4 = (bf16[272,1024]{1,0:T(8,128)(2,1)}, bf16[272,1024]{1,0:T(8,128)(2,1)S(1)}, u32[]{:S(2)}, u32[]{:S(2)}) collective-permute-start(bf16[272,1024]{1,0:T(8,128)(2,1)} %collective-permute-done.refs_2_), channel_id=1, source_target_pairs={{0,8},{8,16},{16,24},{24,28},{28,20},{20,12},{12,4},{4,0},{1,9},{9... | collective-permute-start | bytes 1671176 | tf_op jit(solution)/shard_map/ppermute | solution.py:195
  21.5 5.8 %shard_map.104 = (f32[256,1024]{1,0:T(8,128)S(1)}, f32[256,1024]{1,0:T(8,128)S(1)}, f32[256,128]{1,0:T(8,128)S(1)}) custom-call(s32[2]{0:T(128)S(1)} %broadcast_add_fusion.refs_0_, bf16[272,1024]{1,0:T(8,128)(2,1)} %collective-permute-done.5.refs_1_, bf16[272,1024]{1,0:T(8,128)(2,1)} %collective-permute-done.refs_2_, bf16[352,1024]{1,0:T(8,128)(2,1)S(1)} %bitcast.13, ...), custom_call_target="tpu_custom_call" | custom-call | flops 22145925120 | bytes 74711040 | tf_op jit(solution)/shard_map/pallas_call | solution.py:138
  27.4 6.7 %collective-permute-done.4.refs_2_ = bf16[272,1024]{1,0:T(8,128)(2,1)S(1)} collective-permute-done((bf16[272,1024]{1,0:T(8,128)(2,1)}, bf16[272,1024]{1,0:T(8,128)(2,1)S(1)}, u32[]{:S(2)}, u32[]{:S(2)}) %collective-permute-start.4) | collective-permute-done | bytes 557088 | tf_op jit(solution)/shard_map/ppermute | solution.py:195
  36.1 5.0 %shard_map.105 = (f32[256,1024]{1,0:T(8,128)S(1)}, f32[256,1024]{1,0:T(8,128)S(1)}, f32[256,128]{1,0:T(8,128)S(1)}) custom-call(s32[2]{0:T(128)S(1)} %broadcast_add_fusion.refs_0_, bf16[272,1024]{1,0:T(8,128)(2,1)S(1)} %collective-permute-done.9.refs_1_, bf16[272,1024]{1,0:T(8,128)(2,1)S(1)} %collective-permute-done.4.refs_2_, ...), custom_call_target="tpu_custom_call" | custom-call | flops 22145925120 | bytes 74711040 | tf_op jit(solution)/shard_map/pallas_call | solution.py:138
  41.1 6.5 %collective-permute-done.6.refs_2_ = bf16[272,1024]{1,0:T(8,128)(2,1)S(1)} collective-permute-done((bf16[272,1024]{1,0:T(8,128)(2,1)S(1)}, bf16[272,1024]{1,0:T(8,128)(2,1)S(1)}, u32[]{:S(2)}, u32[]{:S(2)}) %collective-permute-start.6) | collective-permute-done | bytes 557088 | tf_op jit(solution)/shard_map/ppermute | solution.py:195
  50.5 5.0 %shard_map.109 = (f32[256,1024]{1,0:T(8,128)S(1)}, f32[256,1024]{1,0:T(8,128)S(1)}, f32[256,128]{1,0:T(8,128)S(1)}) custom-call(s32[2]{0:T(128)S(1)} %broadcast_add_fusion.refs_0_, bf16[272,1024]{1,0:T(8,128)(2,1)S(1)} %collective-permute-done.15.refs_1_, bf16[272,1024]{1,0:T(8,128)(2,1)S(1)} %collective-permute-done.6.refs_2_, ...), custom_call_target="tpu_custom_call" | custom-call | flops 22145925120 | bytes 74711040 | tf_op jit(solution)/shard_map/pallas_call | solution.py:138
  55.6 2.5 %collective-permute-done.16 = bf16[128,1024]{1,0:T(8,128)(2,1)S(1)} collective-permute-done((bf16[128,1024]{1,0:T(8,128)(2,1)S(1)}, bf16[128,1024]{1,0:T(8,128)(2,1)S(1)}, u32[]{:S(2)}, u32[]{:S(2)}) %collective-permute-start.16) | collective-permute-done | bytes 262176 | tf_op jit(solution)/shard_map/ppermute | solution.py:195
  58.2 5.8 %shard_map.111 = f32[272,1024]{1,0:T(8,128)S(1)} custom-call(s32[2]{0:T(128)S(1)} %broadcast_add_fusion.refs_0_, bf16[272,1024]{1,0:T(8,128)(2,1)S(1)} %slice_dynamic-update-slice_fusion.4.refs_1_, bf16[352,1024]{1,0:T(8,128)(2,1)S(1)} %bitcast.16, bf16[352,1024]{1,0:T(8,128)(2,1)S(1)} %bitcast.23, bf16[352,1024]{1,0:T(8,128)(2,1)S(1)} %bitcast.30, ...), custom_call_target="tpu_custom_call" | custom-call | flops 22145925120 | bytes 102236160 | tf_op jit(solution)/shard_map/pallas_call | solution.py:138
  66.4 5.2 %shard_map.110 = f32[544,1024]{1,0:T(8,128)S(1)} custom-call(s32[2]{0:T(128)S(1)} %broadcast_add_fusion.refs_0_, bf16[272,1024]{1,0:T(8,128)(2,1)S(1)} %collective-permute-done.15.refs_1_, bf16[272,1024]{1,0:T(8,128)(2,1)S(1)} %collective-permute-done.6.refs_2_, bf16[352,1024]{1,0:T(8,128)(2,1)S(1)} %collective-permute-done.7.refs_2_.refs_3_.refs_8_, ...), custom_call_target="tpu_custom_call" | custom-call | flops 22145925120 | bytes 74711040 | tf_op jit(solution)/shard_map/pallas_call | solution.py:138
  71.8 1.8 %collective-permute-done.21 = bf16[128,1024]{1,0:T(8,128)(2,1)S(1)} collective-permute-done((bf16[128,1024]{1,0:T(8,128)(2,1)S(1)}, bf16[128,1024]{1,0:T(8,128)(2,1)S(1)}, u32[]{:S(2)}, u32[]{:S(2)}) %collective-permute-start.21) | collective-permute-done | bytes 262176 | tf_op jit(solution)/shard_map/ppermute | solution.py:195
  73.8 1.6 %collective-permute-start.18 = (bf16[128,1024]{1,0:T(8,128)(2,1)S(1)}, bf16[128,1024]{1,0:T(8,128)(2,1)S(1)}, u32[]{:S(2)}, u32[]{:S(2)}) collective-permute-start(bf16[128,1024]{1,0:T(8,128)(2,1)S(1)} %pad_maximum_fusion.6), channel_id=1, source_target_pairs={{0,8},{8,16},{16,24},{24,28},{28,20},{20,12},{12,4},{4,0},{1,9},{9... | collective-permute-start | bytes 786440 | tf_op jit(solution)/shard_map/ppermute | solution.py:195
  78.4 5.2 %shard_map.108 = f32[544,1024]{1,0:T(8,128)S(1)} custom-call(s32[2]{0:T(128)S(1)} %broadcast_add_fusion.refs_0_, bf16[272,1024]{1,0:T(8,128)(2,1)S(1)} %collective-permute-done.9.refs_1_, bf16[272,1024]{1,0:T(8,128)(2,1)S(1)} %collective-permute-done.4.refs_2_, bf16[352,1024]{1,0:T(8,128)(2,1)S(1)} %collective-permute-done.7.refs_2_.refs_3_.refs_8_, ...), custom_call_target="tpu_custom_call" | custom-call | flops 22145925120 | bytes 74711040 | tf_op jit(solution)/shard_map/pallas_call | solution.py:138
  85.2 1.6 %collective-permute-start.19 = (bf16[128,1024]{1,0:T(8,128)(2,1)S(1)}, bf16[128,1024]{1,0:T(8,128)(2,1)S(1)}, u32[]{:S(2)}, u32[]{:S(2)}) collective-permute-start(bf16[128,1024]{1,0:T(8,128)(2,1)S(1)} %get-tuple-element.69), channel_id=1, source_target_pairs={{0,8},{8,16},{16,24},{24,28},{28,20},{20,12},{12,4},{4,0},{1,9},{9... | collective-permute-start | bytes 786440 | tf_op jit(solution)/shard_map/ppermute | solution.py:195
  87.3 2.2 %collective-permute-done.25 = bf16[144,1024]{1,0:T(8,128)(2,1)S(1)} collective-permute-done((bf16[144,1024]{1,0:T(8,128)(2,1)S(1)}, bf16[144,1024]{1,0:T(8,128)(2,1)S(1)}, u32[]{:S(2)}, u32[]{:S(2)}) %collective-permute-start.25) | collective-permute-done | bytes 294944 | tf_op jit(solution)/shard_map/ppermute | solution.py:195
  89.5 1.9 %collective-permute-done.28 = bf16[144,1024]{1,0:T(8,128)(2,1)S(1)} collective-permute-done((bf16[144,1024]{1,0:T(8,128)(2,1)S(1)}, bf16[144,1024]{1,0:T(8,128)(2,1)S(1)}, u32[]{:S(2)}, u32[]{:S(2)}) %collective-permute-start.28) | collective-permute-done | bytes 294944 | tf_op jit(solution)/shard_map/ppermute | solution.py:195
  91.5 1.6 %collective-permute-start.26 = (bf16[144,1024]{1,0:T(8,128)(2,1)S(1)}, bf16[144,1024]{1,0:T(8,128)(2,1)S(1)}, u32[]{:S(2)}, u32[]{:S(2)}) collective-permute-start(bf16[144,1024]{1,0:T(8,128)(2,1)S(1)} %get-tuple-element.63), channel_id=1, source_target_pairs={{0,8},{8,16},{16,24},{24,28},{28,20},{20,12},{12,4},{4,0},{1,9},{9... | collective-permute-start | bytes 884744 | tf_op jit(solution)/shard_map/ppermute | solution.py:195
  93.6 5.8 %shard_map.107 = f32[544,1024]{1,0:T(8,128)S(1)} custom-call(s32[2]{0:T(128)S(1)} %broadcast_add_fusion.refs_0_, bf16[272,1024]{1,0:T(8,128)(2,1)} %collective-permute-done.5.refs_1_, bf16[272,1024]{1,0:T(8,128)(2,1)} %collective-permute-done.refs_2_, bf16[352,1024]{1,0:T(8,128)(2,1)S(1)} %collective-permute-done.7.refs_2_.refs_3_.refs_8_, ...), custom_call_target="tpu_custom_call" | custom-call | flops 22145925120 | bytes 74711040 | tf_op jit(solution)/shard_map/pallas_call | solution.py:138
  105.5 4.0 %shard_map.106 = f32[272,1024]{1,0:T(8,128)S(1)} custom-call(s32[2]{0:T(128)S(1)} %broadcast_add_fusion.refs_0_, bf16[272,1024]{1,0:T(8,128)(2,1)S(1)} %pad_maximum_fusion.refs_1_, bf16[352,1024]{1,0:T(8,128)(2,1)S(1)} %collective-permute-done.7.refs_2_.refs_3_.refs_8_, bf16[352,1024]{1,0:T(8,128)(2,1)S(1)} %collective-permute-done.11.refs_3_.refs_4_.refs_9_, ...), custom_call_target="tpu_custom_call" | custom-call | flops 11072962560 | bytes 58982400 | tf_op jit(solution)/shard_map/pallas_call | solution.py:138
  110.4 2.1 %collective-permute-done.30 = bf16[144,1024]{1,0:T(8,128)(2,1)S(1)} collective-permute-done((bf16[144,1024]{1,0:T(8,128)(2,1)S(1)}, bf16[144,1024]{1,0:T(8,128)(2,1)S(1)}, u32[]{:S(2)}, u32[]{:S(2)}) %collective-permute-start.30) | collective-permute-done | bytes 294944 | tf_op jit(solution)/shard_map/ppermute | solution.py:195
  (102 shorter events, 27.2 us)
Async XLA Ops:
  3.5 16.0 %collective-permute-start = (bf16[272,1024]{1,0:T(8,128)(2,1)S(1)}, bf16[272,1024]{1,0:T(8,128)(2,1)}, u32[]{:S(2)}, u32[]{:S(2)}) collective-permute-start(bf16[272,1024]{1,0:T(8,128)(2,1)S(1)} %pad_maximum_fusion.refs_1_), channel_id=1, source_target_pairs={{0,8},{8,16},{16,24},{24,28},{28,20},{20,12},{12,4},{4,0},{1,9},{9... | collective-permute-start | bytes 1671176 | tf_op jit(solution)/shard_map/ppermute | solution.py:195
  6.2 15.1 %collective-permute-start.5 = (bf16[272,1024]{1,0:T(8,128)(2,1)S(1)}, bf16[272,1024]{1,0:T(8,128)(2,1)}, u32[]{:S(2)}, u32[]{:S(2)}) collective-permute-start(bf16[272,1024]{1,0:T(8,128)(2,1)S(1)} %pad_maximum_fusion.refs_1_), channel_id=1, source_target_pairs={{8,0},{16,8},{24,16},{28,24},{20,28},{12,20},{4,12},{0,4},{9,1},{1... | collective-permute-start | bytes 1671176 | tf_op jit(solution)/shard_map/ppermute | solution.py:195
  6.4 34.7 %collective-permute-start.7 = (bf16[352,1024]{1,0:T(8,128)(2,1)S(1)}, bf16[352,1024]{1,0:T(8,128)(2,1)S(1)}, u32[]{:S(2)}, u32[]{:S(2)}) collective-permute-start(bf16[352,1024]{1,0:T(8,128)(2,1)S(1)} %bitcast.11), channel_id=1, source_target_pairs={{2,0},{0,2},{3,1},{1,3},{6,4},{4,6},{7,5},{5,7},{10,8},{8,10},{11,... | collective-permute-start | bytes 2162696 | tf_op jit(solution)/shard_map/ppermute | solution.py:192
  8.4 32.7 %collective-permute-start.8 = (bf16[352,1024]{1,0:T(8,128)(2,1)}, bf16[352,1024]{1,0:T(8,128)(2,1)S(1)}, u32[]{:S(2)}, u32[]{:S(2)}) collective-permute-start(bf16[352,1024]{1,0:T(8,128)(2,1)} %bitcast.25), channel_id=1, source_target_pairs={{2,0},{0,2},{3,1},{1,3},{6,4},{4,6},{7,5},{5,7},{10,8},{8,10},{11,... | collective-permute-start | bytes 2162696 | tf_op jit(solution)/shard_map/ppermute | solution.py:192
  8.5 47.1 %collective-permute-start.11 = (bf16[352,1024]{1,0:T(8,128)(2,1)}, bf16[352,1024]{1,0:T(8,128)(2,1)S(1)}, u32[]{:S(2)}, u32[]{:S(2)}) collective-permute-start(bf16[352,1024]{1,0:T(8,128)(2,1)} %bitcast.18), channel_id=1, source_target_pairs={{2,0},{0,2},{3,1},{1,3},{6,4},{4,6},{7,5},{5,7},{10,8},{8,10},{11,... | collective-permute-start | bytes 2162696 | tf_op jit(solution)/shard_map/ppermute | solution.py:192
  19.5 14.6 %collective-permute-start.4 = (bf16[272,1024]{1,0:T(8,128)(2,1)}, bf16[272,1024]{1,0:T(8,128)(2,1)S(1)}, u32[]{:S(2)}, u32[]{:S(2)}) collective-permute-start(bf16[272,1024]{1,0:T(8,128)(2,1)} %collective-permute-done.refs_2_), channel_id=1, source_target_pairs={{0,8},{8,16},{16,24},{24,28},{28,20},{20,12},{12,4},{4,0},{1,9},{9... | collective-permute-start | bytes 1671176 | tf_op jit(solution)/shard_map/ppermute | solution.py:195
  21.3 14.4 %collective-permute-start.9 = (bf16[272,1024]{1,0:T(8,128)(2,1)}, bf16[272,1024]{1,0:T(8,128)(2,1)S(1)}, u32[]{:S(2)}, u32[]{:S(2)}) collective-permute-start(bf16[272,1024]{1,0:T(8,128)(2,1)} %collective-permute-done.5.refs_1_), channel_id=1, source_target_pairs={{8,0},{16,8},{24,16},{28,24},{20,28},{12,20},{4,12},{0,4},{9,1},{1... | collective-permute-start | bytes 1671176 | tf_op jit(solution)/shard_map/ppermute | solution.py:195
  34.1 13.5 %collective-permute-start.6 = (bf16[272,1024]{1,0:T(8,128)(2,1)S(1)}, bf16[272,1024]{1,0:T(8,128)(2,1)S(1)}, u32[]{:S(2)}, u32[]{:S(2)}) collective-permute-start(bf16[272,1024]{1,0:T(8,128)(2,1)S(1)} %collective-permute-done.4.refs_2_), channel_id=1, source_target_pairs={{0,8},{8,16},{16,24},{24,28},{28,20},{20,12},{12,4},{4,0},{1,9},{9... | collective-permute-start | bytes 1671176 | tf_op jit(solution)/shard_map/ppermute | solution.py:195
  35.7 13.9 %collective-permute-start.15 = (bf16[272,1024]{1,0:T(8,128)(2,1)S(1)}, bf16[272,1024]{1,0:T(8,128)(2,1)S(1)}, u32[]{:S(2)}, u32[]{:S(2)}) collective-permute-start(bf16[272,1024]{1,0:T(8,128)(2,1)S(1)} %collective-permute-done.9.refs_1_), channel_id=1, source_target_pairs={{8,0},{16,8},{24,16},{28,24},{20,28},{12,20},{4,12},{0,4},{9,1},{1... | collective-permute-start | bytes 1671176 | tf_op jit(solution)/shard_map/ppermute | solution.py:195
  49.1 9.1 %collective-permute-start.12 = (bf16[352,1024]{1,0:T(8,128)(2,1)S(1)}, bf16[352,1024]{1,0:T(8,128)(2,1)S(1)}, u32[]{:S(2)}, u32[]{:S(2)}) collective-permute-start(bf16[352,1024]{1,0:T(8,128)(2,1)S(1)} %collective-permute-done.7.refs_2_.refs_3_.refs_8_), channel_id=1, source_target_pairs={{1,0},{0,1},{3,2},{2,3},{5,4},{4,5},{7,6},{6,7},{9,8},{8,9},{11,10... | collective-permute-start | bytes 2162696 | tf_op jit(solution)/shard_map/ppermute | solution.py:192
  49.1 9.1 %collective-permute-start.14 = (bf16[352,1024]{1,0:T(8,128)(2,1)S(1)}, bf16[352,1024]{1,0:T(8,128)(2,1)S(1)}, u32[]{:S(2)}, u32[]{:S(2)}) collective-permute-start(bf16[352,1024]{1,0:T(8,128)(2,1)S(1)} %collective-permute-done.8.refs_4_.refs_5_.refs_10_), channel_id=1, source_target_pairs={{1,0},{0,1},{3,2},{2,3},{5,4},{4,5},{7,6},{6,7},{9,8},{8,9},{11,10... | collective-permute-start | bytes 2162696 | tf_op jit(solution)/shard_map/ppermute | solution.py:192
  64.2 9.4 %collective-permute-start.17 = (bf16[144,1024]{1,0:T(8,128)(2,1)S(1)}, bf16[144,1024]{1,0:T(8,128)(2,1)S(1)}, u32[]{:S(2)}, u32[]{:S(2)}) collective-permute-start(bf16[144,1024]{1,0:T(8,128)(2,1)S(1)} %pad_maximum_fusion.2), channel_id=1, source_target_pairs={{0,8},{8,16},{16,24},{24,28},{28,20},{20,12},{12,4},{4,0},{1,9},{9... | collective-permute-start | bytes 884744 | tf_op jit(solution)/shard_map/ppermute | solution.py:195
  73.8 9.8 %collective-permute-start.18 = (bf16[128,1024]{1,0:T(8,128)(2,1)S(1)}, bf16[128,1024]{1,0:T(8,128)(2,1)S(1)}, u32[]{:S(2)}, u32[]{:S(2)}) collective-permute-start(bf16[128,1024]{1,0:T(8,128)(2,1)S(1)} %pad_maximum_fusion.6), channel_id=1, source_target_pairs={{0,8},{8,16},{16,24},{24,28},{28,20},{20,12},{12,4},{4,0},{1,9},{9... | collective-permute-start | bytes 786440 | tf_op jit(solution)/shard_map/ppermute | solution.py:195
  75.5 9.5 %collective-permute-start.22 = (bf16[128,1024]{1,0:T(8,128)(2,1)S(1)}, bf16[128,1024]{1,0:T(8,128)(2,1)S(1)}, u32[]{:S(2)}, u32[]{:S(2)}) collective-permute-start(bf16[128,1024]{1,0:T(8,128)(2,1)S(1)} %pad_maximum_fusion.8), channel_id=1, source_target_pairs={{8,0},{16,8},{24,16},{28,24},{20,28},{12,20},{4,12},{0,4},{9,1},{1... | collective-permute-start | bytes 786440 | tf_op jit(solution)/shard_map/ppermute | solution.py:195
  76.2 13.2 %collective-permute-start.25 = (bf16[144,1024]{1,0:T(8,128)(2,1)S(1)}, bf16[144,1024]{1,0:T(8,128)(2,1)S(1)}, u32[]{:S(2)}, u32[]{:S(2)}) collective-permute-start(bf16[144,1024]{1,0:T(8,128)(2,1)S(1)} %pad_maximum_fusion.3), channel_id=1, source_target_pairs={{0,8},{8,16},{16,24},{24,28},{28,20},{20,12},{12,4},{4,0},{1,9},{9... | collective-permute-start | bytes 884744 | tf_op jit(solution)/shard_map/ppermute | solution.py:195
  77.9 13.4 %collective-permute-start.28 = (bf16[144,1024]{1,0:T(8,128)(2,1)S(1)}, bf16[144,1024]{1,0:T(8,128)(2,1)S(1)}, u32[]{:S(2)}, u32[]{:S(2)}) collective-permute-start(bf16[144,1024]{1,0:T(8,128)(2,1)S(1)} %pad_maximum_fusion.4), channel_id=1, source_target_pairs={{8,0},{16,8},{24,16},{28,24},{20,28},{12,20},{4,12},{0,4},{9,1},{1... | collective-permute-start | bytes 884744 | tf_op jit(solution)/shard_map/ppermute | solution.py:195
  85.2 14.2 %collective-permute-start.19 = (bf16[128,1024]{1,0:T(8,128)(2,1)S(1)}, bf16[128,1024]{1,0:T(8,128)(2,1)S(1)}, u32[]{:S(2)}, u32[]{:S(2)}) collective-permute-start(bf16[128,1024]{1,0:T(8,128)(2,1)S(1)} %get-tuple-element.69), channel_id=1, source_target_pairs={{0,8},{8,16},{16,24},{24,28},{28,20},{20,12},{12,4},{4,0},{1,9},{9... | collective-permute-start | bytes 786440 | tf_op jit(solution)/shard_map/ppermute | solution.py:195
  86.8 12.6 %collective-permute-start.23 = (bf16[128,1024]{1,0:T(8,128)(2,1)S(1)}, bf16[128,1024]{1,0:T(8,128)(2,1)S(1)}, u32[]{:S(2)}, u32[]{:S(2)}) collective-permute-start(bf16[128,1024]{1,0:T(8,128)(2,1)S(1)} %get-tuple-element.70), channel_id=1, source_target_pairs={{8,0},{16,8},{24,16},{28,24},{20,28},{12,20},{4,12},{0,4},{9,1},{1... | collective-permute-start | bytes 786440 | tf_op jit(solution)/shard_map/ppermute | solution.py:195
  91.5 10.1 %collective-permute-start.26 = (bf16[144,1024]{1,0:T(8,128)(2,1)S(1)}, bf16[144,1024]{1,0:T(8,128)(2,1)S(1)}, u32[]{:S(2)}, u32[]{:S(2)}) collective-permute-start(bf16[144,1024]{1,0:T(8,128)(2,1)S(1)} %get-tuple-element.63), channel_id=1, source_target_pairs={{0,8},{8,16},{16,24},{24,28},{28,20},{20,12},{12,4},{4,0},{1,9},{9... | collective-permute-start | bytes 884744 | tf_op jit(solution)/shard_map/ppermute | solution.py:195
  93.1 10.1 %collective-permute-start.29 = (bf16[144,1024]{1,0:T(8,128)(2,1)S(1)}, bf16[144,1024]{1,0:T(8,128)(2,1)S(1)}, u32[]{:S(2)}, u32[]{:S(2)}) collective-permute-start(bf16[144,1024]{1,0:T(8,128)(2,1)S(1)} %get-tuple-element.64), channel_id=1, source_target_pairs={{8,0},{16,8},{24,16},{28,24},{20,28},{12,20},{4,12},{0,4},{9,1},{1... | collective-permute-start | bytes 884744 | tf_op jit(solution)/shard_map/ppermute | solution.py:195
  99.6 10.0 %collective-permute-start.24 = (bf16[128,1024]{1,0:T(8,128)(2,1)S(1)}, bf16[128,1024]{1,0:T(8,128)(2,1)S(1)}, u32[]{:S(2)}, u32[]{:S(2)}) collective-permute-start(bf16[128,1024]{1,0:T(8,128)(2,1)S(1)} %get-tuple-element.68), channel_id=1, source_target_pairs={{8,0},{16,8},{24,16},{28,24},{20,28},{12,20},{4,12},{0,4},{9,1},{1... | collective-permute-start | bytes 786440 | tf_op jit(solution)/shard_map/ppermute | solution.py:195
  100.1 9.5 %collective-permute-start.20 = (bf16[128,1024]{1,0:T(8,128)(2,1)S(1)}, bf16[128,1024]{1,0:T(8,128)(2,1)S(1)}, u32[]{:S(2)}, u32[]{:S(2)}) collective-permute-start(bf16[128,1024]{1,0:T(8,128)(2,1)S(1)} %get-tuple-element.67), channel_id=1, source_target_pairs={{0,8},{8,16},{16,24},{24,28},{28,20},{20,12},{12,4},{4,0},{1,9},{9... | collective-permute-start | bytes 786440 | tf_op jit(solution)/shard_map/ppermute | solution.py:195
  103.5 9.0 %collective-permute-start.30 = (bf16[144,1024]{1,0:T(8,128)(2,1)S(1)}, bf16[144,1024]{1,0:T(8,128)(2,1)S(1)}, u32[]{:S(2)}, u32[]{:S(2)}) collective-permute-start(bf16[144,1024]{1,0:T(8,128)(2,1)S(1)} %get-tuple-element.62), channel_id=1, source_target_pairs={{8,0},{16,8},{24,16},{28,24},{20,28},{12,20},{4,12},{0,4},{9,1},{1... | collective-permute-start | bytes 884744 | tf_op jit(solution)/shard_map/ppermute | solution.py:195
  104.0 8.5 %collective-permute-start.27 = (bf16[144,1024]{1,0:T(8,128)(2,1)S(1)}, bf16[144,1024]{1,0:T(8,128)(2,1)S(1)}, u32[]{:S(2)}, u32[]{:S(2)}) collective-permute-start(bf16[144,1024]{1,0:T(8,128)(2,1)S(1)} %get-tuple-element.61), channel_id=1, source_target_pairs={{0,8},{8,16},{16,24},{24,28},{28,20},{20,12},{12,4},{4,0},{1,9},{9... | collective-permute-start | bytes 884744 | tf_op jit(solution)/shard_map/ppermute | solution.py:195
  (14 other events, 69.6 us)
